TPU v7x, 32 devices: a whole 2x2x4 slice. The times are simulated.
32 devices in a mesh: dp: 8 (over y, x, core), head: 4 (over z).
Axes of the slice: x: 2, y: 2, z: 4, core: 2. Of those that a mesh axis runs over, the one named last changes fastest.
Arguments:
- inputs: bfloat16 [16384, 768], P(('dp', 'head')), may hold values from -6 to 6
- seg_lengths: int32 [8, 8], P('dp'), may hold values from 0 to 1024, as said below
- ln1_gain: bfloat16 [768], replicated, may hold values from 0.5 to 1.5
- ln1_bias: bfloat16 [768], replicated, may hold values from -1.75 to 1.75
- qkv_weight: bfloat16 [768, 3, 768], P(None, None, 'head'), may hold values from -0.3125 to 0.3125
- qkv_bias: bfloat16 [3, 768], P(None, 'head'), may hold values from -1.75 to 1.75
- out_weight: bfloat16 [768, 768], P('head'), may hold values from -0.875 to 0.875
- out_bias: bfloat16 [768], replicated, may hold values from -1.75 to 1.75
- mem_mu: bfloat16 [12, 512], P('head'), may hold values from -0.25 to 0.25
- mem_sig: bfloat16 [12, 512], P('head'), may hold values from -0.25 to 0.25
- ln2_gain: bfloat16 [768], replicated, may hold values from 0.5 to 1.5
- ln2_bias: bfloat16 [768], replicated, may hold values from -1.75 to 1.75
- ff_in: bfloat16 [768, 3072], P(None, 'head'), may hold values from -0.21875 to 0.21875
- ff_in_bias: bfloat16 [3072], P('head'), may hold values from -1.75 to 1.75
- ff_out: bfloat16 [3072, 768], P('head'), may hold values from -0.109375 to 0.109375
- ff_out_bias: bfloat16 [768], replicated, may hold values from -1.75 to 1.75
- cotangent: bfloat16 [16384, 768], P(('dp', 'head')), may hold values from -6 to 6
Outputs:
- outputs: bfloat16 [16384, 768], P(('dp', 'head'))
- input_grad: bfloat16 [16384, 768], P(('dp', 'head'))
- ln1_gain_grad: float32 [768], replicated
- ln1_bias_grad: float32 [768], replicated
- qkv_weight_grad: float32 [768, 3, 768], P(None, None, 'head')
- qkv_bias_grad: float32 [3, 768], P(None, 'head')
- out_weight_grad: float32 [768, 768], P('head')
- out_bias_grad: float32 [768], replicated
- mem_mu_grad: float32 [12, 512], P('head')
- mem_sig_grad: float32 [12, 512], P('head')
- ln2_gain_grad: float32 [768], replicated
- ln2_bias_grad: float32 [768], replicated
- ff_in_grad: float32 [768, 3072], P(None, 'head')
- ff_in_bias_grad: float32 [3072], P('head')
- ff_out_grad: float32 [3072, 768], P('head')
- ff_out_bias_grad: float32 [768], replicated
Inputs may be any that keep to these rules, and one draw needn't show every extreme that they name: `seg_lengths`: each row lists one group's segments in order, four slots for each aligned run of 1024 tokens: lengths of 1, 2 or 4 times 256 that fill the run, then zeros; every group has a segment of 1024.
All inputs are finite; a program needn't handle non-finite values.
Results may differ from a plain program's by a relative error of at most 0.019.
The roundings to bfloat16 on the way count: a program that leaves them out, or rounds other values in their place, can miss the bound.
Values may be sent and summed in bfloat16 or wider, within the bound.
A program may use at most 256 MiB of HBM per device.

v0:
```python
import math

import jax
import jax.numpy as jnp
from jax import lax
from jax.sharding import PartitionSpec as P

HEAD_DIM = 64
BASIS = 512
SEG_UNIT = 256


TAU = 0.75
RIDGE = 0.5
EPSILON = 1e-05
SPREAD = 1.0 / 64.0
HIGHEST = lax.Precision.HIGHEST


def basis_tables(count, dtype):
    centres = jnp.arange(count).astype(dtype) / (count - 1)
    width = 1.0 / count
    apart = centres[:, None] - centres[None, :]
    gram = jnp.exp(-apart * apart / (4.0 * width * width)) + RIDGE * jnp.eye(count, dtype=dtype)
    factor = jnp.linalg.cholesky(gram)
    solve = jax.scipy.linalg.cho_solve((factor, True), jnp.eye(count, dtype=dtype))
    samples = (jnp.arange(count).astype(dtype) + 0.5) / count
    near_gap = TAU * samples[:, None] - centres[None, :]
    far_gap = samples[:, None] - centres[None, :]
    near = jnp.exp(-near_gap * near_gap / (2.0 * width * width))
    far = jnp.exp(-far_gap * far_gap / (2.0 * width * width))
    contract = jnp.dot(near.T, far, precision=HIGHEST) * (
        TAU / (count * width * math.sqrt(math.pi))
    )
    advance = jnp.dot(solve, contract, precision=HIGHEST)
    return (centres, solve, advance)


def segment_layout(lengths, rows, unit):
    units = rows // unit
    slot_units = lengths // unit
    ends = jnp.cumsum(slot_units)
    starts = ends - slot_units
    unit_index = jnp.arange(units, dtype=jnp.int32)
    member = (unit_index[:, None] >= starts[None, :]) & (unit_index[:, None] < ends[None, :])
    slot_ids = jnp.arange(lengths.shape[0], dtype=jnp.int32)
    unit_slot = jnp.sum(jnp.where(member, slot_ids[None, :], 0), axis=1)
    unit_start = jnp.sum(jnp.where(member, starts[None, :], 0), axis=1) * unit
    unit_length = jnp.sum(jnp.where(member, lengths[None, :], 0), axis=1)
    row_index = jnp.arange(rows, dtype=jnp.int32)
    row_slot = jnp.repeat(unit_slot, unit)
    row_pos = row_index - jnp.repeat(unit_start, unit)
    row_len = jnp.repeat(unit_length, unit)
    return (member, row_slot, row_pos, row_len)


def memory_read(queries, keys, values, mu_weight, sig_weight, lengths, layout, tables):
    centres, solve, advance = tables
    member, row_slot, row_pos, row_len = layout
    rows, heads, depth = queries.shape
    count = centres.shape[0]
    units = member.shape[0]
    unit = rows // units
    kind = queries.dtype
    member_f = member.astype(kind)
    width = 1.0 / count
    place = TAU + (1.0 - TAU) * (row_pos.astype(kind) + 0.5) / row_len.astype(kind)
    gap = place[:, None] - centres[None, :]
    psi = jnp.exp(-gap * gap / (2.0 * width * width))
    stacked = jnp.concatenate(
        [keys.reshape(rows, heads * depth), values.reshape(rows, heads * depth)], axis=1
    )
    unit_terms = jnp.einsum(
        "uin,uic->unc",
        psi.reshape(units, unit, count),
        stacked.reshape(units, unit, -1),
        precision=HIGHEST,
    )
    slot_terms = jnp.einsum("us,unc->snc", member_f, unit_terms, precision=HIGHEST)
    scale = (1.0 - TAU) / (jnp.maximum(lengths, 1).astype(kind) * (width * math.sqrt(math.pi)))
    projected = (
        jnp.einsum("mn,snc->smc", solve, slot_terms, precision=HIGHEST) * scale[:, None, None]
    )

    def advance_step(state, inputs):
        term, length = inputs
        updated = jnp.dot(advance, state, precision=HIGHEST) + term
        return (jnp.where(length > 0, updated, state), state)

    _, before = lax.scan(advance_step, jnp.zeros_like(projected[0]), (projected, lengths))
    unit_memory = jnp.einsum("us,snc->unc", member_f, before, precision=HIGHEST)
    memory_keys = unit_memory[:, :, : heads * depth].reshape(units, count, heads, depth)
    memory_values = unit_memory[:, :, heads * depth :].reshape(units, count, heads, depth)
    query_units = queries.reshape(units, unit, heads, depth)
    basis_scores = jnp.einsum(
        "uihd,ujhd->uihj", query_units, memory_keys, precision=HIGHEST
    ) / math.sqrt(depth)
    location = jax.nn.sigmoid(
        jnp.einsum("uihj,hj->uih", basis_scores, mu_weight, precision=HIGHEST)
    )
    variance = (
        jax.nn.softplus(jnp.einsum("uihj,hj->uih", basis_scores, sig_weight, precision=HIGHEST))
        * SPREAD
        + width * width
    )
    offset = location[..., None] - centres
    density = jnp.sqrt(width * width / variance)[..., None] * jnp.exp(
        -offset * offset / (2.0 * variance[..., None])
    )
    gathered = jnp.einsum("uihj,ujhd->uihd", density, memory_values, precision=HIGHEST)
    return gathered.reshape(rows, heads, depth)


def layer_norm(values, gain, shift):
    centred = values - jnp.mean(values, axis=-1, keepdims=True)
    inverse = lax.rsqrt(jnp.mean(centred * centred, axis=-1, keepdims=True) + EPSILON)
    normal = centred * inverse
    return (normal * gain + shift, normal, inverse)


def norm_back(grad, normal, inverse, gain):
    scaled = grad * gain
    return inverse * (
        scaled
        - jnp.mean(scaled, axis=-1, keepdims=True)
        - normal * jnp.mean(scaled * normal, axis=-1, keepdims=True)
    )


def gelu_tanh(values):
    return jax.nn.gelu(values, approximate=True)


def local_attention(queries, keys, values, row_slot, block):
    rows, heads, depth = queries.shape
    count = rows // block
    scale = 1.0 / math.sqrt(depth)
    index = jnp.arange(block, dtype=jnp.int32)

    def local_one_block(args):
        query_part, key_part, value_part, slot_part = args
        scores = (
            jnp.einsum("qhd,khd->hqk", query_part, key_part, preferred_element_type=jnp.float32)
            * scale
        )
        allowed = (slot_part[:, None] == slot_part[None, :]) & (index[:, None] >= index[None, :])
        scores = jnp.where(allowed[None], scores, -1e30)
        highest = jnp.max(scores, axis=-1)
        weights = jnp.exp(scores - highest[..., None])
        totals = jnp.sum(weights, axis=-1)
        probs = (weights / totals[..., None]).astype(jnp.bfloat16)
        result = jnp.einsum("hqk,khd->qhd", probs, value_part, preferred_element_type=jnp.float32)
        return (result, highest + jnp.log(totals))

    shaped = (
        queries.reshape(count, block, heads, depth),
        keys.reshape(count, block, heads, depth),
        values.reshape(count, block, heads, depth),
        row_slot.reshape(count, block),
    )
    result, logsum = lax.map(local_one_block, shaped)
    return (result.reshape(rows, heads, depth), logsum)


def attention_back(queries, keys, values, row_slot, logsum, grad_mixed, block):
    rows, heads, depth = queries.shape
    count = rows // block
    scale = 1.0 / math.sqrt(depth)
    index = jnp.arange(block, dtype=jnp.int32)

    def attention_one_block(args):
        query_part, key_part, value_part, slot_part, log_part, grad_part = args
        scores = (
            jnp.einsum("qhd,khd->hqk", query_part, key_part, preferred_element_type=jnp.float32)
            * scale
        )
        allowed = (slot_part[:, None] == slot_part[None, :]) & (index[:, None] >= index[None, :])
        probs = jnp.where(allowed[None], jnp.exp(scores - log_part[..., None]), 0.0)
        grad_probs = jnp.einsum(
            "qhd,khd->hqk", grad_part, value_part, preferred_element_type=jnp.float32
        )
        inner = jnp.sum(probs * grad_probs, axis=-1, keepdims=True)
        grad_scores = (probs * (grad_probs - inner)).astype(jnp.bfloat16)
        grad_query = (
            jnp.einsum("hqk,khd->qhd", grad_scores, key_part, preferred_element_type=jnp.float32)
            * scale
        )
        grad_key = (
            jnp.einsum("hqk,qhd->khd", grad_scores, query_part, preferred_element_type=jnp.float32)
            * scale
        )
        grad_value = jnp.einsum(
            "hqk,qhd->khd",
            probs.astype(jnp.bfloat16),
            grad_part,
            preferred_element_type=jnp.float32,
        )
        return (grad_query, grad_key, grad_value)

    shaped = (
        queries.reshape(count, block, heads, depth),
        keys.reshape(count, block, heads, depth),
        values.reshape(count, block, heads, depth),
        row_slot.reshape(count, block),
        logsum,
        grad_mixed.reshape(count, block, heads, depth),
    )
    grad_query, grad_key, grad_value = lax.map(attention_one_block, shaped)
    return (
        grad_query.reshape(rows, heads, depth),
        grad_key.reshape(rows, heads, depth),
        grad_value.reshape(rows, heads, depth),
    )


def local(
    inputs,
    seg_lengths,
    ln1_gain,
    ln1_bias,
    qkv_weight,
    qkv_bias,
    out_weight,
    out_bias,
    mem_mu,
    mem_sig,
    ln2_gain,
    ln2_bias,
    ff_in,
    ff_in_bias,
    ff_out,
    ff_out_bias,
    cotangent,
):
    own_rows = inputs.shape[0]
    group = lax.axis_size("head") * own_rows
    local_width = qkv_weight.shape[2]
    local_heads = local_width // HEAD_DIM
    block = 4 * SEG_UNIT
    lengths = seg_lengths[0]
    tables = basis_tables(BASIS, jnp.float32)
    layout = segment_layout(lengths, group, SEG_UNIT)
    row_slot = layout[1]
    source = inputs.astype(jnp.float32)
    gain_one = ln1_gain.astype(jnp.float32)
    gain_two = ln2_gain.astype(jnp.float32)
    normed1, normal1, inverse1 = layer_norm(source, gain_one, ln1_bias.astype(jnp.float32))
    first_rows = lax.all_gather(normed1.astype(jnp.bfloat16), "head", axis=0, tiled=True)
    weight_flat = qkv_weight.reshape(qkv_weight.shape[0], 3 * local_width)
    projected = jnp.dot(
        first_rows, weight_flat, preferred_element_type=jnp.float32
    ) + qkv_bias.reshape(3 * local_width).astype(jnp.float32)
    qkv = projected.astype(jnp.bfloat16).reshape(group, 3, local_heads, HEAD_DIM)
    queries, keys, values = (qkv[:, 0], qkv[:, 1], qkv[:, 2])
    discrete, logsum = local_attention(queries, keys, values, row_slot, block)

    def memory_part(query_f, key_f, value_f, mu_weight, sig_weight):
        return memory_read(query_f, key_f, value_f, mu_weight, sig_weight, lengths, layout, tables)

    gathered, memory_back = jax.vjp(
        memory_part,
        queries.astype(jnp.float32),
        keys.astype(jnp.float32),
        values.astype(jnp.float32),
        mem_mu.astype(jnp.float32),
        mem_sig.astype(jnp.float32),
    )
    mixed = (discrete + gathered).astype(jnp.bfloat16).reshape(group, local_width)
    attended = lax.psum_scatter(
        jnp.dot(mixed, out_weight, preferred_element_type=jnp.float32).astype(jnp.bfloat16),
        "head",
        scatter_dimension=0,
        tiled=True,
    ).astype(jnp.float32)
    residual = source + attended + out_bias.astype(jnp.float32)
    normed2, normal2, inverse2 = layer_norm(residual, gain_two, ln2_bias.astype(jnp.float32))
    second = normed2.astype(jnp.bfloat16)
    grad_out = cotangent.astype(jnp.float32)
    second_rows = lax.all_gather(second, "head", axis=0, tiled=True)
    hidden = jnp.dot(second_rows, ff_in, preferred_element_type=jnp.float32) + ff_in_bias.astype(
        jnp.float32
    )
    activation, gelu_back = jax.vjp(gelu_tanh, hidden)
    act_low = activation.astype(jnp.bfloat16)
    ffn_result = lax.psum_scatter(
        jnp.dot(act_low, ff_out, preferred_element_type=jnp.float32).astype(jnp.bfloat16),
        "head",
        scatter_dimension=0,
        tiled=True,
    ).astype(jnp.float32)
    grad_rows = lax.all_gather(cotangent, "head", axis=0, tiled=True)
    grad_act = jnp.dot(grad_rows, ff_out.T, preferred_element_type=jnp.float32)
    ff_out_grad = jnp.dot(act_low.T, grad_rows, preferred_element_type=jnp.float32)
    grad_hidden = gelu_back(grad_act)[0].astype(jnp.bfloat16)
    ff_in_grad = jnp.dot(second_rows.T, grad_hidden, preferred_element_type=jnp.float32)
    ff_in_bias_grad = jnp.sum(grad_hidden.astype(jnp.float32), axis=0)
    grad_second = lax.psum_scatter(
        jnp.dot(grad_hidden, ff_in.T, preferred_element_type=jnp.float32).astype(jnp.bfloat16),
        "head",
        scatter_dimension=0,
        tiled=True,
    ).astype(jnp.float32)
    outputs = residual + ffn_result + ff_out_bias.astype(jnp.float32)
    ff_out_bias_part = jnp.sum(grad_out, axis=0)
    grad_residual = grad_out + norm_back(grad_second, normal2, inverse2, gain_two)
    ln2_gain_part = jnp.sum(grad_second * normal2, axis=0)
    ln2_bias_part = jnp.sum(grad_second, axis=0)
    out_bias_part = jnp.sum(grad_residual, axis=0)
    attn_rows = lax.all_gather(grad_residual.astype(jnp.bfloat16), "head", axis=0, tiled=True)
    out_weight_grad = jnp.dot(mixed.T, attn_rows, preferred_element_type=jnp.float32)
    grad_mixed = (
        jnp.dot(attn_rows, out_weight.T, preferred_element_type=jnp.float32)
        .astype(jnp.bfloat16)
        .reshape(group, local_heads, HEAD_DIM)
    )
    query_disc, key_disc, value_disc = attention_back(
        queries, keys, values, row_slot, logsum, grad_mixed, block
    )
    query_mem, key_mem, value_mem, mu_grad, sig_grad = memory_back(grad_mixed.astype(jnp.float32))
    grad_qkv = (
        jnp.stack([query_disc + query_mem, key_disc + key_mem, value_disc + value_mem], axis=1)
        .astype(jnp.bfloat16)
        .reshape(group, 3 * local_width)
    )
    qkv_weight_grad = jnp.dot(first_rows.T, grad_qkv, preferred_element_type=jnp.float32).reshape(
        qkv_weight.shape[0], 3, local_width
    )
    qkv_bias_grad = jnp.sum(grad_qkv.astype(jnp.float32), axis=0).reshape(3, local_width)
    grad_first = lax.psum_scatter(
        jnp.dot(grad_qkv, weight_flat.T, preferred_element_type=jnp.float32).astype(jnp.bfloat16),
        "head",
        scatter_dimension=0,
        tiled=True,
    ).astype(jnp.float32)
    grad_source = grad_residual + norm_back(grad_first, normal1, inverse1, gain_one)
    ln1_gain_part = jnp.sum(grad_first * normal1, axis=0)
    ln1_bias_part = jnp.sum(grad_first, axis=0)
    summed = lax.psum(
        (
            qkv_weight_grad,
            qkv_bias_grad,
            out_weight_grad,
            mu_grad,
            sig_grad,
            ff_in_grad,
            ff_in_bias_grad,
            ff_out_grad,
        ),
        "dp",
    )
    shared = lax.psum(
        (
            ln1_gain_part,
            ln1_bias_part,
            out_bias_part,
            ln2_gain_part,
            ln2_bias_part,
            ff_out_bias_part,
        ),
        ("dp", "head"),
    )
    return (
        outputs.astype(jnp.bfloat16),
        grad_source.astype(jnp.bfloat16),
        shared[0],
        shared[1],
        summed[0],
        summed[1],
        summed[2],
        shared[2],
        summed[3],
        summed[4],
        shared[3],
        shared[4],
        summed[5],
        summed[6],
        summed[7],
        shared[5],
    )


def solution(mesh):
    return jax.shard_map(
        local,
        mesh=mesh,
        in_specs=(
            P(("dp", "head"), None),
            P("dp", None),
            P(),
            P(),
            P(None, None, "head"),
            P(None, "head"),
            P("head", None),
            P(),
            P("head", None),
            P("head", None),
            P(),
            P(),
            P(None, "head"),
            P("head"),
            P("head", None),
            P(),
            P(("dp", "head"), None),
        ),
        out_specs=(
            P(("dp", "head"), None),
            P(("dp", "head"), None),
            P(),
            P(),
            P(None, None, "head"),
            P(None, "head"),
            P("head", None),
            P(),
            P("head", None),
            P("head", None),
            P(),
            P(),
            P(None, "head"),
            P("head"),
            P("head", None),
            P(),
        ),
        check_vma=False,
    )
```

profile of v0, /device:TPU:0, one launch (start us, length us, event | category | flops | bytes accessed | tf_op | source)
XLA Modules:
  0.0 1597.5 jit_solution(6541801843127041748)
XLA Ops:
  89.4 22.1 %cholesky.253 = f32[128,128]{1,0:T(8,128)S(1)} custom-call(f32[128,128]{1,0:T(8,128)S(1)} %convolution_subtract_fusion.8), custom_call_target="Cholesky" | custom-call | tf_op jit(solution)/shard_map/jit(cholesky)/cholesky | solution.py:25
  126.8 40.1 %custom-call.37 = f32[4,128,128]{1,2,0:T(8,128)S(1)} custom-call(f32[4,128,128]{2,1,0:T(8,128)} %get-tuple-element.293), custom_call_target="InvertDiagBlocksLowerTriangular" | custom-call | tf_op jit(solution)/shard_map/jit(_cho_solve)/triangular_solve | solution.py:26
  198.5 73.2 %while.62 = (s32[]{:T(128)}, f32[2,1024,3,64]{1,0,3,2:T(2,128)}, f32[2,3,1024]{2,1,0:T(4,128)}, bf16[2,1024,3,64]{1,3,2,0:T(8,128)(2,1)}, s32[2,1024]{1,0:T(2,12...) while((s32[]{:T(128)}, f32[2,1024,3,64]{1,0,3,2:T(2,128)}, ...), condition=%wide.region_7.8_spmd.clone, body=%wide.region_4.7_spmd.clone.sunk | while | flops 846197760 | bytes 47375532 | solution.py:161
  291.6 22.5 %multiply_bitcast_fusion.1 = f32[8,512,384]{1,2,0:T(8,128)} fusion(f32[8]{0:T(128)S(1)} %copy-done.58, f32[8,512,384]{2,0,1:T(8,128)S(1)} %fusion.102, f32[128,512]{1,0:T(8,128)S(1)} %copy-done.19, f32[128,512]{1,0:T(8,128)S(1)} %copy-done.24, f32[128,512]{1,0:T(8,128)S(1)} %copy-done.27, f32[128,512]{1,0:T(8,128)S(1)} %copy-done.37), kind=kOutput, calls=%fused_computation.149 | convolution fusion | flops 9666035712 | bytes 13631520 | tf_op jit(solution)/shard_map/jvp(mn,snc->smc)/dot_general | solution.py:82
  314.2 243.2 %while.64 = (s32[]{:T(128)}, f32[512,384]{1,0:T(8,128)}, f32[8,512,384]{2,0,1:T(8,128)}, pred[8]{0:T(512)(128)(4,1)S(1)}, s32[8]{0:T(128)S(1)}, /*index=5*/f32[5...) while((s32[]{:T(128)}, f32[512,384]{1,0:T(8,128)}, ...), condition=%wide.region_19.20_spmd.clone, body=%wide.region_18.19_spmd.clone.sunk | while | flops 1208942592 | bytes 12845192 | solution.py:90
  327.7 17.3 %dynamic_update_slice.57 = f32[8,512,384]{2,0,1:T(8,128)} dynamic-update-slice(f32[8,512,384]{2,0,1:T(8,128)} %get-tuple-element.827, f32[1,512,384]{2,0,1:T(1,128)} %copy.260, s32[]{:T(128)S(6)} %copy.296, s32[]{:T(128)} %constant.321.clone.1..sunk.2, s32[]{:T(128)} %constant.321.clone.1..sunk.2) | dynamic-update-slice | bytes 1572868 | tf_op jit(solution)/shard_map/jvp()/while/body/jit(dynamic_update_index_in_dim)/dynamic_update_slice | solution.py:90
  358.0 17.3 %dynamic_update_slice.57 = f32[8,512,384]{2,0,1:T(8,128)} dynamic-update-slice(f32[8,512,384]{2,0,1:T(8,128)} %get-tuple-element.827, f32[1,512,384]{2,0,1:T(1,128)} %copy.260, s32[]{:T(128)S(6)} %copy.296, s32[]{:T(128)} %constant.321.clone.1..sunk.2, s32[]{:T(128)} %constant.321.clone.1..sunk.2) | dynamic-update-slice | bytes 1572868 | tf_op jit(solution)/shard_map/jvp()/while/body/jit(dynamic_update_index_in_dim)/dynamic_update_slice | solution.py:90
  388.4 17.3 %dynamic_update_slice.57 = f32[8,512,384]{2,0,1:T(8,128)} dynamic-update-slice(f32[8,512,384]{2,0,1:T(8,128)} %get-tuple-element.827, f32[1,512,384]{2,0,1:T(1,128)} %copy.260, s32[]{:T(128)S(6)} %copy.296, s32[]{:T(128)} %constant.321.clone.1..sunk.2, s32[]{:T(128)} %constant.321.clone.1..sunk.2) | dynamic-update-slice | bytes 1572868 | tf_op jit(solution)/shard_map/jvp()/while/body/jit(dynamic_update_index_in_dim)/dynamic_update_slice | solution.py:90
  418.7 17.3 %dynamic_update_slice.57 = f32[8,512,384]{2,0,1:T(8,128)} dynamic-update-slice(f32[8,512,384]{2,0,1:T(8,128)} %get-tuple-element.827, f32[1,512,384]{2,0,1:T(1,128)} %copy.260, s32[]{:T(128)S(6)} %copy.296, s32[]{:T(128)} %constant.321.clone.1..sunk.2, s32[]{:T(128)} %constant.321.clone.1..sunk.2) | dynamic-update-slice | bytes 1572868 | tf_op jit(solution)/shard_map/jvp()/while/body/jit(dynamic_update_index_in_dim)/dynamic_update_slice | solution.py:90
  449.1 17.3 %dynamic_update_slice.57 = f32[8,512,384]{2,0,1:T(8,128)} dynamic-update-slice(f32[8,512,384]{2,0,1:T(8,128)} %get-tuple-element.827, f32[1,512,384]{2,0,1:T(1,128)} %copy.260, s32[]{:T(128)S(6)} %copy.296, s32[]{:T(128)} %constant.321.clone.1..sunk.2, s32[]{:T(128)} %constant.321.clone.1..sunk.2) | dynamic-update-slice | bytes 1572868 | tf_op jit(solution)/shard_map/jvp()/while/body/jit(dynamic_update_index_in_dim)/dynamic_update_slice | solution.py:90
  479.4 17.3 %dynamic_update_slice.57 = f32[8,512,384]{2,0,1:T(8,128)} dynamic-update-slice(f32[8,512,384]{2,0,1:T(8,128)} %get-tuple-element.827, f32[1,512,384]{2,0,1:T(1,128)} %copy.260, s32[]{:T(128)S(6)} %copy.296, s32[]{:T(128)} %constant.321.clone.1..sunk.2, s32[]{:T(128)} %constant.321.clone.1..sunk.2) | dynamic-update-slice | bytes 1572868 | tf_op jit(solution)/shard_map/jvp()/while/body/jit(dynamic_update_index_in_dim)/dynamic_update_slice | solution.py:90
  509.7 17.3 %dynamic_update_slice.57 = f32[8,512,384]{2,0,1:T(8,128)} dynamic-update-slice(f32[8,512,384]{2,0,1:T(8,128)} %get-tuple-element.827, f32[1,512,384]{2,0,1:T(1,128)} %copy.260, s32[]{:T(128)S(6)} %copy.296, s32[]{:T(128)} %constant.321.clone.1..sunk.2, s32[]{:T(128)} %constant.321.clone.1..sunk.2) | dynamic-update-slice | bytes 1572868 | tf_op jit(solution)/shard_map/jvp()/while/body/jit(dynamic_update_index_in_dim)/dynamic_update_slice | solution.py:90
  540.1 17.3 %dynamic_update_slice.57 = f32[8,512,384]{2,0,1:T(8,128)} dynamic-update-slice(f32[8,512,384]{2,0,1:T(8,128)} %get-tuple-element.827, f32[1,512,384]{2,0,1:T(1,128)} %copy.260, s32[]{:T(128)S(6)} %copy.296, s32[]{:T(128)} %constant.321.clone.1..sunk.2, s32[]{:T(128)} %constant.321.clone.1..sunk.2) | dynamic-update-slice | bytes 1572868 | tf_op jit(solution)/shard_map/jvp()/while/body/jit(dynamic_update_index_in_dim)/dynamic_update_slice | solution.py:90
  615.3 63.0 %reduce-scatter.5.cloned.1.call-done = bf16[512,768]{1,0:T(8,128)(2,1)} async-done(((bf16[2048,768]{1,0:T(8,128)(2,1)}), bf16[512,768]{1,0:T(8,128)(2,1)}) %reduce-scatter.5.cloned.1.call-update) | async-done | bytes 786448 | tf_op jit(solution)/shard_map/reduce_scatter | solution.py:269
  685.0 62.6 %all-gather.7.cloned.1.call-done = bf16[2048,768]{1,0:T(8,128)(2,1)} async-done(((bf16[512,768]{1,0:T(8,128)(2,1)}), bf16[2048,768]{1,0:T(8,128)(2,1)}) %all-gather.7.cloned.1.call-update) | async-done | bytes 3145744 | tf_op jit(solution)/shard_map/all_gather | solution.py:279
  755.0 56.2 %all-gather.9.cloned.1.call-done = bf16[2048,768]{1,0:T(8,128)(2,1)} async-done(((bf16[512,768]{1,0:T(8,128)(2,1)}), bf16[2048,768]{1,0:T(8,128)(2,1)}) %all-gather.9.cloned.1.call-update) | async-done | bytes 3145744 | tf_op jit(solution)/shard_map/all_gather | solution.py:291
  835.7 52.6 %reduce-scatter.9.cloned.1.call-done = bf16[512,768]{1,0:T(8,128)(2,1)} async-done(((bf16[2048,768]{1,0:T(8,128)(2,1)}), bf16[512,768]{1,0:T(8,128)(2,1)}) %reduce-scatter.9.cloned.1.call-update) | async-done | bytes 786448 | tf_op jit(solution)/shard_map/reduce_scatter | solution.py:297
  891.0 59.8 %reduce-scatter.7.cloned.1.call-done = bf16[512,768]{1,0:T(8,128)(2,1)} async-done(((bf16[2048,768]{1,0:T(8,128)(2,1)}), bf16[512,768]{1,0:T(8,128)(2,1)}) %reduce-scatter.7.cloned.1.call-update) | async-done | bytes 786448 | tf_op jit(solution)/shard_map/reduce_scatter | solution.py:285
  957.1 63.4 %all-gather.11.cloned.1.call-done = bf16[2048,768]{1,0:T(8,128)(2,1)} async-done(((bf16[512,768]{1,0:T(8,128)(2,1)}), bf16[2048,768]{1,0:T(8,128)(2,1)}) %all-gather.11.cloned.1.call-update) | async-done | bytes 3145744 | tf_op jit(solution)/shard_map/all_gather | solution.py:309
  1081.3 151.5 %while.63 = (s32[]{:T(128)}, f32[2,1024,3,64]{1,0,3,2:T(2,128)}, f32[2,1024,3,64]{1,0,3,2:T(2,128)}, f32[2,1024,3,64]{1,0,3,2:T(2,128)}, bf16[2,1024,3,64]{1,3,2...) while((s32[]{:T(128)}, f32[2,1024,3,64]{1,0,3,2:T(2,128)}, ...), condition=%wide.region_29.30_spmd.clone, body=%wide.region_27.29_spmd.clone.sunk | while | flops 2063987712 | bytes 213878992 | solution.py:208
  1267.0 87.7 %while.65 = (s32[]{:T(128)}, f32[512,384]{0,1:T(8,128)S(1)}, f32[8,512,384]{1,2,0:T(8,128)}, f32[8,512,384]{2,0,1:T(8,128)}, pred[8]{0:T(512)(128)(4,1)S(1)}, /*...) while((s32[]{:T(128)}, f32[512,384]{0,1:T(8,128)S(1)}, ...), condition=%wide.region_34.35_spmd.clone, body=%wide.region_33.34_spmd.clone.sunk | while | flops 1209532416 | bytes 9699979 | solution.py:90
  1449.5 24.5 %all-reduce.4 = (f32[3,192]{1,0:T(4,128)}, f32[3,512]{1,0:T(4,128)}, f32[3,512]{1,0:T(4,128)}, f32[768]{0:T(1024)}) all-reduce(f32[3,192]{1,0:T(4,128)S(1)} %reshape.593, f32[3,512]{1,0:T(4,128)S(1)} %bitcast.503, f32[3,512]{1,0:T(4,128)S(1)} %bitcast.502, f32[768]{0:T(1024)S(1)} %copy-done.81), channel_id=1, replica_groups=mesh['dp'=8,'head'=4] {'dp'}, use_global_device_ids=true, to_apply=%region_44.45 | all-reduce | flops 4416 | bytes 35328 | tf_op jit(solution)/shard_map/psum | solution.py:338
  1476.3 39.0 %all-reduce.3 = (f32[768]{0:T(1024)}, f32[768]{0:T(1024)}, f32[768]{0:T(1024)}, f32[768]{0:T(1024)}, f32[768]{0:T(1024)}, /*index=5*/f32[768]{0:T(1024)}) all-reduce(f32[768]{0:T(1024)S(1)} %get-tuple-element.423, f32[768]{0:T(1024)S(1)} %get-tuple-element.428, ...), channel_id=1, replica_groups=mesh['dp'=8,'head'=4] {'dp','head'}, use_global_device_ids=true, to_apply=%region_39.40 | all-reduce | flops 4608 | bytes 36864 | tf_op jit(solution)/shard_map/psum | solution.py:351
  1517.8 65.1 %all-reduce.8.cloned.1.call-done = (f32[768,3,192]{0,2,1:T(8,128)}, f32[192,768]{1,0:T(8,128)}, f32[768,768]{1,0:T(8,128)}, f32[768,768]{1,0:T(8,128)}) async-done(((f32[768,3,192]{0,2,1:T(8,128)}, f32[192,768]{1,0:T(8,128)}, f32[768,768]{1,0:T(8,128)}, f32[768,768]{1,0:T(8,128)}), (f32[768,3,192]{0,2,1:T(8,128)}, f32[192,768]{1,0:T(8,128)}, f32[768,768]{1,0:T(8,128)}, ...) | async-done | bytes 7077904 | tf_op jit(solution)/shard_map/psum | solution.py:338
  (576 shorter events, 878.7 us)
Async XLA Ops:
  7.2 804.0 %copy-start = (bf16[768,768]{1,0:T(8,128)(2,1)S(1)}, bf16[768,768]{1,0:T(8,128)(2,1)}, u32[]{:S(2)}) copy-start(bf16[768,768]{1,0:T(8,128)(2,1)} %param.39) | copy-start | bytes 3538948
  7.2 174.6 %all-gather.5.cloned.1.call-start = ((), (), s32[]{:S(2)}) async-start(), calls=%async_computation.4 | async-start | bytes 3932160 | tf_op jit(solution)/shard_map/all_gather | solution.py:248
  14.0 664.3 %reduce-scatter.5.cloned.1.call-start = ((), (), s32[]{:S(2)}) async-start(), calls=%async_computation.5 | async-start | bytes 3932160 | tf_op jit(solution)/shard_map/reduce_scatter | solution.py:269
  17.6 109.1 %copy-start.82 = (bf16[3,192]{1,0:T(4,128)(2,1)S(1)}, bf16[3,192]{1,0:T(4,128)(2,1)}, u32[]{:S(2)}) copy-start(bf16[3,192]{1,0:T(4,128)(2,1)} %param.30) | copy-start | bytes 3460
  314.2 243.2 %copy-start.77 = (s32[8]{0:T(128)S(1)}, s32[8]{0:T(128)}, u32[]{:S(2)}) copy-start(s32[8]{0:T(128)} %copy-done.75) | copy-start | bytes 100
  612.4 65.8 %copy-start.7 = (bf16[512,768]{1,0:T(8,128)(2,1)S(1)}, bf16[512,768]{1,0:T(8,128)(2,1)}, u32[]{:S(2)}) copy-start(bf16[512,768]{1,0:T(8,128)(2,1)} %param.25) | copy-start | bytes 2359300
  615.2 69.8 %copy-start.86 = (bf16[768]{0:T(1024)(128)(2,1)S(1)}, bf16[768]{0:T(1024)(128)(2,1)}, u32[]{:S(2)}) copy-start(bf16[768]{0:T(1024)(128)(2,1)} %param.38) | copy-start | bytes 4612
  615.2 132.3 %all-gather.7.cloned.1.call-start = ((), (), s32[]{:S(2)}) async-start(), calls=%async_computation.6 | async-start | bytes 3932160 | tf_op jit(solution)/shard_map/all_gather | solution.py:279
  683.8 127.3 %all-gather.9.cloned.1.call-start = ((), (), s32[]{:S(2)}) async-start(), calls=%async_computation.8 | async-start | bytes 3932160 | tf_op jit(solution)/shard_map/all_gather | solution.py:291
  684.4 203.9 %reduce-scatter.9.cloned.1.call-start = ((), (), s32[]{:S(2)}) async-start(), calls=%async_computation.9 | async-start | bytes 3932160 | tf_op jit(solution)/shard_map/reduce_scatter | solution.py:297
  829.2 121.5 %reduce-scatter.7.cloned.1.call-start = ((), (), s32[]{:S(2)}) async-start(), calls=%async_computation.7 | async-start | bytes 3932160 | tf_op jit(solution)/shard_map/reduce_scatter | solution.py:285
  829.3 59.0 %copy-start.15 = (bf16[512,768]{1,0:T(8,128)(2,1)S(1)}, bf16[512,768]{1,0:T(8,128)(2,1)}, u32[]{:S(2)}) copy-start(bf16[512,768]{1,0:T(8,128)(2,1)} %reduce-scatter.5.cloned.1.call-done) | copy-start | bytes 2359300
  835.6 115.2 %copy-start.41 = (bf16[512,768]{1,0:T(8,128)(2,1)S(1)}, bf16[512,768]{1,0:T(8,128)(2,1)}, u32[]{:S(2)}) copy-start(bf16[512,768]{1,0:T(8,128)(2,1)} %param.41) | copy-start | bytes 2359300
  835.6 184.9 %all-gather.11.cloned.1.call-start = ((), (), s32[]{:S(2)}) async-start(), calls=%async_computation.10 | async-start | bytes 3932160 | tf_op jit(solution)/shard_map/all_gather | solution.py:309
  956.9 517.2 %reduce-scatter.11.cloned.1.call-start = ((), (), s32[]{:S(2)}) async-start(), calls=%async_computation.11 | async-start | bytes 3932160 | tf_op jit(solution)/shard_map/reduce_scatter | solution.py:329
  1266.9 87.7 %copy-start.20 = (f32[128,512]{1,0:T(8,128)S(1)}, f32[128,512]{1,0:T(8,128)}, u32[]{:S(2)}) copy-start(f32[128,512]{1,0:T(8,128)} %copy-done.18) | copy-start | bytes 786436
  1266.9 87.7 %copy-start.25 = (f32[128,512]{1,0:T(8,128)S(1)}, f32[128,512]{1,0:T(8,128)}, u32[]{:S(2)}) copy-start(f32[128,512]{1,0:T(8,128)} %copy-done.23) | copy-start | bytes 786436
  1266.9 87.7 %copy-start.28 = (f32[128,512]{1,0:T(8,128)S(1)}, f32[128,512]{1,0:T(8,128)}, u32[]{:S(2)}) copy-start(f32[128,512]{1,0:T(8,128)} %copy-done.26) | copy-start | bytes 786436
  1267.0 87.7 %copy-start.59 = (f32[8]{0:T(128)S(1)}, f32[8]{0:T(128)}, u32[]{:S(2)}) copy-start(f32[8]{0:T(128)} %multiply_divide_fusion.1) | copy-start | bytes 100
  1404.7 178.2 %all-reduce.8.cloned.1.call-start = ((), (), s32[]{:S(2)}) async-start(), calls=%async_computation.12 | async-start | bytes 14155776 | tf_op jit(solution)/shard_map/psum | solution.py:338
  1436.0 40.2 %copy-start.68 = (f32[768]{0:T(1024)S(1)}, f32[768]{0:T(1024)}, u32[]{:S(2)}) copy-start(f32[768]{0:T(1024)} %get-tuple-element.421) | copy-start | bytes 9220
  1436.0 40.2 %copy-start.69 = (f32[768]{0:T(1024)S(1)}, f32[768]{0:T(1024)}, u32[]{:S(2)}) copy-start(f32[768]{0:T(1024)} %get-tuple-element.427) | copy-start | bytes 9220
  1436.1 40.2 %copy-start.70 = (f32[768]{0:T(1024)S(1)}, f32[768]{0:T(1024)}, u32[]{:S(2)}) copy-start(f32[768]{0:T(1024)} %get-tuple-element.518) | copy-start | bytes 9220
  1436.1 79.2 %copy-start.17 = (f32[512,768]{1,0:T(8,128)S(1)}, f32[512,768]{1,0:T(8,128)}, u32[]{:S(2)}) copy-start(f32[512,768]{1,0:T(8,128)} %copy-done.16) | copy-start | bytes 4718596
  (90 other events, 737.9 us)
Sparse Core Ops, SparseCore 0:
  14.1 66.2 all-gather.4
  615.3 62.9 reduce-scatter.4
  684.0 63.5 all-gather.6
  748.9 62.1 all-gather.8
  829.4 58.8 reduce-scatter.8
  890.5 60.2 reduce-scatter.6
  957.0 63.5 all-gather.10
  1404.8 58.8 reduce-scatter.10
  1468.6 114.2 all-reduce.7
where the time goes:
time: 1620 us; the launch traced here: 1600 us
  local copies, waits for them, and re-layouts  480 us (30%)
  waiting for transfers between devices  423 us (26%)
  matrix products  384 us (24%)
  other arithmetic  225 us (14%)
  blocking collectives  63.5 us (4%)
  between operations  18.2 us (1%)
    dynamic_update_slice x24, local copies, waits for them, and re-layouts, memory_read(): lax.scan(advance_step, jnp.zeros_like(projected[0]), (projected, lengths))  158 us
    dynamic_update_slice x16, local copies, waits for them, and re-layouts, local_attention(): result, logsum = lax.map(local_one_block, shaped)  122 us
    another operation x15, other arithmetic, basis_tables(): factor = jnp.linalg.cholesky(gram)  91.9 us
    dynamic_slice x40, local copies, waits for them, and re-layouts, memory_read(): lax.scan(advance_step, jnp.zeros_like(projected[0]), (projected, lengths))  82.6 us
    psum x1, waiting for transfers between devices, local(): lax.psum((qkv_weight_grad, qkv_bias_grad, out_weight_grad, mu_grad, sig_g...  65.1 us
    all_gather x1, waiting for transfers between devices, local(): lax.all_gather(grad_residual.astype(jnp.bfloat16), 'head', axis=0, tiled=...  63.4 us
    reduce_scatter x1, waiting for transfers between devices, local(): lax.psum_scatter(jnp.dot(mixed, out_weight, preferred_element_type=jnp.fl...  63 us
    all_gather x1, waiting for transfers between devices, local(): second_rows = lax.all_gather(second, 'head', axis=0, tiled=True)  62.6 us
  transfers between devices with their start and end apart: 9, of which 7 were waited for; matrix products, arithmetic and copies ran while one was open for 14% of the time, Pallas kernels for 0%

commit v1 on v0

v1 whole, which is shorter than its diff:
```python
import functools
import math

import jax
import jax.numpy as jnp
import ml_dtypes
import numpy as np
from jax import lax
from jax.experimental import pallas as pl
from jax.experimental.pallas import tpu as pltpu
from jax.sharding import PartitionSpec as P

HEAD_DIM = 64
BASIS = 512
UNIT = 256
LANES = 256
TAU = 0.75
RIDGE = 0.5
EPSILON = 1e-05
SPREAD = 1.0 / 64.0
WIDTH = 1.0 / BASIS
LIVE = BASIS // 2
HIGHEST = lax.Precision.HIGHEST
F32 = jnp.float32
BF16 = jnp.bfloat16


def split_table(table):
    high = table.astype(np.float32).astype(ml_dtypes.bfloat16)
    low = (table.astype(np.float32) - high.astype(np.float32)).astype(ml_dtypes.bfloat16)
    return high, low


@functools.lru_cache(maxsize=None)
def basis_tables():
    centres = np.arange(BASIS) / (BASIS - 1)
    apart = centres[:, None] - centres[None, :]
    gram = np.exp(-apart * apart / (4.0 * WIDTH * WIDTH)) + RIDGE * np.eye(BASIS)
    solve = np.linalg.inv(gram)
    samples = (np.arange(BASIS) + 0.5) / BASIS
    near_gap = TAU * samples[:, None] - centres[None, :]
    far_gap = samples[:, None] - centres[None, :]
    near = np.exp(-near_gap * near_gap / (2.0 * WIDTH * WIDTH))
    far = np.exp(-far_gap * far_gap / (2.0 * WIDTH * WIDTH))
    contract = (near.T @ far) * (TAU / (BASIS * WIDTH * math.sqrt(math.pi)))
    joined = np.concatenate([solve @ contract, solve[:, LIVE:]], axis=1)
    high, low = split_table(joined)
    forward = np.concatenate([high, high, low], axis=1)
    backward = np.concatenate([high.T, high.T, low.T], axis=1)
    return forward, backward


def term_scale(units):
    return (1.0 - TAU) / (WIDTH * math.sqrt(math.pi) * UNIT) / units.astype(F32)


def split3(value):
    high = value.astype(BF16)
    low = (value - high.astype(F32)).astype(BF16)
    return jnp.concatenate([high, low, high], axis=0)


def dot(a, b, contract=((1,), (0,)), precision=None):
    return lax.dot_general(a, b, (contract, ((), ())), precision=precision, preferred_element_type=F32)


def head_rows(heads, width):
    row = lax.broadcasted_iota(jnp.int32, (8, width), 0)
    lane = lax.broadcasted_iota(jnp.int32, (8, width), 1) // HEAD_DIM
    return ((row == lane) | (row == lane + heads)) & (lane < heads)


def read_parts(logits, heads):
    location = 1.0 / (1.0 + jnp.exp(-logits))
    variance = (jnp.maximum(logits, 0.0) + jnp.log1p(jnp.exp(-jnp.abs(logits)))) * SPREAD + WIDTH * WIDTH
    return location[:heads], variance[heads : 2 * heads]


def place_of(index, length):
    return TAU + (1.0 - TAU) * (index.astype(F32) + 0.5) / (length.astype(F32) * UNIT)


def forward_kernel(heads, info, qkv, musig, table, mixed, logsum, states, memory, sums, probe_rows, value_cols, turned, cols):
    u = pl.program_id(0)
    width = heads * HEAD_DIM
    start, length = info[0, u], info[1, u]
    base = pl.multiple_of(u * UNIT, UNIT)
    here = pl.ds(base, UNIT)

    @pl.when(u == 0)
    def _():
        memory[...] = jnp.zeros_like(memory)

    @pl.when((start == u) & (u > 0))
    def _():
        scale = term_scale(info[1, jnp.maximum(u - 1, 0)])
        stacked = jnp.concatenate([memory[...], sums[...] * scale], axis=0)
        memory[...] = dot(table[...], split3(stacked))
        rows = dot(musig[...], memory[:, :LANES], precision=HIGHEST) * (1.0 / math.sqrt(HEAD_DIM))
        probe_rows[...] = jnp.where(head_rows(heads, LANES), rows, 0.0)
        value_cols[...] = memory[:, LANES:].T.astype(BF16)

    @pl.when(start == u)
    def _():
        states[0] = memory[...]
        sums[...] = jnp.zeros_like(sums)

    value_rows = qkv[here, 2 * LANES : 3 * LANES]
    cols[u] = value_rows.astype(F32).T.astype(BF16)

    token = lax.broadcasted_iota(jnp.int32, (LIVE, UNIT), 1) + (u - start) * UNIT
    centre = (lax.broadcasted_iota(jnp.int32, (LIVE, UNIT), 0) + LIVE).astype(F32) / (BASIS - 1)
    gap = place_of(token, length) - centre
    psi = jnp.exp(gap * gap * (-0.5 / (WIDTH * WIDTH)))
    psi_high = psi.astype(BF16)
    psi_low = (psi - psi_high.astype(F32)).astype(BF16)
    pairs = qkv[here, LANES : 3 * LANES]
    sums[...] += dot(psi_high, pairs) + dot(psi_low, pairs)

    query = qkv[here, 0:LANES]
    lane_head = lax.broadcasted_iota(jnp.int32, (UNIT, LANES), 1) // HEAD_DIM

    def attend(blocks):
        first = pl.multiple_of(start * UNIT, UNIT)
        keys = qkv[pl.ds(first, blocks * UNIT), LANES : 2 * LANES]
        causal = lax.broadcasted_iota(jnp.int32, (UNIT, UNIT), 0) <= lax.broadcasted_iota(
            jnp.int32, (UNIT, UNIT), 1
        )
        for h in range(heads):
            own = jnp.where(lane_head == h, query.astype(F32) * (1.0 / math.sqrt(HEAD_DIM)), 0.0).astype(BF16)
            scores = [dot(keys[j * UNIT : (j + 1) * UNIT], own, ((1,), (1,))) for j in range(blocks)]
            scores[-1] = jnp.where(causal, scores[-1], -1e30)
            highest = functools.reduce(jnp.maximum, [jnp.max(s, axis=0, keepdims=True) for s in scores])
            weights = [jnp.exp(s - highest) for s in scores]
            total = sum(jnp.sum(w, axis=0, keepdims=True) for w in weights)
            rows = slice(h * HEAD_DIM, (h + 1) * HEAD_DIM)
            result = sum(dot(cols[start + j, rows], weights[j].astype(BF16)) for j in range(blocks))
            turned[rows] = result * (1.0 / total)
            logsum[h : h + 1] = highest + jnp.log(total)

    for blocks in range(1, 5):
        pl.when(u - start + 1 == blocks)(functools.partial(attend, blocks))

    @pl.when(start > 0)
    def _():
        probes = probe_rows[...]
        high = probes.astype(BF16)
        rest = probes - high.astype(F32)
        mid = rest.astype(BF16)
        low = (rest - mid.astype(F32)).astype(BF16)
        logits = sum(dot(part, query, ((1,), (1,))) for part in (high, mid, low))
        location, variance = read_parts(logits, heads)
        fall = -0.5 / variance
        peak = WIDTH * lax.rsqrt(variance)
        centres = lax.broadcasted_iota(jnp.int32, (BASIS, UNIT), 0).astype(F32) / (BASIS - 1)
        for h in range(heads):
            gap = centres - location[h : h + 1]
            density = jnp.exp(gap * gap * fall[h : h + 1]).astype(BF16)
            rows = slice(h * HEAD_DIM, (h + 1) * HEAD_DIM)
            turned[rows] += dot(value_cols[rows], density) * peak[h : h + 1]

    mixed[...] = turned[...].T.astype(BF16)


def backward_kernel(
    heads, info, qkv, grad_mixed, logsum, states, musig, musig_cols, table, out, probe_grad,
    carried, spread, value_high, value_low, grad_values, probe_rows, probe_cols, row_grad, key_grad, value_grad, cols, turned,
):
    step = pl.program_id(0)
    units = pl.num_programs(0)
    u = units - 1 - step
    width = heads * HEAD_DIM
    start, length = info[0, u], info[1, u]
    base = pl.multiple_of(u * UNIT, UNIT)
    here = pl.ds(base, UNIT)

    @pl.when(step == 0)
    def _():
        carried[...] = jnp.zeros_like(carried)
        probe_grad[...] = jnp.zeros_like(probe_grad)
        for i in range(cols.shape[0]):
            cols[i] = qkv[i * UNIT : (i + 1) * UNIT, LANES : 2 * LANES].astype(F32).T.astype(BF16)

    @pl.when(u + 1 == start + length)
    def _():
        seg_rows = pl.ds(pl.multiple_of(start * UNIT, UNIT), UNIT)
        key_grad[...] = jnp.zeros_like(key_grad)
        value_grad[...] = jnp.zeros_like(value_grad)
        grad_values[...] = jnp.zeros_like(grad_values)
        row_grad[...] = jnp.zeros_like(row_grad)
        rows = dot(musig[...], states[0, :, :LANES], precision=HIGHEST) * (1.0 / math.sqrt(HEAD_DIM))
        rows = jnp.where(head_rows(heads, LANES), rows, 0.0)
        probe_rows[...] = rows
        probe_cols[...] = jnp.concatenate([rows, jnp.zeros((120, LANES), F32)], axis=0).T
        value = states[0, :, LANES:]
        high = value.astype(BF16)
        value_high[...] = high
        value_low[...] = (value - high.astype(F32)).astype(BF16)

    query = qkv[here, 0:LANES]
    given = jnp.concatenate([grad_mixed[...], jnp.zeros((UNIT, LANES - width), BF16)], axis=1)
    lane_head = lax.broadcasted_iota(jnp.int32, (UNIT, LANES), 1) // HEAD_DIM

    def attend_back(blocks):
        first = pl.multiple_of(start * UNIT, UNIT)
        keys = qkv[pl.ds(first, blocks * UNIT), LANES : 2 * LANES]
        values = qkv[pl.ds(first, blocks * UNIT), 2 * LANES : 3 * LANES]
        causal = lax.broadcasted_iota(jnp.int32, (UNIT, UNIT), 0) <= lax.broadcasted_iota(
            jnp.int32, (UNIT, UNIT), 1
        )
        for h in range(heads):
            own = jnp.where(lane_head == h, query.astype(F32) * (1.0 / math.sqrt(HEAD_DIM)), 0.0).astype(BF16)
            own_given = jnp.where(lane_head == h, given.astype(F32), 0.0).astype(BF16)
            probs, products = [], []
            inner = jnp.zeros((1, UNIT), F32)
            for j in range(blocks):
                part = slice(j * UNIT, (j + 1) * UNIT)
                score = dot(keys[part], own, ((1,), (1,)))
                if j == blocks - 1:
                    score = jnp.where(causal, score, -1e30)
                prob = jnp.exp(score - logsum[h : h + 1])
                product = prob * dot(values[part], own_given, ((1,), (1,)))
                inner += jnp.sum(product, axis=0, keepdims=True)
                probs.append(prob)
                products.append(product)
            rows = slice(h * HEAD_DIM, (h + 1) * HEAD_DIM)
            result = jnp.zeros((HEAD_DIM, UNIT), F32)
            for j in range(blocks):
                part = slice(j * UNIT, (j + 1) * UNIT)
                grad_score = (products[j] - probs[j] * inner).astype(BF16)
                key_grad[part] += dot(grad_score, own)
                value_grad[part] += dot(probs[j].astype(BF16), own_given)
                result += dot(cols[start + j, rows], grad_score)
            turned[rows] = result * (1.0 / math.sqrt(HEAD_DIM))

    for blocks in range(1, 5):
        pl.when(u - start + 1 == blocks)(functools.partial(attend_back, blocks))

    @pl.when(start > 0)
    def _():
        probes = probe_rows[...]
        high = probes.astype(BF16)
        rest = probes - high.astype(F32)
        mid = rest.astype(BF16)
        low = (rest - mid.astype(F32)).astype(BF16)
        logits = sum(dot(part, query, ((1,), (1,))) for part in (high, mid, low))
        location, variance = read_parts(logits, heads)
        inverse = 1.0 / variance
        fall = -0.5 * inverse
        peak = WIDTH * lax.rsqrt(variance)
        centres = lax.broadcasted_iota(jnp.int32, (BASIS, UNIT), 0).astype(F32) / (BASIS - 1)
        along, across = [], []
        for h in range(heads):
            own_given = jnp.where(lane_head == h, given.astype(F32), 0.0).astype(BF16)
            gap = centres - location[h : h + 1]
            square = gap * gap
            density = jnp.exp(square * fall[h : h + 1]) * peak[h : h + 1]
            grad_density = dot(value_high[...], own_given, ((1,), (1,))) + dot(
                value_low[...], own_given, ((1,), (1,))
            )
            grad_values[...] += dot(density.astype(BF16), own_given)
            weighed = density * grad_density
            zeroth = jnp.sum(weighed, axis=0, keepdims=True)
            first = jnp.sum(weighed * gap, axis=0, keepdims=True)
            second = jnp.sum(weighed * square, axis=0, keepdims=True)
            along.append(first * inverse[h : h + 1])
            across.append(0.5 * inverse[h : h + 1] * (second * inverse[h : h + 1] - zeroth))
        sigmoid = 1.0 / (1.0 + jnp.exp(-logits))
        grad_location = jnp.concatenate(along, axis=0) * location * (1.0 - location)
        grad_variance = jnp.concatenate(across, axis=0) * SPREAD * sigmoid[heads : 2 * heads]
        grad_logits = jnp.concatenate(
            [grad_location, grad_variance, jnp.zeros((8 - 2 * heads, UNIT), F32)], axis=0
        )
        padded = jnp.concatenate([grad_logits, jnp.zeros((120, UNIT), F32)], axis=0)
        turned[...] += dot(probe_cols[...], padded, precision=HIGHEST)[:width]
        row_grad[...] += dot(grad_logits, query.astype(F32), precision=HIGHEST)

    local = pl.ds(pl.multiple_of((u - start) * UNIT, UNIT), UNIT)

    @pl.when(start + length < units)
    def _():
        token = lax.broadcasted_iota(jnp.int32, (UNIT, LIVE), 0) + (u - start) * UNIT
        centre = (lax.broadcasted_iota(jnp.int32, (UNIT, LIVE), 1) + LIVE).astype(F32) / (BASIS - 1)
        gap = place_of(token, length) - centre
        psi = jnp.exp(gap * gap * (-0.5 / (WIDTH * WIDTH))).astype(BF16)
        pair_grad = dot(psi, spread[...])
        key_grad[local] += pair_grad[:, :LANES]
        value_grad[local] += pair_grad[:, LANES:]

    query_grad = turned[...].T.astype(BF16)
    out[:, :LANES] = jnp.concatenate([query_grad, jnp.zeros((UNIT, LANES - width), BF16)], axis=1)
    out[:, LANES : 2 * LANES] = key_grad[local].astype(BF16)
    out[:, 2 * LANES :] = value_grad[local].astype(BF16)

    @pl.when((u == start) & (start > 0))
    def _():
        rows = jnp.where(head_rows(heads, LANES), row_grad[...], 0.0) * (1.0 / math.sqrt(HEAD_DIM))
        probe_grad[...] += dot(rows, states[0, :, :LANES], ((1,), (1,)), HIGHEST)
        padded = jnp.concatenate([rows, jnp.zeros((120, LANES), F32)], axis=0)
        grad_keys = dot(musig_cols[...], padded, precision=HIGHEST)
        total = carried[...] + jnp.concatenate([grad_keys, grad_values[...]], axis=1)
        moved = dot(table[...], split3(total))
        carried[...] = moved[:BASIS]
        scale = term_scale(info[1, jnp.maximum(start - 1, 0)])
        spread[...] = (moved[BASIS:] * scale).astype(BF16)


def segment_info(lengths, units):
    slot_units = lengths // UNIT
    slots = jnp.arange(lengths.shape[0], dtype=jnp.int32)
    ends = jnp.sum(jnp.where(slots[None, :] <= slots[:, None], slot_units[None, :], 0), axis=1)
    starts = ends - slot_units
    unit = jnp.arange(units, dtype=jnp.int32)[:, None]
    member = (unit >= starts[None, :]) & (unit < ends[None, :])
    start = jnp.sum(jnp.where(member, starts[None, :], 0), axis=1)
    length = jnp.sum(jnp.where(member, slot_units[None, :], 0), axis=1)
    place = jnp.sum(((ends[None, :] <= unit) & (slot_units > 0)[None, :]).astype(jnp.int32), axis=1)
    return jnp.stack([start, length, place]).astype(jnp.int32)


def attention_forward(info, qkv, musig, heads):
    group = qkv.shape[0]
    units = group // UNIT
    width = heads * HEAD_DIM
    table = jnp.asarray(basis_tables()[0])
    whole = lambda shape: pl.BlockSpec(shape, lambda i, info: (0,) * len(shape))
    return pl.pallas_call(
        functools.partial(forward_kernel, heads),
        grid_spec=pltpu.PrefetchScalarGridSpec(
            num_scalar_prefetch=1,
            grid=(units,),
            in_specs=[whole(qkv.shape), whole(musig.shape), whole(table.shape)],
            out_specs=[
                pl.BlockSpec((UNIT, width), lambda i, info: (i, 0)),
                pl.BlockSpec((8, UNIT), lambda i, info: (0, i)),
                pl.BlockSpec((1, BASIS, 2 * LANES), lambda i, info: (info[2, i], 0, 0)),
            ],
            scratch_shapes=[
                pltpu.VMEM((BASIS, 2 * LANES), F32),
                pltpu.VMEM((LIVE, 2 * LANES), F32),
                pltpu.VMEM((8, LANES), F32),
                pltpu.VMEM((LANES, BASIS), BF16),
                pltpu.VMEM((width, UNIT), F32),
                pltpu.VMEM((units, LANES, UNIT), BF16),
            ],
        ),
        out_shape=[
            jax.ShapeDtypeStruct((group, width), BF16),
            jax.ShapeDtypeStruct((8, group), F32),
            jax.ShapeDtypeStruct((units, BASIS, 2 * LANES), F32),
        ],
        compiler_params=pltpu.CompilerParams(vmem_limit_bytes=56 << 20),
        name="attention_forward",
    )(info, qkv, musig, table)


def attention_backward(info, qkv, grad_mixed, logsum, states, musig, musig_cols, heads):
    group = qkv.shape[0]
    units = group // UNIT
    width = heads * HEAD_DIM
    table = jnp.asarray(basis_tables()[1])
    last = units - 1
    whole = lambda shape: pl.BlockSpec(shape, lambda i, info: (0,) * len(shape))
    return pl.pallas_call(
        functools.partial(backward_kernel, heads),
        grid_spec=pltpu.PrefetchScalarGridSpec(
            num_scalar_prefetch=1,
            grid=(units,),
            in_specs=[
                whole(qkv.shape),
                pl.BlockSpec((UNIT, width), lambda i, info: (last - i, 0)),
                pl.BlockSpec((8, UNIT), lambda i, info: (0, last - i)),
                pl.BlockSpec((1, BASIS, 2 * LANES), lambda i, info: (info[2, last - i], 0, 0)),
                whole(musig.shape),
                whole(musig_cols.shape),
                whole(table.shape),
            ],
            out_specs=[
                pl.BlockSpec((UNIT, 3 * LANES), lambda i, info: (last - i, 0)),
                whole(musig.shape),
            ],
            scratch_shapes=[
                pltpu.VMEM((BASIS, 2 * LANES), F32),
                pltpu.VMEM((LIVE, 2 * LANES), BF16),
                pltpu.VMEM((BASIS, LANES), BF16),
                pltpu.VMEM((BASIS, LANES), BF16),
                pltpu.VMEM((BASIS, LANES), F32),
                pltpu.VMEM((8, LANES), F32),
                pltpu.VMEM((LANES, 128), F32),
                pltpu.VMEM((8, LANES), F32),
                pltpu.VMEM((4 * UNIT, LANES), F32),
                pltpu.VMEM((4 * UNIT, LANES), F32),
                pltpu.VMEM((units, LANES, UNIT), BF16),
                pltpu.VMEM((width, UNIT), F32),
            ],
        ),
        out_shape=[
            jax.ShapeDtypeStruct((group, 3 * LANES), BF16),
            jax.ShapeDtypeStruct(musig.shape, F32),
        ],
        compiler_params=pltpu.CompilerParams(vmem_limit_bytes=56 << 20),
        name="attention_backward",
    )(info, qkv, grad_mixed, logsum, states, musig, musig_cols, table)


def layer_norm(values, gain, shift):
    centred = values - jnp.mean(values, axis=-1, keepdims=True)
    inverse = lax.rsqrt(jnp.mean(centred * centred, axis=-1, keepdims=True) + EPSILON)
    normal = centred * inverse
    return (normal * gain + shift, normal, inverse)


def norm_back(grad, normal, inverse, gain):
    scaled = grad * gain
    return inverse * (
        scaled
        - jnp.mean(scaled, axis=-1, keepdims=True)
        - normal * jnp.mean(scaled * normal, axis=-1, keepdims=True)
    )


def gelu_tanh(values):
    return jax.nn.gelu(values, approximate=True)


def gather_weight(shard, members):
    rows = shard.shape[0] // members
    mine = lax.dynamic_slice_in_dim(shard, lax.axis_index("dp") * rows, rows, 0)
    return lax.all_gather(mine, ("head", "dp"), axis=0, tiled=True)


def scatter_grad(grad, members):
    heads = lax.axis_size("head")
    rows = grad.shape[0] // (heads * members)
    part = lax.psum_scatter(grad, ("head", "dp"), scatter_dimension=0, tiled=True)
    return lax.all_gather(part, "dp", axis=0, tiled=True).astype(F32)


def local(
    inputs, seg_lengths, ln1_gain, ln1_bias, qkv_weight, qkv_bias, out_weight, out_bias, mem_mu, mem_sig,
    ln2_gain, ln2_bias, ff_in, ff_in_bias, ff_out, ff_out_bias, cotangent,
):
    own_rows, model = inputs.shape
    heads_axis = lax.axis_size("head")
    members = lax.axis_size("dp")
    group = heads_axis * own_rows
    units = group // UNIT
    width = qkv_weight.shape[2]
    heads = width // HEAD_DIM
    hidden_part = ff_in.shape[1]

    info = segment_info(seg_lengths[0], units)
    source = inputs.astype(F32)
    gain_one = ln1_gain.astype(F32)
    gain_two = ln2_gain.astype(F32)
    normed1, normal1, inverse1 = layer_norm(source, gain_one, ln1_bias.astype(F32))
    first_rows = lax.all_gather(normed1.astype(BF16), "head", axis=0, tiled=True)

    out_full = gather_weight(out_weight, members)
    in_full = gather_weight(ff_in, members).reshape(heads_axis, model, hidden_part)
    back_full = gather_weight(ff_out, members)
    in_bias = lax.all_gather(ff_in_bias, "head", axis=0, tiled=True).astype(F32)

    pad = ((0, 0), (0, 0), (0, LANES - width))
    weight_flat = jnp.pad(qkv_weight, pad).reshape(model, 3 * LANES)
    bias_flat = jnp.pad(qkv_bias, pad[1:]).reshape(3 * LANES).astype(F32)
    qkv = (jnp.dot(first_rows, weight_flat, preferred_element_type=F32) + bias_flat).astype(BF16)
    musig = jnp.concatenate([mem_mu, mem_sig, jnp.zeros((8 - 2 * heads, BASIS), BF16)], axis=0).astype(F32)
    musig_cols = jnp.pad(musig.T, ((0, 0), (0, 120)))
    mixed_heads, logsum, states = attention_forward(info, qkv, musig, heads)

    mixed = lax.all_to_all(mixed_heads, "head", split_axis=0, concat_axis=1, tiled=True)
    attended = jnp.dot(mixed, out_full, preferred_element_type=F32)
    residual = source + attended + out_bias.astype(F32)
    normed2, normal2, inverse2 = layer_norm(residual, gain_two, ln2_bias.astype(F32))
    second = normed2.astype(BF16)
    grad_out = cotangent.astype(F32)
    hidden = jnp.einsum("rd,zdf->rzf", second, in_full, preferred_element_type=F32).reshape(
        own_rows, -1
    ) + in_bias
    activation, gelu_back = jax.vjp(gelu_tanh, hidden)
    act_low = activation.astype(BF16)
    outputs = residual + jnp.dot(act_low, back_full, preferred_element_type=F32) + ff_out_bias.astype(F32)
    grad_act = jnp.dot(cotangent, back_full.T, preferred_element_type=F32)
    grad_hidden = gelu_back(grad_act)[0].astype(BF16)
    grad_second = jnp.einsum(
        "rzf,zdf->rd", grad_hidden.reshape(own_rows, heads_axis, hidden_part), in_full, preferred_element_type=F32
    )
    grad_residual = grad_out + norm_back(grad_second, normal2, inverse2, gain_two)
    grad_attended = grad_residual.astype(BF16)
    grad_mixed = jnp.dot(grad_attended, out_full.T, preferred_element_type=F32).astype(BF16)
    grad_heads = lax.all_to_all(grad_mixed, "head", split_axis=1, concat_axis=0, tiled=True)

    ff_out_grad = jnp.dot(act_low.T, cotangent, preferred_element_type=F32).astype(BF16)
    ff_in_grad = jnp.einsum(
        "rd,rzf->zdf", second, grad_hidden.reshape(own_rows, heads_axis, hidden_part), preferred_element_type=F32
    ).astype(BF16)
    out_weight_grad = jnp.dot(mixed.T, grad_attended, preferred_element_type=F32).astype(BF16)
    ff_out_sum = scatter_grad(ff_out_grad, members)
    ff_in_sum = scatter_grad(ff_in_grad.reshape(heads_axis * model, hidden_part), members)
    out_weight_sum = scatter_grad(out_weight_grad, members)

    grad_qkv, probe_grad = attention_backward(
        info, qkv, grad_heads, logsum, states, musig, musig_cols, heads
    )
    grad_first = lax.psum_scatter(
        jnp.dot(grad_qkv, weight_flat.T, preferred_element_type=F32).astype(BF16),
        "head", scatter_dimension=0, tiled=True,
    ).astype(F32)
    qkv_weight_grad = (
        jnp.dot(first_rows.T, grad_qkv, preferred_element_type=F32)
        .reshape(model, 3, LANES)[:, :, :width].astype(BF16)
    )
    qkv_bias_grad = jnp.sum(grad_qkv.astype(F32), axis=0).reshape(3, LANES)[:, :width]
    grad_source = grad_residual + norm_back(grad_first, normal1, inverse1, gain_one)
    qkv_weight_sum = lax.psum(qkv_weight_grad, "dp").astype(F32)
    ff_in_bias_part = jnp.sum(grad_hidden.astype(F32), axis=0)
    own_small = lax.psum((qkv_bias_grad, probe_grad), "dp")
    shared = lax.psum(
        jnp.concatenate([
            jnp.sum(grad_first * normal1, axis=0), jnp.sum(grad_first, axis=0), jnp.sum(grad_residual, axis=0),
            jnp.sum(grad_second * normal2, axis=0), jnp.sum(grad_second, axis=0), jnp.sum(grad_out, axis=0),
            ff_in_bias_part,
        ]),
        ("dp", "head"),
    )
    rows = [shared[i * model : (i + 1) * model] for i in range(6)]
    ff_in_bias_grad = lax.dynamic_slice_in_dim(shared, 6 * model + lax.axis_index("head") * hidden_part, hidden_part, 0)
    return (
        outputs.astype(BF16), grad_source.astype(BF16), rows[0], rows[1], qkv_weight_sum, own_small[0], out_weight_sum,
        rows[2], own_small[1][:heads], own_small[1][heads : 2 * heads], rows[3], rows[4], ff_in_sum, ff_in_bias_grad,
        ff_out_sum, rows[5],
    )


def solution(mesh):
    rows, whole = P(("dp", "head"), None), P()
    return jax.shard_map(
        local,
        mesh=mesh,
        in_specs=(
            rows, P("dp", None), whole, whole, P(None, None, "head"), P(None, "head"), P("head", None), whole,
            P("head", None), P("head", None), whole, whole, P(None, "head"), P("head"), P("head", None), whole, rows,
        ),
        out_specs=(
            rows, rows, whole, whole, P(None, None, "head"), P(None, "head"), P("head", None), whole,
            P("head", None), P("head", None), whole, whole, P(None, "head"), P("head"), P("head", None), whole,
        ),
        check_vma=False,
    )
```

time: 1620 us -> 799 us (0.49)
  local copies, waits for them, and re-layouts: 480 us -> 21 us
  matrix products: 384 us -> 69.6 us
  other arithmetic: 225 us -> 25.1 us
  Pallas kernels: 0 us -> 69.2 us
  waiting for transfers between devices: 423 us -> 478 us
  blocking collectives: 63.5 us -> 104 us
    dot_general x62 -> x12, matrix products: 375 us -> 69.6 us  [the longest x1 9.59 us: local(): jnp.dot(act_low, back_full, preferred_element_type=F32)]
    dynamic_update_slice x40 -> x0, local copies, waits for them, and re-layouts: 279 us -> none  [the longest x24 158 us: memory_read(): lax.scan(advance_step, jnp.zeros_like(projected[0]), (projected, lengths))]
    another operation x23 -> x1, other arithmetic: 133 us -> 0.6 us  [segment_info(): return jnp.stack([start, length, place]).astype(jnp.int32)]
    dynamic_slice x44 -> x3, local copies, waits for them, and re-layouts: 82.6 us -> 3.66 us  [gather_weight(): mine = lax.dynamic_slice_in_dim(shard, lax.axis_index('dp') * rows, rows, 0)]
    pallas_call x0 -> x2, Pallas kernels: none -> 69.2 us  [the longest x1 43.4 us: attention_backward(): pl.pallas_call(functools.partial(backward_kernel, heads), grid_spec=pltpu...]
    reduce_scatter x1, waiting for transfers between devices: 0.01 us -> 59.3 us  [local(): lax.psum_scatter(jnp.dot(grad_qkv, weight_flat.T, preferred_element_type=...]
    all_gather x0 -> x2, blocking collectives: none -> 39.4 us  [the longest x1 29.9 us: local(): in_bias = lax.all_gather(ff_in_bias, 'head', axis=0, tiled=True).astype(F32)]
    unnamed x212 -> x53, local copies, waits for them, and re-layouts: 31.3 us -> 0.34 us
  transfers between devices with their start and end apart: 9 -> 13, of which waited for: 7 -> 10; matrix products, arithmetic and copies ran while one was open for 14% -> 12% of each run, Pallas kernels for 0% -> 9%
where the time goes in v1:
time: 799 us; the launch traced here: 790 us
  waiting for transfers between devices  478 us (60%)
  blocking collectives  104 us (13%)
  matrix products  69.6 us (9%)
  Pallas kernels  69.2 us (9%)
  other arithmetic  25.1 us (3%)
  local copies, waits for them, and re-layouts  21 us (3%)
  between operations  14.8 us (2%)
  starting transfers between devices  8.33 us (1%)
    reduce_scatter x3, waiting for transfers between devices, scatter_grad(): lax.psum_scatter(grad, ('head', 'dp'), scatter_dimension=0, tiled=True)  178 us
    all_gather x3, waiting for transfers between devices, gather_weight(): return lax.all_gather(mine, ('head', 'dp'), axis=0, tiled=True)  110 us
    all_gather x1, waiting for transfers between devices, local(): lax.all_gather(normed1.astype(BF16), 'head', axis=0, tiled=True)  60.7 us
    reduce_scatter x1, waiting for transfers between devices, local(): lax.psum_scatter(jnp.dot(grad_qkv, weight_flat.T, preferred_element_type=...  59.3 us
    psum x1, waiting for transfers between devices, local(): qkv_weight_sum = lax.psum(qkv_weight_grad, 'dp').astype(F32)  47.8 us
    pallas_call x1, Pallas kernels, attention_backward(): pl.pallas_call(functools.partial(backward_kernel, heads), grid_spec=pltpu...  43.4 us
    psum x1, blocking collectives, local(): lax.psum(jnp.concatenate([jnp.sum(grad_first * normal1, axis=0), jnp.sum(...  40.4 us
    all_gather x1, blocking collectives, local(): in_bias = lax.all_gather(ff_in_bias, 'head', axis=0, tiled=True).astype(F32)  29.9 us
  transfers between devices with their start and end apart: 13, of which 10 were waited for; matrix products, arithmetic and copies ran while one was open for 12% of the time, Pallas kernels for 9%

profile of v1, /device:TPU:0, one launch (start us, length us, event | category | flops | bytes accessed | tf_op | source)
XLA Modules:
  0.0 790.1 jit_solution(4793275384690307229)
XLA Ops:
  19.7 60.7 %all-gather.8.cloned.1.call-done = bf16[2048,768]{1,0:T(8,128)(2,1)} async-done(((bf16[512,768]{1,0:T(8,128)(2,1)}), bf16[2048,768]{1,0:T(8,128)(2,1)}) %all-gather.8.cloned.1.call-update) | async-done | bytes 3145744 | tf_op jit(solution)/shard_map/all_gather | solution.py:457
  80.4 6.2 add_convert_fusion.qkv
  86.6 25.9 %attention_forward.1 = (bf16[2048,192]{1,0:T(8,128)(2,1)}, f32[8,2048]{1,0:T(8,128)}, f32[8,512,512]{2,1,0:T(8,128)}) custom-call(s32[3,8]{1,0:T(4,128)} %pad_add_fusion.info, bf16[2048,768]{1,0:T(8,128)(2,1)} %add_convert_fusion.qkv, f32[8,512]{1,0:T(8,128)} %maximum_convert_fusion.musig, bf16[512,2304]{1,0:T(8,128)(2,1)} %constant.74.clone.table), custom_call_target="tpu_custom_call" | custom-call | tf_op jit(solution)/shard_map/attention_forward/pallas_call | solution.py:327
  118.4 29.9 %all-gather = bf16[4,1,768]{2,1,0:T(2,128)(2,1)S(1)} all-gather(bf16[1,1,768]{2,1,0:T(2,128)(2,1)S(1)} %reshape.124), channel_id=1, replica_groups=mesh['dp'=8,'head'=4] {'head'}, dimensions={0}, use_global_device_ids=true | all-gather | bytes 7680 | tf_op jit(solution)/shard_map/all_gather | solution.py:462
  150.8 58.1 %all-gather.12.cloned.1.call-done = bf16[3072,768]{1,0:T(8,128)(2,1)} async-done(((bf16[96,768]{1,0:T(8,128)(2,1)}), bf16[3072,768]{1,0:T(8,128)(2,1)}) %all-gather.12.cloned.1.call-update) | async-done | bytes 4718608 | tf_op jit(solution)/shard_map/all_gather | solution.py:429
  208.9 6.6 copy.79
  215.5 7.1 fusion.44
  222.7 52.1 %all-gather.14.cloned.1.call-done = bf16[3072,768]{1,0:T(8,128)(2,1)} async-done(((bf16[96,768]{1,0:T(8,128)(2,1)}), bf16[3072,768]{1,0:T(8,128)(2,1)}) %all-gather.14.cloned.1.call-update) | async-done | bytes 4718608 | tf_op jit(solution)/shard_map/all_gather | solution.py:429
  274.7 9.1 %convert_reduce_fusion.1 = (f32[3072]{0:T(1024)S(1)}, bf16[512,3072]{1,0:T(8,128)(2,1)S(1)}) fusion(f32[512,3072]{1,0:T(8,128)} %fusion.44, f32[3072]{0:T(1024)S(1)} %bitcast.100, bf16[3072,768]{1,0:T(8,128)(2,1)} %all-gather.14.cloned.1.call-done, bf16[512,768]{1,0:T(8,128)(2,1)} %param.35), kind=kOutput, calls=%fused_computation.15 | convolution fusion | flops 2452091904 | bytes 14966784 | tf_op jit(solution)/shard_map/dot_general | solution.py:484
  283.8 4.9 fusion.14
  288.9 8.9 %convolution_convert_fusion = bf16[3072,768]{1,0:T(8,128)(2,1)} fusion(bf16[512,768]{1,0:T(8,128)(2,1)} %param.35, f32[512,3072]{1,0:T(8,128)} %fusion.44, f32[3072]{0:T(1024)S(1)} %bitcast.101), kind=kOutput, calls=%fused_computation.18 | convolution fusion | flops 2434007040 | bytes 11808768 | tf_op jit(solution)/shard_map/dot_general | solution.py:494
  297.8 7.1 fusion.36
  318.3 18.1 %all-to-all-done.1 = bf16[512,4,192]{0,2,1:T(8,128)(2,1)} async-done(((bf16[512,4,192]{0,2,1:T(8,128)(2,1)}), bf16[512,4,192]{0,2,1:T(8,128)(2,1)}, u32[]{:S(2)}, u32[]{:S(2)}) %all-to-all-start.1) | async-done | bytes 786464 | tf_op jit(solution)/shard_map/all_to_all | solution.py:492
  338.8 43.4 %attention_backward.1 = (bf16[2048,768]{1,0:T(8,128)(2,1)}, f32[8,512]{1,0:T(8,128)}) custom-call(s32[3,8]{1,0:T(4,128)} %pad_add_fusion.info, bf16[2048,768]{1,0:T(8,128)(2,1)} %add_convert_fusion.qkv, bf16[2048,192]{1,0:T(8,128)(2,1)} %bitcast.90, f32[8,2048]{1,0:T(8,128)} %get-tuple-element.22.logsum, f32[8,512,512]{2,1,0:T(8,128)} %get-tuple-element.23.states, ...), custom_call_target="tpu_custom_call" | custom-call | tf_op jit(solution)/shard_map/attention_backward/pallas_call | solution.py:364
  382.2 4.5 convolution_convert_fusion.3
  387.8 6.5 convolution_convert_fusion.1
  395.0 9.6 %add_convert_fusion.1 = bf16[512,768]{1,0:T(8,128)(2,1)} fusion(f32[512,768]{1,0:T(8,128)} %copy-done.3, bf16[3072,768]{1,0:T(8,128)(2,1)} %all-gather.14.cloned.1.call-done, f32[768]{0:T(1024)S(1)} %convert_element_type.128, f32[512,3072]{1,0:T(8,128)} %fusion.44, f32[3072]{0:T(1024)S(1)} %bitcast.102), kind=kOutput, calls=%fused_computation.57 | convolution fusion | flops 2432827392 | bytes 13384704 | tf_op jit(solution)/shard_map/dot_general | solution.py:483
  405.3 24.6 %all-reduce.3 = (f32[3,192]{1,0:T(4,128)}, f32[8,512]{1,0:T(8,128)S(1)}) all-reduce(f32[3,192]{1,0:T(4,128)S(1)} %bitcast.99, f32[8,512]{1,0:T(8,128)S(1)} %copy-done.9), channel_id=1, replica_groups=mesh['dp'=8,'head'=4] {'dp'}, use_global_device_ids=true, to_apply=%region_23.24 | all-reduce | flops 4672 | bytes 37376 | tf_op jit(solution)/shard_map/psum | solution.py:518
  430.5 76.5 %reduce-scatter.11.cloned.1.call-done = bf16[96,768]{1,0:T(8,128)(2,1)} async-done(((bf16[3072,768]{1,0:T(8,128)(2,1)}), bf16[96,768]{1,0:T(8,128)(2,1)}) %reduce-scatter.11.cloned.1.call-update) | async-done | bytes 147472 | tf_op jit(solution)/shard_map/reduce_scatter | solution.py:435
  507.0 101.0 %reduce-scatter.7.cloned.1.call-done = bf16[24,768]{1,0:T(8,128)(2,1)} async-done(((bf16[768,768]{1,0:T(8,128)(2,1)}), bf16[24,768]{1,0:T(8,128)(2,1)}) %reduce-scatter.7.cloned.1.call-update) | async-done | bytes 36880 | tf_op jit(solution)/shard_map/reduce_scatter | solution.py:435
  608.0 9.5 %all_gather.29 = bf16[192,768]{1,0:T(8,128)(2,1)S(1)} all-gather(bf16[24,768]{1,0:T(8,128)(2,1)} %reduce-scatter.7.cloned.1.call-done), channel_id=1, replica_groups=mesh['dp'=8,'head'=4] {'dp'}, dimensions={0}, use_global_device_ids=true | all-gather | bytes 331776 | tf_op jit(solution)/shard_map/all_gather | solution.py:436
  618.4 47.8 %all-reduce.6.cloned.1.call-done = bf16[768,3,192]{0,2,1:T(8,128)(2,1)} async-done(((bf16[768,3,192]{0,2,1:T(8,128)(2,1)}), bf16[768,3,192]{0,2,1:T(8,128)(2,1)}) %all-reduce.6.cloned.1.call-update) | async-done | bytes 884752 | tf_op jit(solution)/shard_map/psum | solution.py:516
  668.7 59.3 %reduce-scatter.5.cloned.1.call-done = bf16[512,768]{1,0:T(8,128)(2,1)} async-done(((bf16[2048,768]{1,0:T(8,128)(2,1)}), bf16[512,768]{1,0:T(8,128)(2,1)}) %reduce-scatter.5.cloned.1.call-update) | async-done | bytes 786448 | tf_op jit(solution)/shard_map/reduce_scatter | solution.py:506
  730.0 40.4 %psum.28 = f32[7680]{0:T(1024)S(1)} all-reduce(f32[7680]{0:T(1024)S(1)} %constant_dynamic-update-slice_fusion), channel_id=1, replica_groups=mesh['dp'=8,'head'=4] {'dp','head'}, use_global_device_ids=true, to_apply=%region_20.21 | all-reduce | flops 7680 | bytes 61440 | tf_op jit(solution)/shard_map/psum | solution.py:519
  (136 shorter events, 57.9 us)
Async XLA Ops:
  7.2 8.4 %copy-start = (bf16[768,768]{1,0:T(8,128)(2,1)S(1)}, bf16[768,768]{1,0:T(8,128)(2,1)}, u32[]{:S(2)}) copy-start(bf16[768,768]{1,0:T(8,128)(2,1)} %param.31) | copy-start | bytes 3538948
  7.2 73.2 %all-gather.8.cloned.1.call-start = ((), (), s32[]{:S(2)}) async-start(), calls=%async_computation.6 | async-start | bytes 3932160 | tf_op jit(solution)/shard_map/all_gather | solution.py:457
  8.7 9.2 %copy-start.13 = (bf16[3,192]{1,0:T(4,128)(2,1)S(1)}, bf16[3,192]{1,0:T(4,128)(2,1)}, u32[]{:S(2)}) copy-start(bf16[3,192]{1,0:T(4,128)(2,1)} %param.24) | copy-start | bytes 3460
  8.7 9.3 %copy-start.6 = (bf16[768,3,192]{0,2,1:T(8,128)(2,1)S(1)}, bf16[768,3,192]{0,2,1:T(8,128)(2,1)}, u32[]{:S(2)}) copy-start(bf16[768,3,192]{0,2,1:T(8,128)(2,1)} %param.23) | copy-start | bytes 2654212
  14.0 134.2 %all-gather.10.cloned.1.call-start = ((), (), s32[]{:S(2)}) async-start(), calls=%async_computation.7 | async-start | bytes 1216512 | tf_op jit(solution)/shard_map/all_gather | solution.py:429
  15.5 193.4 %all-gather.12.cloned.1.call-start = ((), (), s32[]{:S(2)}) async-start(), calls=%async_computation.8 | async-start | bytes 4866048 | tf_op jit(solution)/shard_map/all_gather | solution.py:429
  16.3 258.5 %all-gather.14.cloned.1.call-start = ((), (), s32[]{:S(2)}) async-start(), calls=%async_computation.9 | async-start | bytes 4866048 | tf_op jit(solution)/shard_map/all_gather | solution.py:429
  18.0 68.5 %copy-start.5 = (bf16[768,3,256]{0,2,1:T(8,128)(2,1)}, bf16[768,3,256]{0,2,1:T(8,128)(2,1)S(1)}, u32[]{:S(2)}) copy-start(bf16[768,3,256]{0,2,1:T(8,128)(2,1)S(1)} %pad.12) | copy-start | bytes 3538948
  112.5 35.8 %copy-start.2 = (bf16[512,768]{1,0:T(8,128)(2,1)S(1)}, bf16[512,768]{1,0:T(8,128)(2,1)}, u32[]{:S(2)}) copy-start(bf16[512,768]{1,0:T(8,128)(2,1)} %param.19) | copy-start | bytes 2359300
  114.7 33.5 %all-to-all-start = ((bf16[4,512,192]{1,2,0:T(8,128)(2,1)}), bf16[4,512,192]{1,2,0:T(8,128)(2,1)S(1)}, u32[]{:S(2)}, u32[]{:S(2)}) async-start(bf16[4,512,192]{1,2,0:T(8,128)(2,1)} %copy.78), calls=%async_computation | async-start | bytes 1572864 | tf_op jit(solution)/shard_map/all_to_all | solution.py:472
  118.2 276.4 %reduce-scatter.9.cloned.1.call-start = ((), (), s32[]{:S(2)}) async-start(), calls=%async_computation.13 | async-start | bytes 4866048 | tf_op jit(solution)/shard_map/reduce_scatter | solution.py:435
  150.5 147.3 %copy-start.3 = (f32[512,768]{1,0:T(8,128)}, f32[512,768]{1,0:T(8,128)S(1)}, u32[]{:S(2)}) copy-start(f32[512,768]{1,0:T(8,128)S(1)} %get-tuple-element.54) | copy-start | bytes 4718596
  288.7 218.3 %reduce-scatter.11.cloned.1.call-start = ((), (), s32[]{:S(2)}) async-start(), calls=%async_computation.15 | async-start | bytes 4866048 | tf_op jit(solution)/shard_map/reduce_scatter | solution.py:435
  297.8 7.1 copy-start.7
  311.2 25.1 %all-to-all-start.1 = ((bf16[512,4,192]{0,2,1:T(8,128)(2,1)}), bf16[512,4,192]{0,2,1:T(8,128)(2,1)}, u32[]{:S(2)}, u32[]{:S(2)}) async-start(bf16[512,4,192]{0,2,1:T(8,128)(2,1)} %bitcast.93), calls=%async_computation.1 | async-start | bytes 1572864 | tf_op jit(solution)/shard_map/all_to_all | solution.py:492
  315.5 292.5 %reduce-scatter.7.cloned.1.call-start = ((), (), s32[]{:S(2)}) async-start(), calls=%async_computation.12 | async-start | bytes 1216512 | tf_op jit(solution)/shard_map/reduce_scatter | solution.py:435
  317.3 348.8 %all-reduce.6.cloned.1.call-start = ((), (), s32[]{:S(2)}) async-start(), calls=%async_computation.11 | async-start | bytes 1769472 | tf_op jit(solution)/shard_map/psum | solution.py:516
  338.8 43.4 %copy-start.19 = (bf16[2048,768]{1,0:T(8,128)(2,1)S(1)}, bf16[2048,768]{1,0:T(8,128)(2,1)}, u32[]{:S(2)}) copy-start(bf16[2048,768]{1,0:T(8,128)(2,1)} %all-gather.8.cloned.1.call-done) | copy-start | bytes 9437188
  387.7 340.2 %reduce-scatter.5.cloned.1.call-start = ((), (), s32[]{:S(2)}) async-start(), calls=%async_computation.10 | async-start | bytes 3932160 | tf_op jit(solution)/shard_map/reduce_scatter | solution.py:506
  394.4 379.3 %all-gather.16.cloned.1.call-start = ((), (), s32[]{:S(2)}) async-start(), calls=%async_computation.14 | async-start | bytes 1327104 | tf_op jit(solution)/shard_map/all_gather | solution.py:436
  394.9 385.4 %all-gather.18.cloned.1.call-start = ((), (), s32[]{:S(2)}) async-start(), calls=%async_computation.16 | async-start | bytes 1327104 | tf_op jit(solution)/shard_map/all_gather | solution.py:436
  395.0 9.6 %copy-start.4 = (bf16[2048,768]{1,0:T(8,128)(2,1)S(1)}, bf16[2048,768]{1,0:T(8,128)(2,1)}, u32[]{:S(2)}) copy-start(bf16[2048,768]{1,0:T(8,128)(2,1)} %get-tuple-element.24) | copy-start | bytes 9437188
  618.4 111.5 %copy-start.12 = (f32[768]{0:T(1024)S(1)}, f32[768]{0:T(1024)}, u32[]{:S(2)}) copy-start(f32[768]{0:T(1024)} %get-tuple-element.26) | copy-start | bytes 9220
  773.7 9.5 %copy-start.1 = (bf16[768,768]{1,0:T(8,128)(2,1)S(1)}, bf16[768,768]{1,0:T(8,128)(2,1)}, u32[]{:S(2)}) copy-start(bf16[768,768]{1,0:T(8,128)(2,1)} %param.31) | copy-start | bytes 3538948
  (12 other events, 50.7 us)
Sparse Core Ops, SparseCore 0:
  14.1 66.1 all-gather.7
  83.8 58.1 all-gather.9
  145.5 63.3 all-gather.11
  212.2 62.4 all-gather.13
  288.8 105.7 reduce-scatter.8
  400.9 106.0 reduce-scatter.10
  512.6 95.2 reduce-scatter.6
  611.2 54.9 all-reduce.5
  668.4 59.4 reduce-scatter.4
  729.7 24.1 all-gather.15
  755.7 24.5 all-gather.17

commit v2 on v1

--- a/solution.py
+++ b/solution.py
@@ -403,6 +403,159 @@
     )(info, qkv, grad_mixed, logsum, states, musig, musig_cols, table)
 
 
+def middle_kernel(
+    place, source, cotangent, mixed, out_weight, vectors, in_bias, own_in, own_out, far_in, far_out,
+    outputs, grad_residual, grad_mixed, grad_in, grad_out, grad_out_weight, sums, grad_in_bias,
+    residual, inverse, second, second_cols, total, grad_second, in_now, out_now,
+):
+    r = pl.program_id(0)
+    own = place[0]
+    slices, rows = own_in.shape[0], own_in.shape[1]
+    model = source.shape[1]
+    hidden_part = own_in.shape[2]
+    out_bias, gain, shift, last_bias = (vectors[k : k + 1] for k in range(4))
+
+    @pl.when(r == 0)
+    def _():
+        value = source[...].astype(F32) + dot(mixed[...], out_weight[...]) + out_bias
+        residual[...] = value
+        centred = value - jnp.mean(value, axis=-1, keepdims=True)
+        factor = lax.rsqrt(jnp.mean(centred * centred, axis=-1, keepdims=True) + EPSILON)
+        inverse[...] = factor
+        normal = centred * factor
+        grad_residual[...] = normal
+        rounded = (normal * gain + shift).astype(BF16)
+        second[...] = rounded
+        second_cols[...] = rounded.astype(F32).T.astype(BF16)
+        total[...] = jnp.zeros_like(total)
+        grad_second[...] = jnp.zeros_like(grad_second)
+        grad_in_bias[...] = jnp.zeros_like(grad_in_bias)
+        for j in range(slices):
+            in_now[j * rows : (j + 1) * rows] = own_in[j]
+            out_now[j * rows : (j + 1) * rows] = own_out[j]
+
+    @pl.when(r > 0)
+    def _():
+        for j in range(slices):
+            in_now[j * rows : (j + 1) * rows] = far_in[0, j ^ own]
+            out_now[j * rows : (j + 1) * rows] = far_out[0, j ^ own]
+
+    half = hidden_part // 2
+    for t in range(2):
+        span = slice(t * half, (t + 1) * half)
+        hidden = dot(second[...], in_now[:, span]) + in_bias[pl.ds(r, 1), span]
+        cube = hidden * hidden
+        root = math.sqrt(2.0 / math.pi)
+        bent = jnp.tanh(hidden * (root + (root * 0.044715) * cube))
+        lifted = 0.5 + 0.5 * bent
+        activation = (hidden * lifted).astype(BF16)
+        slope = lifted + hidden * ((0.5 - 0.5 * bent * bent) * (root + (3.0 * root * 0.044715) * cube))
+        total[...] += dot(activation, out_now[span])
+        given = dot(cotangent[...], out_now[span], ((1,), (1,)))
+        grad_hidden = (given * slope).astype(BF16)
+        grad_second[...] += dot(grad_hidden, in_now[:, span], ((1,), (1,)))
+        grad_in_bias[pl.ds(r, 1), span] = jnp.sum(grad_hidden.astype(F32), axis=0, keepdims=True)
+        part = dot(activation, cotangent[...], ((0,), (0,))).astype(BF16)
+        per = half // rows
+        for k in range(per):
+            grad_out[0, (t * per + k) ^ own] = part[k * rows : (k + 1) * rows]
+        part = dot(second_cols[...], grad_hidden).astype(BF16)
+        for j in range(slices):
+            grad_in[0, j ^ own, :, span] = part[j * rows : (j + 1) * rows]
+
+    @pl.when(r == pl.num_programs(0) - 1)
+    def _():
+        given = cotangent[...].astype(F32)
+        outputs[...] = (residual[...] + total[...] + last_bias).astype(BF16)
+        normal = grad_residual[...]
+        grad = grad_second[...]
+        scaled = grad * gain
+        value = given + inverse[...] * (
+            scaled
+            - jnp.mean(scaled, axis=-1, keepdims=True)
+            - normal * jnp.mean(scaled * normal, axis=-1, keepdims=True)
+        )
+        sums[0:1] = jnp.sum(value, axis=0, keepdims=True)
+        sums[1:2] = jnp.sum(grad * normal, axis=0, keepdims=True)
+        sums[2:3] = jnp.sum(grad, axis=0, keepdims=True)
+        sums[3:4] = jnp.sum(given, axis=0, keepdims=True)
+        sums[4:8] = jnp.zeros((4, model), F32)
+        grad_residual[...] = value
+        rounded = value.astype(BF16)
+        grad_mixed[...] = dot(rounded, out_weight[...], ((1,), (1,))).astype(BF16)
+        grad_out_weight[...] = dot(mixed[...], rounded, ((0,), (0,))).astype(BF16)
+
+
+def middle(place, source, cotangent, mixed, out_weight, vectors, in_bias, own_in, own_out, far_in, far_out):
+    own_rows, model = source.shape
+    shards = far_in.shape[0] + 1
+    slices, rows, hidden_part = own_in.shape
+    whole = lambda shape: pl.BlockSpec(shape, lambda r, place: (0,) * len(shape))
+    far = pl.BlockSpec((1,) + own_in.shape, lambda r, place: (jnp.maximum(r - 1, 0), 0, 0, 0))
+    part = pl.BlockSpec((1,) + own_in.shape, lambda r, place: (r, 0, 0, 0))
+    square = (model, model)
+    macs = own_rows * model * (6 * shards * hidden_part + 3 * model)
+    return pl.pallas_call(
+        middle_kernel,
+        grid_spec=pltpu.PrefetchScalarGridSpec(
+            num_scalar_prefetch=1,
+            grid=(shards,),
+            in_specs=[whole(source.shape)] * 3 + [
+                whole(square), whole(vectors.shape), whole(in_bias.shape), whole(own_in.shape), whole(own_out.shape),
+                far, far,
+            ],
+            out_specs=[whole(source.shape)] * 3 + [part, part, whole(square), whole((8, model)), whole(in_bias.shape)],
+            scratch_shapes=[
+                pltpu.VMEM((own_rows, model), F32),
+                pltpu.VMEM((own_rows, 1), F32),
+                pltpu.VMEM((own_rows, model), BF16),
+                pltpu.VMEM((model, own_rows), BF16),
+                pltpu.VMEM((own_rows, model), F32),
+                pltpu.VMEM((own_rows, model), F32),
+                pltpu.VMEM((model, hidden_part), BF16),
+                pltpu.VMEM((hidden_part, model), BF16),
+            ],
+        ),
+        out_shape=[
+            jax.ShapeDtypeStruct(source.shape, BF16),
+            jax.ShapeDtypeStruct(source.shape, F32),
+            jax.ShapeDtypeStruct(source.shape, BF16),
+            jax.ShapeDtypeStruct((shards, slices, rows, hidden_part), BF16),
+            jax.ShapeDtypeStruct((shards, slices, rows, hidden_part), BF16),
+            jax.ShapeDtypeStruct(square, BF16),
+            jax.ShapeDtypeStruct((8, model), F32),
+            jax.ShapeDtypeStruct(in_bias.shape, F32),
+        ],
+        compiler_params=pltpu.CompilerParams(vmem_limit_bytes=60 << 20),
+        cost_estimate=pl.CostEstimate(flops=2 * macs, bytes_accessed=30 << 20, transcendentals=own_rows * shards * hidden_part),
+        name="middle",
+    )(place, source, cotangent, mixed, out_weight, vectors, in_bias, own_in, own_out, far_in, far_out)
+
+
+def finish_kernel(place, given_in, given_out, grad_in, grad_out):
+    own = place[0]
+    slices, rows = given_in.shape[0], given_in.shape[1]
+    for j in range(slices):
+        grad_in[j * rows : (j + 1) * rows] = given_in[j ^ own].astype(F32)
+        grad_out[j * rows : (j + 1) * rows] = given_out[j ^ own].astype(F32)
+
+
+def finish(place, given_in, given_out):
+    slices, rows, columns = given_in.shape
+    return pl.pallas_call(
+        finish_kernel,
+        grid_spec=pltpu.PrefetchScalarGridSpec(
+            num_scalar_prefetch=1,
+            grid=(1,),
+            in_specs=[pl.BlockSpec(given_in.shape, lambda k, place: (0, 0, 0))] * 2,
+            out_specs=[pl.BlockSpec((slices * rows, columns), lambda k, place: (0, 0))] * 2,
+        ),
+        out_shape=[jax.ShapeDtypeStruct((slices * rows, columns), F32)] * 2,
+        compiler_params=pltpu.CompilerParams(vmem_limit_bytes=40 << 20),
+        name="finish",
+    )(place, given_in, given_out)
+
+
 def layer_norm(values, gain, shift):
     centred = values - jnp.mean(values, axis=-1, keepdims=True)
     inverse = lax.rsqrt(jnp.mean(centred * centred, axis=-1, keepdims=True) + EPSILON)
@@ -419,21 +572,47 @@
     )
 
 
-def gelu_tanh(values):
-    return jax.nn.gelu(values, approximate=True)
-
-
-def gather_weight(shard, members):
-    rows = shard.shape[0] // members
-    mine = lax.dynamic_slice_in_dim(shard, lax.axis_index("dp") * rows, rows, 0)
-    return lax.all_gather(mine, ("head", "dp"), axis=0, tiled=True)
-
-
-def scatter_grad(grad, members):
-    heads = lax.axis_size("head")
-    rows = grad.shape[0] // (heads * members)
-    part = lax.psum_scatter(grad, ("head", "dp"), scatter_dimension=0, tiled=True)
-    return lax.all_gather(part, "dp", axis=0, tiled=True).astype(F32)
+def exchange(value, axis, bit):
+    size = lax.axis_size(axis)
+    return lax.ppermute(value, axis, [(j, j ^ bit) for j in range(size)])
+
+
+def plane_gather(part, bits):
+    held = {0: part}
+    for bit in bits:
+        order = sorted(held)
+        sent = jnp.stack([held[m] for m in order])
+        received = exchange(sent, "dp", bit)
+        held.update({m ^ bit: received[k] for k, m in enumerate(order)})
+    return jnp.stack([held[m] for m in sorted(held)])
+
+
+def plane_sum(stacked, bits, outer):
+    order = list(range(stacked.shape[0]))
+    for bit in bits:
+        keep = [k for k, m in enumerate(order) if not m & bit]
+        send = [order.index(order[k] | bit) for k in keep]
+        received = exchange(take(stacked, send), "dp", bit)
+        stacked = (take(stacked, keep).astype(F32) + received.astype(F32)).astype(BF16)
+        order = [order[k] for k in keep]
+    own = stacked[0]
+    for bit in outer:
+        own = (own.astype(F32) + exchange(own, "dp", bit).astype(F32)).astype(BF16)
+    return own
+
+
+def take(stacked, indices):
+    return jnp.concatenate([stacked[k : k + 1] for k in indices])
+
+
+def to_order(stacked, own):
+    size = stacked.shape[0]
+    bit = 1
+    while bit < size:
+        shaped = stacked.reshape((size // (2 * bit), 2, bit) + stacked.shape[1:])
+        stacked = jnp.where((own & bit) > 0, shaped[:, ::-1], shaped).reshape(stacked.shape)
+        bit *= 2
+    return stacked
 
 
 def local(
@@ -456,10 +635,29 @@
     normed1, normal1, inverse1 = layer_norm(source, gain_one, ln1_bias.astype(F32))
     first_rows = lax.all_gather(normed1.astype(BF16), "head", axis=0, tiled=True)
 
-    out_full = gather_weight(out_weight, members)
-    in_full = gather_weight(ff_in, members).reshape(heads_axis, model, hidden_part)
-    back_full = gather_weight(ff_out, members)
-    in_bias = lax.all_gather(ff_in_bias, "head", axis=0, tiled=True).astype(F32)
+    slices = min(8, members)
+    inner = [bit for bit in (2, 4, 1) if bit < slices]
+    outer = [1 << k for k in range(3, 16) if 1 << k < members]
+    turned = inner[1::-1] + inner[2:]
+    own = lax.axis_index("dp") % slices
+    place = own.reshape(1).astype(jnp.int32)
+    rows = model // slices
+    narrow = width // slices
+    mine = lambda array, count: lax.dynamic_slice_in_dim(array, own * count, count, 0)
+    small = jnp.concatenate(
+        [mine(out_weight, narrow), jnp.broadcast_to(ff_in_bias[None], (8, hidden_part))[:, :model]], axis=0
+    )
+    small = jnp.stack([small] + [exchange(small, "head", r) for r in range(1, heads_axis)])
+    in_bias = small[:, narrow].astype(F32)
+    out_full = to_order(plane_gather(small[:, :narrow], [1] + inner[:-1]), own)
+    out_full = jnp.swapaxes(out_full, 0, 1)
+    z = lax.axis_index("head")
+    out_full = to_order(out_full, z).reshape(model, model)
+    ff_mine = (mine(ff_in, rows), mine(ff_out, rows))
+    far_in = jnp.stack([exchange(ff_mine[0], "head", r) for r in range(1, heads_axis)])
+    far_out = jnp.stack([exchange(ff_mine[1], "head", r) for r in range(1, heads_axis)])
+    far_in = jnp.swapaxes(plane_gather(far_in, inner), 0, 1)
+    far_out = jnp.swapaxes(plane_gather(far_out, turned), 0, 1)
 
     pad = ((0, 0), (0, 0), (0, LANES - width))
     weight_flat = jnp.pad(qkv_weight, pad).reshape(model, 3 * LANES)
@@ -470,35 +668,32 @@
     mixed_heads, logsum, states = attention_forward(info, qkv, musig, heads)
 
     mixed = lax.all_to_all(mixed_heads, "head", split_axis=0, concat_axis=1, tiled=True)
-    attended = jnp.dot(mixed, out_full, preferred_element_type=F32)
-    residual = source + attended + out_bias.astype(F32)
-    normed2, normal2, inverse2 = layer_norm(residual, gain_two, ln2_bias.astype(F32))
-    second = normed2.astype(BF16)
-    grad_out = cotangent.astype(F32)
-    hidden = jnp.einsum("rd,zdf->rzf", second, in_full, preferred_element_type=F32).reshape(
-        own_rows, -1
-    ) + in_bias
-    activation, gelu_back = jax.vjp(gelu_tanh, hidden)
-    act_low = activation.astype(BF16)
-    outputs = residual + jnp.dot(act_low, back_full, preferred_element_type=F32) + ff_out_bias.astype(F32)
-    grad_act = jnp.dot(cotangent, back_full.T, preferred_element_type=F32)
-    grad_hidden = gelu_back(grad_act)[0].astype(BF16)
-    grad_second = jnp.einsum(
-        "rzf,zdf->rd", grad_hidden.reshape(own_rows, heads_axis, hidden_part), in_full, preferred_element_type=F32
-    )
-    grad_residual = grad_out + norm_back(grad_second, normal2, inverse2, gain_two)
-    grad_attended = grad_residual.astype(BF16)
-    grad_mixed = jnp.dot(grad_attended, out_full.T, preferred_element_type=F32).astype(BF16)
+    vectors = jnp.concatenate(
+        [out_bias[None], ln2_gain[None], ln2_bias[None], ff_out_bias[None], jnp.zeros((4, model), BF16)], axis=0
+    ).astype(F32)
+    outputs, grad_residual, grad_mixed, ff_in_part, ff_out_part, out_weight_part, sums, in_bias_part = middle(
+        place, inputs, cotangent, mixed, out_full, vectors, in_bias,
+        ff_in.reshape(slices, rows, hidden_part), ff_out.reshape(slices, rows, model), far_in, far_out,
+    )
     grad_heads = lax.all_to_all(grad_mixed, "head", split_axis=1, concat_axis=0, tiled=True)
 
-    ff_out_grad = jnp.dot(act_low.T, cotangent, preferred_element_type=F32).astype(BF16)
-    ff_in_grad = jnp.einsum(
-        "rd,rzf->zdf", second, grad_hidden.reshape(own_rows, heads_axis, hidden_part), preferred_element_type=F32
-    ).astype(BF16)
-    out_weight_grad = jnp.dot(mixed.T, grad_attended, preferred_element_type=F32).astype(BF16)
-    ff_out_sum = scatter_grad(ff_out_grad, members)
-    ff_in_sum = scatter_grad(ff_in_grad.reshape(heads_axis * model, hidden_part), members)
-    out_weight_sum = scatter_grad(out_weight_grad, members)
+    reduce_bits = [bit for bit in [1] + inner[:-1] if bit < slices]
+    reduce_turned = [reduce_bits[0]] + reduce_bits[:0:-1]
+
+    def owner_sum(part, bits):
+        summed = plane_sum(jnp.swapaxes(part, 0, 1), bits, outer)
+        terms = [summed[0]] + [exchange(summed[r], "head", r) for r in range(1, heads_axis)]
+        return sum(term.astype(F32) for term in terms).astype(BF16)
+
+    ff_out_slice = owner_sum(ff_out_part, reduce_bits)
+    ff_in_slice = owner_sum(ff_in_part, reduce_turned)
+    out_part = to_order(out_weight_part.reshape(heads_axis, slices, narrow, model), z)
+    out_part = jnp.swapaxes(to_order(jnp.swapaxes(out_part, 0, 1), own), 0, 1)
+    out_slice = owner_sum(out_part, reduce_bits)
+    ff_in_sum, ff_out_sum = finish(
+        place, plane_gather(ff_in_slice, inner), plane_gather(ff_out_slice, turned)
+    )
+    out_weight_sum = to_order(plane_gather(out_slice, inner), own).reshape(width, model).astype(F32)
 
     grad_qkv, probe_grad = attention_backward(
         info, qkv, grad_heads, logsum, states, musig, musig_cols, heads
@@ -514,22 +709,19 @@
     qkv_bias_grad = jnp.sum(grad_qkv.astype(F32), axis=0).reshape(3, LANES)[:, :width]
     grad_source = grad_residual + norm_back(grad_first, normal1, inverse1, gain_one)
     qkv_weight_sum = lax.psum(qkv_weight_grad, "dp").astype(F32)
-    ff_in_bias_part = jnp.sum(grad_hidden.astype(F32), axis=0)
     own_small = lax.psum((qkv_bias_grad, probe_grad), "dp")
     shared = lax.psum(
         jnp.concatenate([
-            jnp.sum(grad_first * normal1, axis=0), jnp.sum(grad_first, axis=0), jnp.sum(grad_residual, axis=0),
-            jnp.sum(grad_second * normal2, axis=0), jnp.sum(grad_second, axis=0), jnp.sum(grad_out, axis=0),
-            ff_in_bias_part,
+            jnp.sum(grad_first * normal1, axis=0)[None], jnp.sum(grad_first, axis=0)[None], sums[:4],
+            to_order(in_bias_part, z),
         ]),
         ("dp", "head"),
     )
-    rows = [shared[i * model : (i + 1) * model] for i in range(6)]
-    ff_in_bias_grad = lax.dynamic_slice_in_dim(shared, 6 * model + lax.axis_index("head") * hidden_part, hidden_part, 0)
+    ff_in_bias_grad = lax.dynamic_index_in_dim(shared, 6 + z, 0, False)
     return (
-        outputs.astype(BF16), grad_source.astype(BF16), rows[0], rows[1], qkv_weight_sum, own_small[0], out_weight_sum,
-        rows[2], own_small[1][:heads], own_small[1][heads : 2 * heads], rows[3], rows[4], ff_in_sum, ff_in_bias_grad,
-        ff_out_sum, rows[5],
+        outputs, grad_source.astype(BF16), shared[0], shared[1], qkv_weight_sum, own_small[0], out_weight_sum,
+        shared[2], own_small[1][:heads], own_small[1][heads : 2 * heads], shared[3], shared[4], ff_in_sum,
+        ff_in_bias_grad, ff_out_sum, shared[5],
     )
 
 

time: 799 us -> 547 us (0.68)
  waiting for transfers between devices: 478 us -> 167 us
  starting transfers between devices: 8.33 us -> 67 us
  matrix products: 69.6 us -> 16.2 us
  Pallas kernels: 69.2 us -> 107 us
  local copies, waits for them, and re-layouts: 21 us -> 57.3 us
  blocking collectives: 104 us -> 70.9 us
  other arithmetic: 25.1 us -> 44.2 us
    reduce_scatter x3 -> x0, waiting for transfers between devices: 178 us -> none  [scatter_grad(): lax.psum_scatter(grad, ('head', 'dp'), scatter_dimension=0, tiled=True)]
    ppermute x0 -> x45, waiting for transfers between devices: none -> 152 us  [exchange(): return lax.ppermute(value, axis, [(j, j ^ bit) for j in range(size)])]
    all_gather x5 -> x0, waiting for transfers between devices: 114 us -> none  [the longest x3 110 us: gather_weight(): return lax.all_gather(mine, ('head', 'dp'), axis=0, tiled=True)]
    all_gather x1, waiting for transfers between devices: 60.7 us -> 0.01 us  [local(): lax.all_gather(normed1.astype(BF16), 'head', axis=0, tiled=True)]
    reduce_scatter x1, waiting for transfers between devices: 59.3 us -> 0.01 us  [local(): lax.psum_scatter(jnp.dot(grad_qkv, weight_flat.T, preferred_element_type=...]
    ppermute x0 -> x45, starting transfers between devices: none -> 59 us  [exchange(): return lax.ppermute(value, axis, [(j, j ^ bit) for j in range(size)])]
    dot_general x9 -> x0, matrix products: 52.3 us -> none  [the longest x1 9.59 us: local(): jnp.dot(act_low, back_full, preferred_element_type=F32)]
    psum x1, waiting for transfers between devices: 47.8 us -> 0.01 us  [local(): qkv_weight_sum = lax.psum(qkv_weight_grad, 'dp').astype(F32)]
  transfers between devices with their start and end apart: 13 -> 50, of which waited for: 10 -> 21; matrix products, arithmetic and copies ran while one was open for 12% -> 17% of each run, Pallas kernels for 9% -> 7%
where the time goes in v2:
time: 547 us; the launch traced here: 545 us
  waiting for transfers between devices  167 us (31%)
  Pallas kernels  107 us (20%)
  blocking collectives  70.9 us (13%)
  starting transfers between devices  67 us (12%)
  local copies, waits for them, and re-layouts  57.3 us (10%)
  other arithmetic  44.2 us (8%)
  matrix products  16.2 us (3%)
  between operations  15.2 us (3%)
    ppermute x45, waiting for transfers between devices, exchange(): return lax.ppermute(value, axis, [(j, j ^ bit) for j in range(size)])  152 us
    ppermute x45, starting transfers between devices, exchange(): return lax.ppermute(value, axis, [(j, j ^ bit) for j in range(size)])  59 us
    psum x1, blocking collectives, local(): lax.psum(jnp.concatenate([jnp.sum(grad_first * normal1, axis=0)[None], jn...  38.6 us
    pallas_call x1, Pallas kernels, attention_backward(): pl.pallas_call(functools.partial(backward_kernel, heads), grid_spec=pltpu...  37 us
    pallas_call x1, Pallas kernels, attention_forward(): pl.pallas_call(functools.partial(forward_kernel, heads), grid_spec=pltpu....  34.4 us
    pallas_call x1, Pallas kernels, middle(): pl.pallas_call(middle_kernel, grid_spec=pltpu.PrefetchScalarGridSpec(num_...  32.7 us
    psum x1, blocking collectives, local(): own_small = lax.psum((qkv_bias_grad, probe_grad), 'dp')  32.4 us
    unnamed x142, local copies, waits for them, and re-layouts  21.9 us
  transfers between devices with their start and end apart: 50, of which 21 were waited for; matrix products, arithmetic and copies ran while one was open for 17% of the time, Pallas kernels for 7%

profile of v2, /device:TPU:0, one launch (start us, length us, event | category | flops | bytes accessed | tf_op | source)
XLA Modules:
  0.0 544.8 jit_solution(17105063382302877908)
XLA Ops:
  8.8 5.1 collective-permute-start.2
  31.0 8.3 %collective-permute-done.7 = bf16[96,768]{1,0:T(8,128)(2,1)S(1)} collective-permute-done((bf16[96,768]{1,0:T(8,128)(2,1)S(1)}, bf16[96,768]{1,0:T(8,128)(2,1)S(1)}, u32[]{:S(2)}, u32[]{:S(2)}) %collective-permute-start.7) | collective-permute-done | bytes 147488 | tf_op jit(solution)/shard_map/ppermute | solution.py:577
  45.3 16.2 %collective-permute-done.13 = bf16[96,768]{1,0:T(8,128)(2,1)S(1)} collective-permute-done((bf16[96,768]{1,0:T(8,128)(2,1)S(1)}, bf16[96,768]{1,0:T(8,128)(2,1)S(1)}, u32[]{:S(2)}, u32[]{:S(2)}) %collective-permute-start.13) | collective-permute-done | bytes 147488 | tf_op jit(solution)/shard_map/ppermute | solution.py:577
  68.3 7.2 %collective-permute-done.15 = bf16[1,3,96,768]{3,2,0,1:T(8,128)(2,1)S(1)} collective-permute-done((bf16[1,3,96,768]{3,2,0,1:T(8,128)(2,1)S(1)}, bf16[1,3,96,768]{3,2,0,1:T(8,128)(2,1)S(1)}, u32[]{:S(2)}, u32[]{:S(2)}) %collective-permute-start.15) | collective-permute-done | bytes 442400 | tf_op jit(solution)/shard_map/ppermute | solution.py:577
  90.1 11.9 %collective-permute-done.10 = bf16[2,3,96,768]{3,2,0,1:T(8,128)(2,1)S(1)} collective-permute-done((bf16[2,3,96,768]{3,2,0,1:T(8,128)(2,1)}, bf16[2,3,96,768]{3,2,0,1:T(8,128)(2,1)S(1)}, u32[]{:S(2)}, u32[]{:S(2)}) %collective-permute-start.10) | collective-permute-done | bytes 884768 | tf_op jit(solution)/shard_map/ppermute | solution.py:577
  114.0 6.2 %add_convert_fusion.qkv = bf16[2048,768]{1,0:T(8,128)(2,1)} fusion(bf16[2048,768]{1,0:T(8,128)(2,1)} %all-gather.2.cloned.1.call-done, bf16[768,768]{0,1:T(8,128)(2,1)S(1)} %bitcast.156, f32[768]{0:T(1024)S(1)} %reshape.166), kind=kOutput, calls=%fused_computation.1 | convolution fusion | flops 2419064832 | bytes 7474176 | tf_op jit(solution)/shard_map/dot_general | solution.py:665
  120.2 34.4 %attention_forward.1 = (bf16[2048,192]{1,0:T(8,128)(2,1)}, f32[8,2048]{1,0:T(8,128)}, f32[8,512,512]{2,1,0:T(8,128)}) custom-call(s32[3,8]{1,0:T(4,128)} %pad_add_fusion.info, bf16[2048,768]{1,0:T(8,128)(2,1)} %add_convert_fusion.qkv, f32[8,512]{1,0:T(8,128)} %copy-done.33, bf16[512,2304]{1,0:T(8,128)(2,1)} %constant.78.clone.table), custom_call_target="tpu_custom_call" | custom-call | tf_op jit(solution)/shard_map/attention_forward/pallas_call | solution.py:327
  166.4 15.1 %all-to-all-done = bf16[4,512,192]{1,2,0:T(8,128)(2,1)S(1)} async-done(((bf16[4,512,192]{1,2,0:T(8,128)(2,1)}), bf16[4,512,192]{1,2,0:T(8,128)(2,1)S(1)}, u32[]{:S(2)}, u32[]{:S(2)}) %all-to-all-start) | async-done | bytes 786464 | tf_op jit(solution)/shard_map/all_to_all | solution.py:670
  182.7 32.7 %middle.1 = (bf16[512,768]{1,0:T(8,128)(2,1)}, f32[512,768]{1,0:T(8,128)}, bf16[512,768]{1,0:T(8,128)(2,1)}, bf16[4,8,96,768]{3,2,1,0:T(8,128)(2,1)}, bf16[4,8,9...) custom-call(s32[1]{0:T(128)} %bitcast.place, bf16[512,768]{1,0:T(8,128)(2,1)} %source.1, ...), custom_call_target="tpu_custom_call" | custom-call | flops 16307453952 | bytes 31457280 | tf_op jit(solution)/shard_map/middle/pallas_call | solution.py:498
  217.8 4.2 all-to-all-start.1
  226.9 4.5 copy_bitcast_fusion
  242.5 6.0 %collective-permute-done.19 = bf16[2,4,24,768]{3,2,1,0:T(8,128)(2,1)S(1)} collective-permute-done((bf16[2,4,24,768]{3,2,1,0:T(8,128)(2,1)S(1)}, bf16[2,4,24,768]{3,2,1,0:T(8,128)(2,1)S(1)}, u32[]{:S(2)}, u32[]{:S(2)}) %collective-permute-start.19) | collective-permute-done | bytes 294944 | tf_op jit(solution)/shard_map/ppermute | solution.py:577
  273.6 37.0 %attention_backward.1 = (bf16[2048,768]{1,0:T(8,128)(2,1)}, f32[8,512]{1,0:T(8,128)}) custom-call(s32[3,8]{1,0:T(4,128)} %pad_add_fusion.info, bf16[2048,768]{1,0:T(8,128)(2,1)} %add_convert_fusion.qkv, bf16[2048,192]{1,0:T(8,128)(2,1)} %bitcast.151, f32[8,2048]{1,0:T(8,128)} %get-tuple-element.35.logsum, f32[8,512,512]{2,1,0:T(8,128)} %get-tuple-element.36.states, ...), custom_call_target="tpu_custom_call" | custom-call | tf_op jit(solution)/shard_map/attention_backward/pallas_call | solution.py:364
  310.6 4.7 convolution_convert_fusion.1
  316.4 5.2 convolution_convert_fusion
  322.9 32.4 %all-reduce.3 = (f32[3,192]{1,0:T(4,128)}, f32[8,512]{1,0:T(8,128)S(1)}) all-reduce(f32[3,192]{1,0:T(4,128)S(1)} %bitcast.181, f32[8,512]{1,0:T(8,128)S(1)} %copy-done.40), channel_id=1, replica_groups=mesh['dp'=8,'head'=4] {'dp'}, use_global_device_ids=true, to_apply=%region_14.15 | all-reduce | flops 4672 | bytes 37376 | tf_op jit(solution)/shard_map/psum | solution.py:712
  365.1 26.3 %collective-permute-done.28 = bf16[2,4,96,768]{3,2,1,0:T(8,128)(2,1)S(1)} collective-permute-done((bf16[2,4,96,768]{3,2,1,0:T(8,128)(2,1)S(1)}, bf16[2,4,96,768]{3,2,1,0:T(8,128)(2,1)S(1)}, u32[]{:S(2)}, u32[]{:S(2)}) %collective-permute-start.28) | collective-permute-done | bytes 1179680 | tf_op jit(solution)/shard_map/ppermute | solution.py:577
  397.1 10.7 %collective-permute-done.29 = bf16[1,4,96,768]{3,2,1,0:T(8,128)(2,1)S(1)} collective-permute-done((bf16[1,4,96,768]{3,2,1,0:T(8,128)(2,1)S(1)}, bf16[1,4,96,768]{3,2,1,0:T(8,128)(2,1)S(1)}, u32[]{:S(2)}, u32[]{:S(2)}) %collective-permute-start.29) | collective-permute-done | bytes 589856 | tf_op jit(solution)/shard_map/ppermute | solution.py:577
  414.2 5.8 %collective-permute-done.32 = bf16[96,768]{1,0:T(8,128)(2,1)S(1)} collective-permute-done((bf16[96,768]{1,0:T(8,128)(2,1)S(1)}, bf16[96,768]{1,0:T(8,128)(2,1)S(1)}, u32[]{:S(2)}, u32[]{:S(2)}) %collective-permute-start.32) | collective-permute-done | bytes 147488 | tf_op jit(solution)/shard_map/ppermute | solution.py:577
  420.0 10.1 %collective-permute-start.39 = (bf16[96,768]{1,0:T(8,128)(2,1)S(1)}, bf16[96,768]{1,0:T(8,128)(2,1)S(1)}, u32[]{:S(2)}, u32[]{:S(2)}) collective-permute-start(bf16[96,768]{1,0:T(8,128)(2,1)S(1)} %get-tuple-element.100), channel_id=1, source_target_pairs={{0,1},{1,0},{2,3},{3,2},{4,5},{5,4},{6,7},{7,6},{8,9},{9,8},{10,11... | collective-permute-start | bytes 442376 | tf_op jit(solution)/shard_map/ppermute | solution.py:577
  430.1 16.3 %collective-permute-done.31 = bf16[96,768]{1,0:T(8,128)(2,1)S(1)} collective-permute-done((bf16[96,768]{1,0:T(8,128)(2,1)S(1)}, bf16[96,768]{1,0:T(8,128)(2,1)S(1)}, u32[]{:S(2)}, u32[]{:S(2)}) %collective-permute-start.31) | collective-permute-done | bytes 147488 | tf_op jit(solution)/shard_map/ppermute | solution.py:577
  446.6 19.0 %collective-permute-done.40 = bf16[96,768]{1,0:T(8,128)(2,1)S(1)} collective-permute-done((bf16[96,768]{1,0:T(8,128)(2,1)S(1)}, bf16[96,768]{1,0:T(8,128)(2,1)S(1)}, u32[]{:S(2)}, u32[]{:S(2)}) %collective-permute-start.40) | collective-permute-done | bytes 147488 | tf_op jit(solution)/shard_map/ppermute | solution.py:577
  467.9 4.6 collective-permute-done.42
  495.9 38.6 %psum.28 = f32[10,768]{1,0:T(8,128)S(1)} all-reduce(f32[10,768]{1,0:T(8,128)S(1)} %pad_maximum_fusion.20), channel_id=1, replica_groups=mesh['dp'=8,'head'=4] {'dp','head'}, use_global_device_ids=true, to_apply=%region_11.12 | all-reduce | flops 7680 | bytes 61440 | tf_op jit(solution)/shard_map/psum | solution.py:713
  (365 shorter events, 167.1 us)
Async XLA Ops:
  7.2 106.8 %all-gather.2.cloned.1.call-start = ((), (), s32[]{:S(2)}) async-start(), calls=%async_computation.3 | async-start | bytes 3932160 | tf_op jit(solution)/shard_map/all_gather | solution.py:636
  19.3 20.0 %collective-permute-start.7 = (bf16[96,768]{1,0:T(8,128)(2,1)S(1)}, bf16[96,768]{1,0:T(8,128)(2,1)S(1)}, u32[]{:S(2)}, u32[]{:S(2)}) collective-permute-start(bf16[96,768]{1,0:T(8,128)(2,1)S(1)} %constant_dynamic-slice_fusion.1), channel_id=1, source_target_pairs={{0,2},{1,3},{2,0},{3,1},{4,6},{5,7},{6,4},{7,5},{8,10},{9,11},{10,... | collective-permute-start | bytes 442376 | tf_op jit(solution)/shard_map/ppermute | solution.py:577
  25.7 19.6 %collective-permute-start.14 = (bf16[96,768]{1,0:T(8,128)(2,1)S(1)}, bf16[96,768]{1,0:T(8,128)(2,1)S(1)}, u32[]{:S(2)}, u32[]{:S(2)}) collective-permute-start(bf16[96,768]{1,0:T(8,128)(2,1)S(1)} %constant_dynamic-slice_fusion), channel_id=1, source_target_pairs={{0,3},{1,2},{2,1},{3,0},{4,7},{5,6},{6,5},{7,4},{8,11},{9,10},{10,... | collective-permute-start | bytes 442376 | tf_op jit(solution)/shard_map/ppermute | solution.py:577
  30.6 30.9 %collective-permute-start.13 = (bf16[96,768]{1,0:T(8,128)(2,1)S(1)}, bf16[96,768]{1,0:T(8,128)(2,1)S(1)}, u32[]{:S(2)}, u32[]{:S(2)}) collective-permute-start(bf16[96,768]{1,0:T(8,128)(2,1)S(1)} %constant_dynamic-slice_fusion), channel_id=1, source_target_pairs={{0,2},{1,3},{2,0},{3,1},{4,6},{5,7},{6,4},{7,5},{8,10},{9,11},{10,... | collective-permute-start | bytes 442376 | tf_op jit(solution)/shard_map/ppermute | solution.py:577
  39.3 22.2 %collective-permute-start.12 = (bf16[96,768]{1,0:T(8,128)(2,1)S(1)}, bf16[96,768]{1,0:T(8,128)(2,1)S(1)}, u32[]{:S(2)}, u32[]{:S(2)}) collective-permute-start(bf16[96,768]{1,0:T(8,128)(2,1)S(1)} %constant_dynamic-slice_fusion), channel_id=1, source_target_pairs={{0,1},{1,0},{2,3},{3,2},{4,5},{5,4},{6,7},{7,6},{8,9},{9,8},{10,11... | collective-permute-start | bytes 442376 | tf_op jit(solution)/shard_map/ppermute | solution.py:577
  42.9 22.8 %collective-permute-start.9 = (bf16[1,3,96,768]{3,2,0,1:T(8,128)(2,1)S(1)}, bf16[1,3,96,768]{3,2,0,1:T(8,128)(2,1)S(1)}, u32[]{:S(2)}, u32[]{:S(2)}) collective-permute-start(bf16[1,3,96,768]{3,2,0,1:T(8,128)(2,1)S(1)} %maximum_bitcast_fusion), channel_id=1, source_target_pairs={{0,8},{4,12},{8,0},{12,4},{16,24},{20,28},{24,16},{28,20},{1,9},{5... | collective-permute-start | bytes 1327112 | tf_op jit(solution)/shard_map/ppermute | solution.py:577
  65.2 23.0 %collective-permute-start.5 = (bf16[4,4,24,768]{3,1,2,0:T(4,128)(2,1)}, bf16[4,4,24,768]{3,1,2,0:T(4,128)(2,1)}, u32[]{:S(2)}, u32[]{:S(2)}) collective-permute-start(bf16[4,4,24,768]{3,1,2,0:T(4,128)(2,1)} %pad_maximum_fusion.8), channel_id=1, source_target_pairs={{0,16},{4,20},{8,24},{12,28},{16,0},{20,4},{24,8},{28,12},{1,17},{... | collective-permute-start | bytes 1769480 | tf_op jit(solution)/shard_map/ppermute | solution.py:577
  66.7 35.3 %collective-permute-start.10 = (bf16[2,3,96,768]{3,2,0,1:T(8,128)(2,1)}, bf16[2,3,96,768]{3,2,0,1:T(8,128)(2,1)S(1)}, u32[]{:S(2)}, u32[]{:S(2)}) collective-permute-start(bf16[2,3,96,768]{3,2,0,1:T(8,128)(2,1)} %pad_maximum_fusion.6), channel_id=1, source_target_pairs={{0,16},{4,20},{8,24},{12,28},{16,0},{20,4},{24,8},{28,12},{1,17},{... | collective-permute-start | bytes 2654216 | tf_op jit(solution)/shard_map/ppermute | solution.py:577
  76.4 25.8 %collective-permute-start.16 = (bf16[2,3,96,768]{3,2,0,1:T(8,128)(2,1)}, bf16[2,3,96,768]{3,2,0,1:T(8,128)(2,1)}, u32[]{:S(2)}, u32[]{:S(2)}) collective-permute-start(bf16[2,3,96,768]{3,2,0,1:T(8,128)(2,1)} %pad_maximum_fusion.7), channel_id=1, source_target_pairs={{0,8},{4,12},{8,0},{12,4},{16,24},{20,28},{24,16},{28,20},{1,9},{5... | collective-permute-start | bytes 2654216 | tf_op jit(solution)/shard_map/ppermute | solution.py:577
  156.9 24.7 %all-to-all-start = ((bf16[4,512,192]{1,2,0:T(8,128)(2,1)}), bf16[4,512,192]{1,2,0:T(8,128)(2,1)S(1)}, u32[]{:S(2)}, u32[]{:S(2)}) async-start(bf16[4,512,192]{1,2,0:T(8,128)(2,1)} %copy.154), calls=%async_computation | async-start | bytes 1572864 | tf_op jit(solution)/shard_map/all_to_all | solution.py:670
  217.8 53.6 %all-to-all-start.1 = ((bf16[512,4,192]{0,2,1:T(8,128)(2,1)}), bf16[512,4,192]{0,2,1:T(8,128)(2,1)}, u32[]{:S(2)}, u32[]{:S(2)}) async-start(bf16[512,4,192]{0,2,1:T(8,128)(2,1)} %bitcast.38), calls=%async_computation.1 | async-start | bytes 1572864 | tf_op jit(solution)/shard_map/all_to_all | solution.py:678
  222.0 259.1 %all-reduce.6.cloned.1.call-start = ((), (), s32[]{:S(2)}) async-start(), calls=%async_computation.5 | async-start | bytes 1769472 | tf_op jit(solution)/shard_map/psum | solution.py:711
  237.3 120.3 %collective-permute-start.27 = (bf16[4,4,96,768]{3,2,1,0:T(8,128)(2,1)}, bf16[4,4,96,768]{3,2,1,0:T(8,128)(2,1)}, u32[]{:S(2)}, u32[]{:S(2)}) collective-permute-start(bf16[4,4,96,768]{3,2,1,0:T(8,128)(2,1)} %pad_maximum_fusion), channel_id=1, source_target_pairs={{0,4},{4,0},{8,12},{12,8},{16,20},{20,16},{24,28},{28,24},{1,5},{5... | collective-permute-start | bytes 7077896 | tf_op jit(solution)/shard_map/ppermute | solution.py:577
  267.8 92.0 %collective-permute-start.36 = (bf16[4,4,96,768]{3,2,1,0:T(8,128)(2,1)}, bf16[4,4,96,768]{3,2,1,0:T(8,128)(2,1)}, u32[]{:S(2)}, u32[]{:S(2)}) collective-permute-start(bf16[4,4,96,768]{3,2,1,0:T(8,128)(2,1)} %pad_maximum_fusion.1), channel_id=1, source_target_pairs={{0,4},{4,0},{8,12},{12,8},{16,20},{20,16},{24,28},{28,24},{1,5},{5... | collective-permute-start | bytes 7077896 | tf_op jit(solution)/shard_map/ppermute | solution.py:577
  269.6 85.6 %collective-permute-start.25 = (bf16[2,24,768]{2,1,0:T(8,128)(2,1)}, bf16[2,24,768]{2,1,0:T(8,128)(2,1)}, u32[]{:S(2)}, u32[]{:S(2)}) collective-permute-start(bf16[2,24,768]{2,1,0:T(8,128)(2,1)} %pad_maximum_fusion.18), channel_id=1, source_target_pairs={{0,16},{4,20},{8,24},{12,28},{16,0},{20,4},{24,8},{28,12},{1,17},{... | collective-permute-start | bytes 221192 | tf_op jit(solution)/shard_map/ppermute | solution.py:577
  316.3 177.5 %reduce-scatter.2.cloned.1.call-start = ((), (), s32[]{:S(2)}) async-start(), calls=%async_computation.4 | async-start | bytes 3932160 | tf_op jit(solution)/shard_map/reduce_scatter | solution.py:701
  359.8 31.7 %collective-permute-start.28 = (bf16[2,4,96,768]{3,2,1,0:T(8,128)(2,1)S(1)}, bf16[2,4,96,768]{3,2,1,0:T(8,128)(2,1)S(1)}, u32[]{:S(2)}, u32[]{:S(2)}) collective-permute-start(bf16[2,4,96,768]{3,2,1,0:T(8,128)(2,1)S(1)} %concatenate.65), channel_id=1, source_target_pairs={{0,16},{4,20},{8,24},{12,28},{16,0},{20,4},{24,8},{28,12},{1,17},{... | collective-permute-start | bytes 3538952 | tf_op jit(solution)/shard_map/ppermute | solution.py:577
  363.5 32.5 %collective-permute-start.37 = (bf16[2,4,96,768]{3,2,1,0:T(8,128)(2,1)S(1)}, bf16[2,4,96,768]{3,2,1,0:T(8,128)(2,1)S(1)}, u32[]{:S(2)}, u32[]{:S(2)}) collective-permute-start(bf16[2,4,96,768]{3,2,1,0:T(8,128)(2,1)S(1)} %pad_maximum_fusion.5), channel_id=1, source_target_pairs={{0,8},{4,12},{8,0},{12,4},{16,24},{20,28},{24,16},{28,20},{1,9},{5... | collective-permute-start | bytes 3538952 | tf_op jit(solution)/shard_map/ppermute | solution.py:577
  409.4 37.0 %collective-permute-start.31 = (bf16[96,768]{1,0:T(8,128)(2,1)S(1)}, bf16[96,768]{1,0:T(8,128)(2,1)S(1)}, u32[]{:S(2)}, u32[]{:S(2)}) collective-permute-start(bf16[96,768]{1,0:T(8,128)(2,1)S(1)} %get-tuple-element.105), channel_id=1, source_target_pairs={{0,2},{1,3},{2,0},{3,1},{4,6},{5,7},{6,4},{7,5},{8,10},{9,11},{10,... | collective-permute-start | bytes 442376 | tf_op jit(solution)/shard_map/ppermute | solution.py:577
  410.1 36.3 %collective-permute-start.30 = (bf16[96,768]{1,0:T(8,128)(2,1)S(1)}, bf16[96,768]{1,0:T(8,128)(2,1)S(1)}, u32[]{:S(2)}, u32[]{:S(2)}) collective-permute-start(bf16[96,768]{1,0:T(8,128)(2,1)S(1)} %get-tuple-element.103), channel_id=1, source_target_pairs={{0,1},{1,0},{2,3},{3,2},{4,5},{5,4},{6,7},{7,6},{8,9},{9,8},{10,11... | collective-permute-start | bytes 442376 | tf_op jit(solution)/shard_map/ppermute | solution.py:577
  412.6 33.9 %collective-permute-start.41 = (bf16[96,768]{1,0:T(8,128)(2,1)S(1)}, bf16[96,768]{1,0:T(8,128)(2,1)S(1)}, u32[]{:S(2)}, u32[]{:S(2)}) collective-permute-start(bf16[96,768]{1,0:T(8,128)(2,1)S(1)} %get-tuple-element.101), channel_id=1, source_target_pairs={{0,3},{1,2},{2,1},{3,0},{4,7},{5,6},{6,5},{7,4},{8,11},{9,10},{10,... | collective-permute-start | bytes 442376 | tf_op jit(solution)/shard_map/ppermute | solution.py:577
  414.1 51.5 %collective-permute-start.40 = (bf16[96,768]{1,0:T(8,128)(2,1)S(1)}, bf16[96,768]{1,0:T(8,128)(2,1)S(1)}, u32[]{:S(2)}, u32[]{:S(2)}) collective-permute-start(bf16[96,768]{1,0:T(8,128)(2,1)S(1)} %get-tuple-element.102), channel_id=1, source_target_pairs={{0,2},{1,3},{2,0},{3,1},{4,6},{5,7},{6,4},{7,5},{8,10},{9,11},{10,... | collective-permute-start | bytes 442376 | tf_op jit(solution)/shard_map/ppermute | solution.py:577
  420.0 45.5 %collective-permute-start.39 = (bf16[96,768]{1,0:T(8,128)(2,1)S(1)}, bf16[96,768]{1,0:T(8,128)(2,1)S(1)}, u32[]{:S(2)}, u32[]{:S(2)}) collective-permute-start(bf16[96,768]{1,0:T(8,128)(2,1)S(1)} %get-tuple-element.100), channel_id=1, source_target_pairs={{0,1},{1,0},{2,3},{3,2},{4,5},{5,4},{6,7},{7,6},{8,9},{9,8},{10,11... | collective-permute-start | bytes 442376 | tf_op jit(solution)/shard_map/ppermute | solution.py:577
  446.5 20.1 %collective-permute-start.33 = (bf16[1,96,768]{2,1,0:T(8,128)(2,1)S(1)}, bf16[1,96,768]{2,1,0:T(8,128)(2,1)S(1)}, u32[]{:S(2)}, u32[]{:S(2)}) collective-permute-start(bf16[1,96,768]{2,1,0:T(8,128)(2,1)S(1)} %get-tuple-element.65), channel_id=1, source_target_pairs={{0,8},{4,12},{8,0},{12,4},{16,24},{20,28},{24,16},{28,20},{1,9},{5... | collective-permute-start | bytes 442376 | tf_op jit(solution)/shard_map/ppermute | solution.py:577
  (82 other events, 841.8 us)
Sparse Core Ops, SparseCore 0:
  23.8 71.5 all-gather.1
  316.4 65.8 all-reduce.5
  384.6 78.3 reduce-scatter.1

commit v3 on v2

v3 whole, which is shorter than its diff:
```python
import functools
import math

import jax
import jax.numpy as jnp
import ml_dtypes
import numpy as np
from jax import lax
from jax.experimental import pallas as pl
from jax.experimental.pallas import tpu as pltpu
from jax.sharding import PartitionSpec as P

HEAD_DIM = 64
BASIS = 512
UNIT = 256
LANES = 256
TAU = 0.75
RIDGE = 0.5
EPSILON = 1e-05
SPREAD = 1.0 / 64.0
WIDTH = 1.0 / BASIS
LIVE = BASIS // 2
HIGHEST = lax.Precision.HIGHEST
F32 = jnp.float32
BF16 = jnp.bfloat16


def split_table(table):
    high = table.astype(np.float32).astype(ml_dtypes.bfloat16)
    low = (table.astype(np.float32) - high.astype(np.float32)).astype(ml_dtypes.bfloat16)
    return high, low


@functools.lru_cache(maxsize=None)
def basis_tables():
    centres = np.arange(BASIS) / (BASIS - 1)
    apart = centres[:, None] - centres[None, :]
    gram = np.exp(-apart * apart / (4.0 * WIDTH * WIDTH)) + RIDGE * np.eye(BASIS)
    solve = np.linalg.inv(gram)
    samples = (np.arange(BASIS) + 0.5) / BASIS
    near_gap = TAU * samples[:, None] - centres[None, :]
    far_gap = samples[:, None] - centres[None, :]
    near = np.exp(-near_gap * near_gap / (2.0 * WIDTH * WIDTH))
    far = np.exp(-far_gap * far_gap / (2.0 * WIDTH * WIDTH))
    contract = (near.T @ far) * (TAU / (BASIS * WIDTH * math.sqrt(math.pi)))
    joined = np.concatenate([solve @ contract, solve[:, LIVE:]], axis=1)
    high, low = split_table(joined)
    forward = np.concatenate([high, high, low], axis=1)
    backward = np.concatenate([high.T, high.T, low.T], axis=1)
    return forward, backward


def term_scale(units):
    return (1.0 - TAU) / (WIDTH * math.sqrt(math.pi) * UNIT) / units.astype(F32)


def split3(value):
    high = value.astype(BF16)
    low = (value - high.astype(F32)).astype(BF16)
    return jnp.concatenate([high, low, high], axis=0)


def dot(a, b, contract=((1,), (0,)), precision=None):
    return lax.dot_general(a, b, (contract, ((), ())), precision=precision, preferred_element_type=F32)


def head_rows(heads, width):
    row = lax.broadcasted_iota(jnp.int32, (8, width), 0)
    lane = lax.broadcasted_iota(jnp.int32, (8, width), 1) // HEAD_DIM
    return ((row == lane) | (row == lane + heads)) & (lane < heads)


def read_parts(logits, heads):
    location = 1.0 / (1.0 + jnp.exp(-logits))
    variance = (jnp.maximum(logits, 0.0) + jnp.log1p(jnp.exp(-jnp.abs(logits)))) * SPREAD + WIDTH * WIDTH
    return location[:heads], variance[heads : 2 * heads]


def place_of(index, length):
    return TAU + (1.0 - TAU) * (index.astype(F32) + 0.5) / (length.astype(F32) * UNIT)


def split_rows(value):
    high = value.astype(BF16)
    rest = value - high.astype(F32)
    mid = rest.astype(BF16)
    return high, mid, (rest - mid.astype(F32)).astype(BF16)


def three_pass(left, right_high, right_low, contract=((1,), (0,))):
    high = left.astype(BF16)
    low = (left - high.astype(F32)).astype(BF16)
    return dot(high, right_high, contract) + dot(low, right_high, contract) + dot(high, right_low, contract)


def advance_values(table, value):
    joined = BASIS + LIVE if table.shape[0] == BASIS else BASIS
    high, low = table[:BASIS, :BASIS], table[:BASIS, 2 * joined : 2 * joined + BASIS]
    value_high = value.astype(BF16)
    value_low = (value - value_high.astype(F32)).astype(BF16)
    return dot(high, value_high) + dot(high, value_low) + dot(low, value_high)


def state_kernel(heads, info, qkv, musig, table, states, value_end, key_end, rows, proj, memory, sums):
    b = pl.program_id(0)
    width = heads * HEAD_DIM
    start, length = info[0, b], info[1, b]

    @pl.when(b == 0)
    def _():
        memory[...] = jnp.zeros_like(memory)
        row = musig[...]
        rows[0:8] = row
        wide = 2 * (BASIS + LIVE)
        for k in range(1, 4):
            row = three_pass(row, table[:, :BASIS], table[:, wide : wide + BASIS])
            rows[8 * k : 8 * k + 8] = row

    @pl.when(start == b)
    def _():
        states[0] = memory[...]
        sums[...] = jnp.zeros_like(sums)

    token = lax.broadcasted_iota(jnp.int32, (LIVE, UNIT), 1) + (b - start) * UNIT
    centre = (lax.broadcasted_iota(jnp.int32, (LIVE, UNIT), 0) + LIVE).astype(F32) / (BASIS - 1)
    gap = place_of(token, length) - centre
    psi = jnp.exp(gap * gap * (-0.5 / (WIDTH * WIDTH)))
    psi_high = psi.astype(BF16)
    psi_low = (psi - psi_high.astype(F32)).astype(BF16)
    pairs = qkv[0, :, LANES : 3 * LANES]
    sums[...] += dot(psi_high, pairs) + dot(psi_low, pairs)

    @pl.when(b + 1 == start + length)
    def _():
        stacked = jnp.concatenate([memory[...], sums[...] * term_scale(length)], axis=0)
        memory[...] = dot(table[...], split3(stacked))

    @pl.when(b == pl.num_programs(0) - 1)
    def _():
        key = memory[:, :LANES]
        key_end[...] = key
        value_end[...] = memory[:, LANES : LANES + width].astype(BF16)
        seen = dot(rows[...], key, precision=HIGHEST)
        mask = head_rows(heads, LANES)
        for k in range(4):
            proj[8 * k : 8 * k + 8] = jnp.where(mask, seen[8 * k : 8 * k + 8], 0.0)


def attend_kernel(heads, info, qkv, result, logsum, cols):
    b = pl.program_id(0)
    start = info[0, b]
    flip = info[3, 0] * (pl.num_programs(0) // 2)
    cols[b] = qkv[b ^ flip, :, 2 * LANES : 3 * LANES].astype(F32).T.astype(BF16)
    query = qkv[b ^ flip, :, 0:LANES]
    lane_head = lax.broadcasted_iota(jnp.int32, (UNIT, LANES), 1) // HEAD_DIM

    def attend(blocks):
        causal = lax.broadcasted_iota(jnp.int32, (UNIT, UNIT), 0) <= lax.broadcasted_iota(
            jnp.int32, (UNIT, UNIT), 1
        )
        for h in range(heads):
            own = jnp.where(lane_head == h, query.astype(F32) * (1.0 / math.sqrt(HEAD_DIM)), 0.0).astype(BF16)
            scores = [
                dot(qkv[(start + j) ^ flip, :, LANES : 2 * LANES], own, ((1,), (1,))) for j in range(blocks)
            ]
            scores[-1] = jnp.where(causal, scores[-1], -1e30)
            highest = functools.reduce(jnp.maximum, [jnp.max(s, axis=0, keepdims=True) for s in scores])
            weights = [jnp.exp(s - highest) for s in scores]
            total = sum(jnp.sum(w, axis=0, keepdims=True) for w in weights)
            rows = slice(h * HEAD_DIM, (h + 1) * HEAD_DIM)
            part = sum(dot(cols[start + j, rows], weights[j].astype(BF16)) for j in range(blocks))
            result[0, rows] = part * (1.0 / total)
            logsum[0, h : h + 1] = highest + jnp.log(total)

    for blocks in range(1, 5):
        pl.when(b - start + 1 == blocks)(functools.partial(attend, blocks))


def read_kernel(
    heads, info, qkv, discrete, states, musig, table, value_in, proj, mixed, values, probes, carried, value_cols,
):
    b = pl.program_id(0)
    width = heads * HEAD_DIM
    start, order, run = info[0, b], info[2, b], info[3, 1]

    @pl.when(b == 0)
    def _():
        carried[...] = jnp.zeros_like(carried)
        carried[:, :width] = value_in[...].astype(F32)

    @pl.when((start == b) & (b > 0) & (run > 0))
    def _():
        carried[...] = advance_values(table, carried[...])

    seen = (start > 0) | (run > 0)

    @pl.when(start == b)
    def _():
        rows = dot(musig[...], states[0, :, :LANES], precision=HIGHEST)
        rows = jnp.where(head_rows(heads, LANES), rows, 0.0)
        incoming = proj[pl.ds(pl.multiple_of(order * 8, 8), 8)]
        probes[0] = (rows + incoming) * (1.0 / math.sqrt(HEAD_DIM))
        value = states[0, :, LANES:] + carried[...]
        values[0] = value
        value_cols[...] = value.T.astype(BF16)

    @pl.when(jnp.logical_not(seen))
    def _():
        mixed[0] = discrete[0].T.astype(BF16)

    @pl.when(seen)
    def _():
        query = qkv[0]
        logits = sum(dot(part, query, ((1,), (1,))) for part in split_rows(probes[0]))
        location, variance = read_parts(logits, heads)
        fall = -0.5 / variance
        peak = WIDTH * lax.rsqrt(variance)
        centres = lax.broadcasted_iota(jnp.int32, (BASIS, UNIT), 0).astype(F32) / (BASIS - 1)
        parts = []
        for h in range(heads):
            gap = centres - location[h : h + 1]
            density = jnp.exp(gap * gap * fall[h : h + 1]).astype(BF16)
            rows = slice(h * HEAD_DIM, (h + 1) * HEAD_DIM)
            parts.append(discrete[0, rows] + dot(value_cols[rows], density) * peak[h : h + 1])
        mixed[0] = jnp.concatenate(parts, axis=0).T.astype(BF16)


def read_back_kernel(
    heads, info, qkv, grad_mixed, values, probes, states, table, query_grad, value_back, row_grads, value_grads,
    probe_grad, carried, value_high, value_low, grad_values, probe_cols, row_grad,
):
    step = pl.program_id(0)
    b = pl.num_programs(0) - 1 - step
    width = heads * HEAD_DIM
    start, length, order, run = info[0, b], info[1, b], info[2, b], info[3, 1]
    seen = (start > 0) | (run > 0)

    @pl.when(step == 0)
    def _():
        carried[...] = jnp.zeros_like(carried)
        probe_grad[...] = jnp.zeros_like(probe_grad)
        row_grads[...] = jnp.zeros_like(row_grads)

    @pl.when(b + 1 == start + length)
    def _():
        grad_values[...] = jnp.zeros_like(grad_values)
        row_grad[...] = jnp.zeros_like(row_grad)
        probe_cols[...] = jnp.concatenate([probes[0], jnp.zeros((120, LANES), F32)], axis=0).T
        value = values[0]
        high = value.astype(BF16)
        value_high[...] = high
        value_low[...] = (value - high.astype(F32)).astype(BF16)

    @pl.when(jnp.logical_not(seen))
    def _():
        query_grad[...] = jnp.zeros_like(query_grad)

    @pl.when(seen)
    def _():
        query = qkv[0]
        given = jnp.concatenate([grad_mixed[0], jnp.zeros((UNIT, LANES - width), BF16)], axis=1)
        lane_head = lax.broadcasted_iota(jnp.int32, (UNIT, LANES), 1) // HEAD_DIM
        logits = sum(dot(part, query, ((1,), (1,))) for part in split_rows(probes[0]))
        location, variance = read_parts(logits, heads)
        inverse = 1.0 / variance
        fall = -0.5 * inverse
        peak = WIDTH * lax.rsqrt(variance)
        centres = lax.broadcasted_iota(jnp.int32, (BASIS, UNIT), 0).astype(F32) / (BASIS - 1)
        along, across = [], []
        for h in range(heads):
            own_given = jnp.where(lane_head == h, given.astype(F32), 0.0).astype(BF16)
            gap = centres - location[h : h + 1]
            square = gap * gap
            density = jnp.exp(square * fall[h : h + 1]) * peak[h : h + 1]
            grad_density = dot(value_high[...], own_given, ((1,), (1,))) + dot(
                value_low[...], own_given, ((1,), (1,))
            )
            grad_values[...] += dot(density.astype(BF16), own_given)
            weighed = density * grad_density
            zeroth = jnp.sum(weighed, axis=0, keepdims=True)
            first = jnp.sum(weighed * gap, axis=0, keepdims=True)
            second = jnp.sum(weighed * square, axis=0, keepdims=True)
            along.append(first * inverse[h : h + 1])
            across.append(0.5 * inverse[h : h + 1] * (second * inverse[h : h + 1] - zeroth))
        sigmoid = 1.0 / (1.0 + jnp.exp(-logits))
        grad_location = jnp.concatenate(along, axis=0) * location * (1.0 - location)
        grad_variance = jnp.concatenate(across, axis=0) * SPREAD * sigmoid[heads : 2 * heads]
        grad_logits = jnp.concatenate(
            [grad_location, grad_variance, jnp.zeros((8 - 2 * heads, UNIT), F32)], axis=0
        )
        padded = jnp.concatenate([grad_logits, jnp.zeros((120, UNIT), F32)], axis=0)
        query_grad[0] = dot(probe_cols[...], padded, precision=HIGHEST)[:width]
        row_grad[...] += dot(grad_logits, query.astype(F32), precision=HIGHEST)

    @pl.when((b == start) & seen)
    def _():
        rows = jnp.where(head_rows(heads, LANES), row_grad[...], 0.0) * (1.0 / math.sqrt(HEAD_DIM))
        row_grads[pl.ds(pl.multiple_of(order * 8, 8), 8)] = rows
        probe_grad[...] += dot(rows, states[0], ((1,), (1,)), HIGHEST)

    @pl.when(b == start)
    def _():
        value_grads[0] = grad_values[...]
        total = carried[...] + grad_values[...]
        value_back[...] = total[:, :width].astype(BF16)

        @pl.when(start > 0)
        def _():
            carried[...] = advance_values(table, total)


def attend_back_kernel(
    heads, info, qkv, grad_mixed, logsum, read_query, row_grads, value_grads, musig, rows_in, row_back, value_back,
    key_end, probe_part, table, out, probe_grad, carried, spread, key_grad, value_grad, cols, turned,
):
    step = pl.program_id(0)
    units = pl.num_programs(0)
    b = units - 1 - step
    width = heads * HEAD_DIM
    start, length, order, run = info[0, b], info[1, b], info[2, b], info[3, 1]
    flip = info[3, 0] * (units // 2)

    @pl.when(step == 0)
    def _():
        for i in range(cols.shape[0]):
            cols[i] = qkv[i, :, LANES : 2 * LANES].astype(F32).T.astype(BF16)
        probe_grad[...] = probe_part[...]

    def carry(total, units_before):
        moved = dot(table[...], split3(total))
        carried[...] = moved[:BASIS]
        spread[...] = (moved[BASIS:] * term_scale(units_before)).astype(BF16)

    @pl.when((step == 0) & (run > 0))
    def _():
        carried[...] = jnp.zeros_like(carried)
        spread[...] = jnp.zeros_like(spread)

    @pl.when((step == 0) & (run == 0))
    def _():
        grad_keys = dot(rows_in[...], row_back[...], ((0,), (0,)), HIGHEST)
        pad = jnp.zeros((BASIS, LANES - width), F32)
        carry(jnp.concatenate([grad_keys, value_back[...].astype(F32), pad], axis=1), length)
        seen = dot(row_back[...], key_end[...], ((1,), (1,)), HIGHEST)
        gained = seen[24:32]
        for k in (2, 1, 0):
            gained = three_pass(gained, table[:BASIS, :BASIS], table[:BASIS, 2 * BASIS : 3 * BASIS])
            gained = gained + seen[8 * k : 8 * k + 8]
        probe_grad[...] += gained

    @pl.when(b + 1 == start + length)
    def _():
        key_grad[...] = jnp.zeros_like(key_grad)
        value_grad[...] = jnp.zeros_like(value_grad)

    query = qkv[b ^ flip, :, 0:LANES]
    given = jnp.concatenate([grad_mixed[0], jnp.zeros((UNIT, LANES - width), BF16)], axis=1)
    lane_head = lax.broadcasted_iota(jnp.int32, (UNIT, LANES), 1) // HEAD_DIM

    def attend_back(blocks):
        causal = lax.broadcasted_iota(jnp.int32, (UNIT, UNIT), 0) <= lax.broadcasted_iota(
            jnp.int32, (UNIT, UNIT), 1
        )
        for h in range(heads):
            own = jnp.where(lane_head == h, query.astype(F32) * (1.0 / math.sqrt(HEAD_DIM)), 0.0).astype(BF16)
            own_given = jnp.where(lane_head == h, given.astype(F32), 0.0).astype(BF16)
            probs, products = [], []
            inner = jnp.zeros((1, UNIT), F32)
            for j in range(blocks):
                score = dot(qkv[(start + j) ^ flip, :, LANES : 2 * LANES], own, ((1,), (1,)))
                if j == blocks - 1:
                    score = jnp.where(causal, score, -1e30)
                prob = jnp.exp(score - logsum[0, h : h + 1])
                product = prob * dot(qkv[(start + j) ^ flip, :, 2 * LANES : 3 * LANES], own_given, ((1,), (1,)))
                inner += jnp.sum(product, axis=0, keepdims=True)
                probs.append(prob)
                products.append(product)
            rows = slice(h * HEAD_DIM, (h + 1) * HEAD_DIM)
            result = jnp.zeros((HEAD_DIM, UNIT), F32)
            for j in range(blocks):
                part = slice(j * UNIT, (j + 1) * UNIT)
                grad_score = (products[j] - probs[j] * inner).astype(BF16)
                key_grad[part] += dot(grad_score, own)
                value_grad[part] += dot(probs[j].astype(BF16), own_given)
                result += dot(cols[(start + j) ^ flip, rows], grad_score)
            turned[rows] = result * (1.0 / math.sqrt(HEAD_DIM)) + read_query[0, rows]

    for blocks in range(1, 5):
        pl.when(b - start + 1 == blocks)(functools.partial(attend_back, blocks))

    local = pl.ds(pl.multiple_of((b - start) * UNIT, UNIT), UNIT)

    @pl.when((start + length < units) | (run == 0))
    def _():
        token = lax.broadcasted_iota(jnp.int32, (UNIT, LIVE), 0) + (b - start) * UNIT
        centre = (lax.broadcasted_iota(jnp.int32, (UNIT, LIVE), 1) + LIVE).astype(F32) / (BASIS - 1)
        gap = place_of(token, length) - centre
        psi = jnp.exp(gap * gap * (-0.5 / (WIDTH * WIDTH))).astype(BF16)
        pair_grad = dot(psi, spread[...])
        key_grad[local] += pair_grad[:, :LANES]
        value_grad[local] += pair_grad[:, LANES:]

    query_grad = turned[...].T.astype(BF16)
    out[0, :, :LANES] = jnp.concatenate([query_grad, jnp.zeros((UNIT, LANES - width), BF16)], axis=1)
    out[0, :, LANES : 2 * LANES] = key_grad[local].astype(BF16)
    out[0, :, 2 * LANES :] = value_grad[local].astype(BF16)

    @pl.when((b == start) & (start > 0))
    def _():
        rows = row_grads[pl.ds(pl.multiple_of(order * 8, 8), 8)]
        grad_keys = dot(musig[...], rows, ((0,), (0,)), HIGHEST)
        total = carried[...] + jnp.concatenate([grad_keys, value_grads[0]], axis=1)
        carry(total, info[1, jnp.maximum(start - 1, 0)])


def segment_info(lengths, units, flip, run):
    slot_units = lengths // UNIT
    slots = jnp.arange(lengths.shape[0], dtype=jnp.int32)
    ends = jnp.sum(jnp.where(slots[None, :] <= slots[:, None], slot_units[None, :], 0), axis=1)
    starts = ends - slot_units
    unit = jnp.arange(units, dtype=jnp.int32)[:, None]
    member = (unit >= starts[None, :]) & (unit < ends[None, :])
    start = jnp.sum(jnp.where(member, starts[None, :], 0), axis=1)
    length = jnp.sum(jnp.where(member, slot_units[None, :], 0), axis=1)
    place = jnp.sum(((ends[None, :] <= unit) & (slot_units > 0)[None, :]).astype(jnp.int32), axis=1)
    own = jnp.where(jnp.arange(units) == 0, flip, run)
    return jnp.stack([start, length, place, own]).astype(jnp.int32)


def whole(shape):
    return pl.BlockSpec(shape, lambda i, info: (0,) * len(shape))


def call(kernel, heads, units, in_specs, out_specs, out_shape, scratch, flops, exps, name):
    return pl.pallas_call(
        functools.partial(kernel, heads),
        grid_spec=pltpu.PrefetchScalarGridSpec(
            num_scalar_prefetch=1, grid=(units,), in_specs=in_specs, out_specs=out_specs, scratch_shapes=scratch
        ),
        out_shape=[jax.ShapeDtypeStruct(shape, kind) for shape, kind in out_shape],
        compiler_params=pltpu.CompilerParams(vmem_limit_bytes=56 << 20),
        cost_estimate=pl.CostEstimate(flops=flops, bytes_accessed=8 << 20, transcendentals=exps),
        name=name,
    )


def unit_block(shape, turn, back=False):
    last = shape[0] - 1

    def index(i, info):
        b = last - i if back else i
        b = b ^ (info[3, 0] * ((last + 1) // 2)) if turn else b
        return (b,) + (0,) * (len(shape) - 1)

    return pl.BlockSpec((1,) + shape[1:], index)


def place_block(shape, back=False):
    last = shape[0] - 1
    return pl.BlockSpec(
        (1,) + shape[1:], lambda i, info: (info[2, last - i if back else i],) + (0,) * (len(shape) - 1)
    )


def memory_state(info, qkv, musig, heads):
    units, width = qkv.shape[0], heads * HEAD_DIM
    table = jnp.asarray(basis_tables()[0])
    states = (units, BASIS, 2 * LANES)
    return call(
        state_kernel, heads, units,
        [unit_block(qkv.shape, True), whole(musig.shape), whole(table.shape)],
        [place_block(states), whole((BASIS, width)), whole((BASIS, LANES)), whole((32, BASIS)), whole((32, LANES))],
        [(states, F32), ((BASIS, width), BF16), ((BASIS, LANES), F32), ((32, BASIS), F32), ((32, LANES), F32)],
        [pltpu.VMEM((BASIS, 2 * LANES), F32), pltpu.VMEM((LIVE, 2 * LANES), F32)],
        5 << 30, units * UNIT * LIVE, "memory_state",
    )(info, qkv, musig, table)


def attention(info, qkv, heads):
    units, width = qkv.shape[0], heads * HEAD_DIM
    return call(
        attend_kernel, heads, units,
        [whole(qkv.shape)],
        [unit_block((units, width, UNIT), False), unit_block((units, 8, UNIT), False)],
        [((units, width, UNIT), F32), ((units, 8, UNIT), F32)],
        [pltpu.VMEM((units, LANES, UNIT), BF16)],
        8 << 30, 2 << 20, "attention",
    )(info, qkv)


def memory_read(info, qkv, discrete, states, musig, value_in, proj, heads):
    units, width = qkv.shape[0], heads * HEAD_DIM
    table = jnp.asarray(basis_tables()[0])
    return call(
        read_kernel, heads, units,
        [
            unit_block((units, UNIT, LANES), True), unit_block(discrete.shape, False), place_block(states.shape),
            whole(musig.shape), whole(table.shape), whole(value_in.shape), whole(proj.shape),
        ],
        [unit_block((units, UNIT, width), True), place_block((units, BASIS, LANES)), place_block((units, 8, LANES))],
        [((units, UNIT, width), BF16), ((units, BASIS, LANES), F32), ((units, 8, LANES), F32)],
        [pltpu.VMEM((BASIS, LANES), F32), pltpu.VMEM((LANES, BASIS), BF16)],
        3 << 30, 2 << 20, "memory_read",
    )(info, qkv, discrete, states, musig, table, value_in, proj)


def memory_read_back(info, qkv, grad_mixed, values, probes, states, heads):
    units, width = qkv.shape[0], heads * HEAD_DIM
    table = jnp.asarray(basis_tables()[1])
    return call(
        read_back_kernel, heads, units,
        [
            unit_block((units, UNIT, LANES), True, True), unit_block(grad_mixed.shape, True, True),
            place_block(values.shape, True), place_block(probes.shape, True),
            place_block((units, BASIS, LANES), True), whole(table.shape),
        ],
        [
            unit_block((units, width, UNIT), False, True), whole((BASIS, width)), whole((32, LANES)),
            place_block((units, BASIS, LANES), True), whole((8, BASIS)),
        ],
        [
            ((units, width, UNIT), F32), ((BASIS, width), BF16), ((32, LANES), F32), ((units, BASIS, LANES), F32),
            ((8, BASIS), F32),
        ],
        [
            pltpu.VMEM((BASIS, LANES), F32), pltpu.VMEM((BASIS, LANES), BF16), pltpu.VMEM((BASIS, LANES), BF16),
            pltpu.VMEM((BASIS, LANES), F32), pltpu.VMEM((LANES, 128), F32), pltpu.VMEM((8, LANES), F32),
        ],
        6 << 30, 2 << 20, "memory_read_back",
    )(info, qkv, grad_mixed, values, probes, states, table)


def attention_back(
    info, qkv, grad_mixed, logsum, read_query, row_grads, value_grads, musig, rows, row_back, value_back, key_end,
    probe_part, heads,
):
    units, width = qkv.shape[0], heads * HEAD_DIM
    table = jnp.asarray(basis_tables()[1])
    return call(
        attend_back_kernel, heads, units,
        [
            whole(qkv.shape), unit_block(grad_mixed.shape, True, True), unit_block(logsum.shape, False, True),
            unit_block(read_query.shape, False, True), whole(row_grads.shape), place_block(value_grads.shape, True),
            whole(musig.shape), whole(rows.shape), whole(row_back.shape), whole(value_back.shape), whole(key_end.shape),
            whole(probe_part.shape), whole(table.shape),
        ],
        [unit_block(qkv.shape, True, True), whole((8, BASIS))],
        [(qkv.shape, BF16), ((8, BASIS), F32)],
        [
            pltpu.VMEM((BASIS, 2 * LANES), F32), pltpu.VMEM((LIVE, 2 * LANES), BF16),
            pltpu.VMEM((4 * UNIT, LANES), F32), pltpu.VMEM((4 * UNIT, LANES), F32),
            pltpu.VMEM((units, LANES, UNIT), BF16), pltpu.VMEM((width, UNIT), F32),
        ],
        20 << 30, 2 << 20, "attention_back",
    )(
        info, qkv, grad_mixed, logsum, read_query, row_grads, value_grads, musig, rows, row_back, value_back, key_end,
        probe_part, table,
    )


def middle_kernel(
    place, source, cotangent, mixed_0, mixed_1, mixed_2, mixed_3, out_weight, vectors, in_bias, own_in, own_out, far_in,
    far_out, outputs, grad_residual, grad_mixed_0, grad_mixed_1, grad_mixed_2, grad_mixed_3, grad_in, grad_out,
    grad_out_weight, sums, grad_in_bias,
    residual, inverse, second, second_cols, total, grad_second, in_now, out_now,
):
    r = pl.program_id(0)
    own = place[0]
    slices, rows = own_in.shape[0], own_in.shape[1]
    model = source.shape[1]
    hidden_part = own_in.shape[2]
    out_bias, gain, shift, last_bias = (vectors[k : k + 1] for k in range(4))

    @pl.when(r == 0)
    def _():
        value = source[...].astype(F32) + out_bias
        for k, mixed in enumerate((mixed_0, mixed_1, mixed_2, mixed_3)):
            value += dot(mixed[...], out_weight[k])
        residual[...] = value
        centred = value - jnp.mean(value, axis=-1, keepdims=True)
        factor = lax.rsqrt(jnp.mean(centred * centred, axis=-1, keepdims=True) + EPSILON)
        inverse[...] = factor
        normal = centred * factor
        grad_residual[...] = normal
        rounded = (normal * gain + shift).astype(BF16)
        second[...] = rounded
        second_cols[...] = rounded.astype(F32).T.astype(BF16)
        total[...] = jnp.zeros_like(total)
        grad_second[...] = jnp.zeros_like(grad_second)
        grad_in_bias[...] = jnp.zeros_like(grad_in_bias)
        for j in range(slices):
            in_now[j * rows : (j + 1) * rows] = own_in[j]
            out_now[j * rows : (j + 1) * rows] = own_out[j]

    @pl.when(r > 0)
    def _():
        for j in range(slices):
            in_now[j * rows : (j + 1) * rows] = far_in[0, j ^ own]
            out_now[j * rows : (j + 1) * rows] = far_out[0, j ^ own]

    half = hidden_part // 2
    for t in range(2):
        span = slice(t * half, (t + 1) * half)
        hidden = dot(second[...], in_now[:, span]) + in_bias[pl.ds(r, 1), span]
        cube = hidden * hidden
        root = math.sqrt(2.0 / math.pi)
        bent = jnp.tanh(hidden * (root + (root * 0.044715) * cube))
        lifted = 0.5 + 0.5 * bent
        activation = (hidden * lifted).astype(BF16)
        slope = lifted + hidden * ((0.5 - 0.5 * bent * bent) * (root + (3.0 * root * 0.044715) * cube))
        total[...] += dot(activation, out_now[span])
        given = dot(cotangent[...], out_now[span], ((1,), (1,)))
        grad_hidden = (given * slope).astype(BF16)
        grad_second[...] += dot(grad_hidden, in_now[:, span], ((1,), (1,)))
        grad_in_bias[pl.ds(r, 1), span] = jnp.sum(grad_hidden.astype(F32), axis=0, keepdims=True)
        part = dot(activation, cotangent[...], ((0,), (0,))).astype(BF16)
        per = half // rows
        for k in range(per):
            grad_out[0, (t * per + k) ^ own] = part[k * rows : (k + 1) * rows]
        part = dot(second_cols[...], grad_hidden).astype(BF16)
        for j in range(slices):
            grad_in[0, j ^ own, :, span] = part[j * rows : (j + 1) * rows]

    @pl.when(r == pl.num_programs(0) - 1)
    def _():
        given = cotangent[...].astype(F32)
        outputs[...] = (residual[...] + total[...] + last_bias).astype(BF16)
        normal = grad_residual[...]
        grad = grad_second[...]
        scaled = grad * gain
        value = given + inverse[...] * (
            scaled
            - jnp.mean(scaled, axis=-1, keepdims=True)
            - normal * jnp.mean(scaled * normal, axis=-1, keepdims=True)
        )
        sums[0:1] = jnp.sum(value, axis=0, keepdims=True)
        sums[1:2] = jnp.sum(grad * normal, axis=0, keepdims=True)
        sums[2:3] = jnp.sum(grad, axis=0, keepdims=True)
        sums[3:4] = jnp.sum(given, axis=0, keepdims=True)
        sums[4:8] = jnp.zeros((4, model), F32)
        grad_residual[...] = value
        rounded = value.astype(BF16)
        grads = (grad_mixed_0, grad_mixed_1, grad_mixed_2, grad_mixed_3)
        for k, mixed in enumerate((mixed_0, mixed_1, mixed_2, mixed_3)):
            grads[k][...] = dot(rounded, out_weight[k], ((1,), (1,))).astype(BF16)
            grad_out_weight[k] = dot(mixed[...], rounded, ((0,), (0,))).astype(BF16)


def middle(place, source, cotangent, mixed, out_weight, vectors, in_bias, own_in, own_out, far_in, far_out):
    own_rows, model = source.shape
    shards = far_in.shape[0] + 1
    slices, rows, hidden_part = own_in.shape
    narrow = mixed[0].shape
    far = pl.BlockSpec((1,) + own_in.shape, lambda r, place: (jnp.maximum(r - 1, 0), 0, 0, 0))
    part = pl.BlockSpec((1,) + own_in.shape, lambda r, place: (r, 0, 0, 0))
    macs = own_rows * model * (6 * shards * hidden_part + 3 * model)
    return pl.pallas_call(
        middle_kernel,
        grid_spec=pltpu.PrefetchScalarGridSpec(
            num_scalar_prefetch=1,
            grid=(shards,),
            in_specs=[whole(source.shape)] * 2 + [whole(narrow)] * 4 + [
                whole(out_weight.shape), whole(vectors.shape), whole(in_bias.shape), whole(own_in.shape),
                whole(own_out.shape), far, far,
            ],
            out_specs=[whole(source.shape)] * 2 + [whole(narrow)] * 4 + [
                part, part, whole(out_weight.shape), whole((8, model)), whole(in_bias.shape)
            ],
            scratch_shapes=[
                pltpu.VMEM((own_rows, model), F32),
                pltpu.VMEM((own_rows, 1), F32),
                pltpu.VMEM((own_rows, model), BF16),
                pltpu.VMEM((model, own_rows), BF16),
                pltpu.VMEM((own_rows, model), F32),
                pltpu.VMEM((own_rows, model), F32),
                pltpu.VMEM((model, hidden_part), BF16),
                pltpu.VMEM((hidden_part, model), BF16),
            ],
        ),
        out_shape=[
            jax.ShapeDtypeStruct(source.shape, BF16),
            jax.ShapeDtypeStruct(source.shape, F32),
        ] + [jax.ShapeDtypeStruct(narrow, BF16)] * 4 + [
            jax.ShapeDtypeStruct((shards, slices, rows, hidden_part), BF16),
            jax.ShapeDtypeStruct((shards, slices, rows, hidden_part), BF16),
            jax.ShapeDtypeStruct(out_weight.shape, BF16),
            jax.ShapeDtypeStruct((8, model), F32),
            jax.ShapeDtypeStruct(in_bias.shape, F32),
        ],
        compiler_params=pltpu.CompilerParams(vmem_limit_bytes=60 << 20),
        cost_estimate=pl.CostEstimate(
            flops=2 * macs, bytes_accessed=30 << 20, transcendentals=own_rows * shards * hidden_part
        ),
        name="middle",
    )(place, source, cotangent, *mixed, out_weight, vectors, in_bias, own_in, own_out, far_in, far_out)


def finish_kernel(place, given_in, given_out, grad_in, grad_out):
    own = place[0]
    slices, rows = given_in.shape[0], given_in.shape[1]
    for j in range(slices):
        grad_in[j * rows : (j + 1) * rows] = given_in[j ^ own].astype(F32)
        grad_out[j * rows : (j + 1) * rows] = given_out[j ^ own].astype(F32)


def finish(place, given_in, given_out):
    slices, rows, columns = given_in.shape
    return pl.pallas_call(
        finish_kernel,
        grid_spec=pltpu.PrefetchScalarGridSpec(
            num_scalar_prefetch=1,
            grid=(1,),
            in_specs=[pl.BlockSpec(given_in.shape, lambda k, place: (0, 0, 0))] * 2,
            out_specs=[pl.BlockSpec((slices * rows, columns), lambda k, place: (0, 0))] * 2,
        ),
        out_shape=[jax.ShapeDtypeStruct((slices * rows, columns), F32)] * 2,
        compiler_params=pltpu.CompilerParams(vmem_limit_bytes=40 << 20),
        name="finish",
    )(place, given_in, given_out)


def layer_norm(values, gain, shift):
    centred = values - jnp.mean(values, axis=-1, keepdims=True)
    inverse = lax.rsqrt(jnp.mean(centred * centred, axis=-1, keepdims=True) + EPSILON)
    normal = centred * inverse
    return (normal * gain + shift, normal, inverse)


def norm_back(grad, normal, inverse, gain):
    scaled = grad * gain
    return inverse * (
        scaled
        - jnp.mean(scaled, axis=-1, keepdims=True)
        - normal * jnp.mean(scaled * normal, axis=-1, keepdims=True)
    )


def exchange(value, axis, bit):
    size = lax.axis_size(axis)
    return lax.ppermute(value, axis, [(j, j ^ bit) for j in range(size)])


def plane_gather(part, bits):
    held = {0: part}
    for bit in bits:
        order = sorted(held)
        sent = jnp.stack([held[m] for m in order])
        received = exchange(sent, "dp", bit)
        held.update({m ^ bit: received[k] for k, m in enumerate(order)})
    return jnp.stack([held[m] for m in sorted(held)])


def plane_sum(stacked, bits, outer):
    order = list(range(stacked.shape[0]))
    for bit in bits:
        keep = [k for k, m in enumerate(order) if not m & bit]
        send = [order.index(order[k] | bit) for k in keep]
        received = exchange(take(stacked, send), "dp", bit)
        stacked = (take(stacked, keep).astype(F32) + received.astype(F32)).astype(BF16)
        order = [order[k] for k in keep]
    own = stacked[0]
    for bit in outer:
        own = (own.astype(F32) + exchange(own, "dp", bit).astype(F32)).astype(BF16)
    return own


def take(stacked, indices):
    return jnp.concatenate([stacked[k : k + 1] for k in indices])


def to_order(stacked, own):
    size = stacked.shape[0]
    bit = 1
    while bit < size:
        shaped = stacked.reshape((size // (2 * bit), 2, bit) + stacked.shape[1:])
        stacked = jnp.where((own & bit) > 0, shaped[:, ::-1], shaped).reshape(stacked.shape)
        bit *= 2
    return stacked


def local(
    inputs, seg_lengths, ln1_gain, ln1_bias, qkv_weight, qkv_bias, out_weight, out_bias, mem_mu, mem_sig,
    ln2_gain, ln2_bias, ff_in, ff_in_bias, ff_out, ff_out_bias, cotangent,
):
    own_rows, model = inputs.shape
    shards = lax.axis_size("head")
    members = lax.axis_size("dp")
    width = qkv_weight.shape[2]
    heads = width // HEAD_DIM
    hidden_part = ff_in.shape[1]
    units = 2 * own_rows // UNIT
    slots = seg_lengths.shape[1] // 2
    z = lax.axis_index("head")
    run = z // 2
    next_run = lambda value: lax.ppermute(value, "head", [(0, 2), (1, 3)])
    last_run = lambda value: lax.ppermute(value, "head", [(2, 0), (3, 1)])

    slices = min(8, members)
    forth = [bit for bit in (2, 4, 1) if bit < slices]
    turned = forth[1::-1] + forth[2:]
    plain = [bit for bit in (1, 2, 4) if bit < slices]
    back_turned = plain[:1] + plain[:0:-1]
    outer = [1 << k for k in range(3, 16) if 1 << k < members]
    own = lax.axis_index("dp") % slices
    place = own.reshape(1).astype(jnp.int32)
    rows = model // slices
    narrow = width // slices
    mine = lambda array, count: lax.dynamic_slice_in_dim(array, own * count, count, 0)

    source = inputs.astype(F32)
    gain_one = ln1_gain.astype(F32)
    normed1, normal1, inverse1 = layer_norm(source, gain_one, ln1_bias.astype(F32))
    first_own = normed1.astype(BF16)
    first_rows = jnp.concatenate([first_own, exchange(first_own, "head", 1)], axis=0)

    info = segment_info(lax.dynamic_slice_in_dim(seg_lengths[0], run * slots, slots, 0), units, z % 2, run)

    far_slice = exchange(mine(qkv_weight.reshape(model, 3 * width), rows), "head", 2)
    far_weight = to_order(plane_gather(far_slice, plain), own).reshape(model, 3, width)
    far_small = exchange(
        jnp.concatenate([qkv_bias.reshape(1, 3 * width), mem_mu.reshape(1, -1), mem_sig.reshape(1, -1)], axis=1),
        "head", 2,
    )
    far_bias, far_probe = far_small[:, : 3 * width].reshape(3, width), far_small[0, 3 * width :].reshape(-1, BASIS)

    def project(weight, bias, probe):
        pad = ((0, 0), (0, 0), (0, LANES - width))
        flat = jnp.pad(weight, pad).reshape(model, 3 * LANES)
        shift = jnp.pad(bias, pad[1:]).reshape(3 * LANES).astype(F32)
        value = (jnp.dot(first_rows, flat, preferred_element_type=F32) + shift).astype(BF16)
        musig = jnp.concatenate([probe, jnp.zeros((8 - 2 * heads, BASIS), BF16)], axis=0).astype(F32)
        return flat, value.reshape(units, UNIT, 3 * LANES), musig

    sides = [
        project(qkv_weight, qkv_bias, jnp.concatenate([mem_mu, mem_sig], axis=0)),
        project(far_weight, far_bias, far_probe),
    ]
    states = [memory_state(info, qkv, musig, heads) for _, qkv, musig in sides]
    arrived = [(next_run(state[1]), next_run(state[4])) for state in states[::-1]]
    discrete = [attention(info, qkv, heads) for _, qkv, _ in sides]
    reads = [
        memory_read(info, qkv, discrete[k][0], states[k][0], musig, *arrived[k], heads)
        for k, (_, qkv, musig) in enumerate(sides)
    ]
    mixed = [None] * 4
    for k in range(2):
        shared_rows = reads[k][0].reshape(2, own_rows, width)
        mixed[2 * k] = shared_rows[0]
        mixed[2 * k + 1] = exchange(shared_rows[1], "head", 1)

    small = jnp.concatenate(
        [mine(out_weight, narrow), jnp.broadcast_to(ff_in_bias[None], (8, hidden_part))[:, :model]], axis=0
    )
    ff_mine = (mine(ff_in, rows), mine(ff_out, rows))
    small, ff_mine, first_rows = lax.optimization_barrier((small, ff_mine, first_rows))
    small = jnp.stack([small] + [exchange(small, "head", r) for r in range(1, shards)])
    in_bias = small[:, narrow].astype(F32)
    out_full = to_order(plane_gather(small[:, :narrow], plain), own)
    out_full = jnp.swapaxes(out_full, 0, 1).reshape(shards, width, model)
    far_in = jnp.stack([exchange(ff_mine[0], "head", r) for r in range(1, shards)])
    far_out = jnp.stack([exchange(ff_mine[1], "head", r) for r in range(1, shards)])
    far_in = jnp.swapaxes(plane_gather(far_in, forth), 0, 1)
    far_out = jnp.swapaxes(plane_gather(far_out, turned), 0, 1)

    vectors = jnp.concatenate(
        [out_bias[None], ln2_gain[None], ln2_bias[None], ff_out_bias[None], jnp.zeros((4, model), BF16)], axis=0
    ).astype(F32)
    outputs, grad_residual, *rest = middle(
        place, inputs, cotangent, mixed, out_full, vectors, in_bias,
        ff_in.reshape(slices, rows, hidden_part), ff_out.reshape(slices, rows, model), far_in, far_out,
    )
    grad_mixed, (ff_in_part, ff_out_part, out_weight_part, sums, in_bias_part) = rest[:4], rest[4:]
    given = [
        jnp.stack([grad_mixed[2 * k], exchange(grad_mixed[2 * k + 1], "head", 1)]).reshape(units, UNIT, width)
        for k in range(2)
    ]

    read_backs = [
        memory_read_back(info, qkv, given[k], reads[k][1], reads[k][2], states[k][0], heads)
        for k, (_, qkv, _) in enumerate(sides)
    ]
    returned = [(last_run(back[1]), last_run(back[2])) for back in read_backs[::-1]]
    grads = []
    for k, (_, qkv, musig) in enumerate(sides):
        query_part, _, row_grads, value_grads, probe_part = read_backs[k]
        grads.append(attention_back(
            info, qkv, given[k], discrete[k][1], query_part, row_grads, value_grads, musig, states[k][3],
            returned[k][1], returned[k][0], states[k][2], probe_part, heads,
        ))
    flats = [grad[0].reshape(2 * own_rows, 3 * LANES) for grad in grads]
    grad_rows = sum(
        jnp.dot(flat, sides[k][0].T, preferred_element_type=F32) for k, flat in enumerate(flats)
    ).astype(BF16)
    grad_first = grad_rows[:own_rows].astype(F32) + exchange(grad_rows[own_rows:], "head", 1).astype(F32)
    grad_source = grad_residual + norm_back(grad_first, normal1, inverse1, gain_one)

    def owner_sum(part, bits):
        summed = plane_sum(jnp.swapaxes(part, 0, 1), bits, outer)
        terms = [summed[0]] + [exchange(summed[r], "head", r) for r in range(1, shards)]
        return sum(term.astype(F32) for term in terms).astype(BF16)

    ff_out_slice = owner_sum(ff_out_part, plain)
    ff_in_slice = owner_sum(ff_in_part, back_turned)
    out_part = out_weight_part.reshape(shards, slices, narrow, model)
    out_slice = owner_sum(jnp.swapaxes(to_order(jnp.swapaxes(out_part, 0, 1), own), 0, 1), plain)
    ff_in_sum, ff_out_sum = finish(place, plane_gather(ff_in_slice, forth), plane_gather(ff_out_slice, turned))
    out_weight_sum = to_order(plane_gather(out_slice, forth), own).reshape(width, model).astype(F32)

    def qkv_part(flat):
        part = jnp.dot(first_rows.T, flat, preferred_element_type=F32).reshape(model, 3, LANES)[:, :, :width]
        part = to_order(part.astype(BF16).reshape(slices, rows, 3 * width), own)
        return plane_sum(part, plain, outer)

    qkv_slice = qkv_part(flats[0]).astype(F32) + exchange(qkv_part(flats[1]), "head", 2).astype(F32)
    qkv_weight_sum = to_order(plane_gather(qkv_slice.astype(BF16), forth), own).reshape(model, 3, width).astype(F32)

    def owned(k):
        bias = jnp.sum(flats[k].astype(F32), axis=0).reshape(3, LANES)[:, :width].reshape(-1)
        probe = grads[k][1][: 2 * heads].reshape(-1)
        return jnp.concatenate([bias, probe])

    kept = jnp.concatenate([in_bias_part[0], owned(0)])
    kept = kept + exchange(jnp.concatenate([in_bias_part[2], owned(1)]), "head", 2)
    other = in_bias_part[1] + exchange(in_bias_part[3], "head", 2)
    kept = kept.at[:hidden_part].add(exchange(other, "head", 1))
    kept = lax.psum(kept, "dp")
    shared = jnp.concatenate([
        jnp.sum(grad_first * normal1, axis=0)[None], jnp.sum(grad_first, axis=0)[None], sums[:4]
    ])
    for axis, count in (("dp", members), ("head", shards)):
        bit = 1
        while bit < count:
            shared = shared + exchange(shared, axis, bit)
            bit *= 2
    bias_end = hidden_part + 3 * width
    probe_sum = kept[bias_end:].reshape(2 * heads, BASIS)
    return (
        outputs, grad_source.astype(BF16), shared[0], shared[1], qkv_weight_sum,
        kept[hidden_part:bias_end].reshape(3, width), out_weight_sum, shared[2], probe_sum[:heads], probe_sum[heads:],
        shared[3], shared[4], ff_in_sum, kept[:hidden_part], ff_out_sum, shared[5],
    )


def solution(mesh):
    rows, whole = P(("dp", "head"), None), P()
    return jax.shard_map(
        local,
        mesh=mesh,
        in_specs=(
            rows, P("dp", None), whole, whole, P(None, None, "head"), P(None, "head"), P("head", None), whole,
            P("head", None), P("head", None), whole, whole, P(None, "head"), P("head"), P("head", None), whole, rows,
        ),
        out_specs=(
            rows, rows, whole, whole, P(None, None, "head"), P(None, "head"), P("head", None), whole,
            P("head", None), P("head", None), whole, whole, P(None, "head"), P("head"), P("head", None), whole,
        ),
        check_vma=False,
    )
```

time: 547 us -> 590 us (1.079)
  Pallas kernels: 107 us -> 166 us
  blocking collectives: 70.9 us -> 22.3 us
  local copies, waits for them, and re-layouts: 57.3 us -> 103 us
  waiting for transfers between devices: 167 us -> 123 us
  starting transfers between devices: 67 us -> 90.7 us
  other arithmetic: 44.2 us -> 60.2 us
  between operations: 15.2 us -> 3.1 us
    pallas_call x2 -> x10, Pallas kernels: 71.5 us -> 130 us  [the longest x2 47.4 us: attention_back(): call(attend_back_kernel, heads, units, [whole(qkv.shape), unit_block(grad...]
    psum x2 -> x1, blocking collectives: 70.9 us -> 22.3 us  [local(): kept = lax.psum(kept, 'dp')]
    rev x1 -> x4, local copies, waits for them, and re-layouts: 0.19 us -> 34.3 us  [to_order(): shaped[:, ::-1]]
    ppermute x45 -> x74, waiting for transfers between devices: 152 us -> 123 us  [exchange(): return lax.ppermute(value, axis, [(j, j ^ bit) for j in range(size)])]
    ppermute x45 -> x74, starting transfers between devices: 59 us -> 78.5 us  [exchange(): return lax.ppermute(value, axis, [(j, j ^ bit) for j in range(size)])]
    all_to_all x2 -> x0, waiting for transfers between devices: 15.1 us -> none  [the longest x1 15.1 us: local(): lax.all_to_all(mixed_heads, 'head', split_axis=0, concat_axis=1, tiled=True)]
    ppermute x0 -> x8, starting transfers between devices: none -> 12.3 us  [the longest x4 7.11 us: local(): next_run = lambda value: lax.ppermute(value, 'head', [(0, 2), (1, 3)])]
    all_to_all x2 -> x0, starting transfers between devices: 7.69 us -> none  [the longest x1 4.2 us: local(): lax.all_to_all(grad_mixed, 'head', split_axis=1, concat_axis=0, tiled=True)]
  transfers between devices with their start and end apart: 50 -> 82, of which waited for: 21 -> 32; matrix products, arithmetic and copies ran while one was open for 17% -> 29% of each run, Pallas kernels for 7% -> 22%
where the time goes in v3:
time: 590 us; the launch traced here: 587 us
  Pallas kernels  166 us (28%)
  waiting for transfers between devices  123 us (21%)
  local copies, waits for them, and re-layouts  103 us (17%)
  starting transfers between devices  90.7 us (15%)
  other arithmetic  60.2 us (10%)
  blocking collectives  22.3 us (4%)
  matrix products  18.1 us (3%)
    ppermute x74, waiting for transfers between devices, exchange(): return lax.ppermute(value, axis, [(j, j ^ bit) for j in range(size)])  123 us
    ppermute x74, starting transfers between devices, exchange(): return lax.ppermute(value, axis, [(j, j ^ bit) for j in range(size)])  78.5 us
    pallas_call x2, Pallas kernels, attention_back(): call(attend_back_kernel, heads, units, [whole(qkv.shape), unit_block(grad...  47.4 us
    rev x4, local copies, waits for them, and re-layouts, to_order(): shaped[:, ::-1]  34.3 us
    pallas_call x1, Pallas kernels, middle(): pl.pallas_call(middle_kernel, grid_spec=pltpu.PrefetchScalarGridSpec(num_...  34.2 us
    pallas_call x2, Pallas kernels, memory_read_back(): call(read_back_kernel, heads, units, [unit_block((units, UNIT, LANES), Tr...  27.7 us
    pallas_call x2, Pallas kernels, memory_state(): call(state_kernel, heads, units, [unit_block(qkv.shape, True), whole(musi...  25.3 us
    psum x1, blocking collectives, local(): kept = lax.psum(kept, 'dp')  22.3 us
  transfers between devices with their start and end apart: 82, of which 32 were waited for; matrix products, arithmetic and copies ran while one was open for 29% of the time, Pallas kernels for 22%

profile of v3, /device:TPU:0, one launch (start us, length us, event | category | flops | bytes accessed | tf_op | source)
XLA Modules:
  0.0 586.8 jit_solution(8599842699336780318)
XLA Ops:
  21.9 5.8 collective-permute-done.3
  52.5 12.6 %memory_state.2 = (f32[4,512,512]{2,1,0:T(8,128)}, bf16[512,192]{1,0:T(8,128)(2,1)}, f32[512,256]{1,0:T(8,128)}, f32[32,512]{1,0:T(8,128)}, f32[32,256]{1,0:T(8,128)}) custom-call(s32[4,4]{1,0:T(4,128)} %pad_add_fusion.info, bf16[4,256,768]{2,1,0:T(8,128)(2,1)} %bitcast.302, f32[8,512]{1,0:T(8,128)} %maximum_convert_fusion.musig, ...), custom_call_target="tpu_custom_call" | custom-call | flops 5368709120 | bytes 8388608 | tf_op jit(solution)/shard_map/memory_state/pallas_call | solution.py:469
  73.0 7.4 %rev.63 = bf16[4,2,1,96,576]{3,1,0,4,2:T(2,128)(2,1)S(1)} reverse(bf16[4,2,1,96,576]{3,1,0,4,2:T(2,128)(2,1)S(1)} %copy.150), dimensions={1} | reverse | bytes 1769472 | tf_op jit(solution)/shard_map/rev | solution.py:776
  87.6 5.8 attention.3
  93.3 12.7 %memory_state.3 = (f32[4,512,512]{2,1,0:T(8,128)}, bf16[512,192]{1,0:T(8,128)(2,1)}, f32[512,256]{1,0:T(8,128)}, f32[32,512]{1,0:T(8,128)}, f32[32,256]{1,0:T(8,128)}) custom-call(s32[4,4]{1,0:T(4,128)} %pad_add_fusion.info, bf16[4,256,768]{2,1,0:T(8,128)(2,1)} %bitcast.307, f32[8,512]{1,0:T(8,128)} %pad_convert_fusion.musig, ...), custom_call_target="tpu_custom_call" | custom-call | flops 5368709120 | bytes 8388608 | tf_op jit(solution)/shard_map/memory_state/pallas_call | solution.py:469
  124.3 9.0 %memory_read.3 = (bf16[4,256,192]{2,1,0:T(8,128)(2,1)}, f32[4,512,256]{2,1,0:T(8,128)}, f32[4,8,256]{2,1,0:T(8,128)}) custom-call(s32[4,4]{1,0:T(4,128)} %pad_add_fusion.info, bf16[4,256,768]{2,1,0:T(8,128)(2,1)} %bitcast.308, f32[4,192,256]{2,1,0:T(8,128)} %get-tuple-element.84.discrete, f32[4,512,512]{2,1,0:T(8,128)} %get-tuple-element.85.states, ...), custom_call_target="tpu_custom_call" | custom-call | flops 3221225472 | bytes 8388608 | tf_op jit(solution)/shard_map/memory_read/pallas_call | solution.py:494
  135.0 10.1 %collective-permute-start.11 = (bf16[512,192]{1,0:T(8,128)(2,1)S(1)}, bf16[512,192]{1,0:T(8,128)(2,1)}, u32[]{:S(2)}, u32[]{:S(2)}) collective-permute-start(bf16[512,192]{1,0:T(8,128)(2,1)S(1)} %bitcast.274), channel_id=1, source_target_pairs={{0,1},{1,0},{2,3},{3,2},{4,5},{5,4},{6,7},{7,6},{8,9},{9,8},{10,11... | collective-permute-start | bytes 589832 | tf_op jit(solution)/shard_map/ppermute | solution.py:740
  147.5 8.7 %memory_read.2 = (bf16[4,256,192]{2,1,0:T(8,128)(2,1)}, f32[4,512,256]{2,1,0:T(8,128)}, f32[4,8,256]{2,1,0:T(8,128)}) custom-call(s32[4,4]{1,0:T(4,128)} %pad_add_fusion.info, bf16[4,256,768]{2,1,0:T(8,128)(2,1)} %bitcast.303, f32[4,192,256]{2,1,0:T(8,128)} %get-tuple-element.79.discrete, f32[4,512,512]{2,1,0:T(8,128)} %get-tuple-element.80.states, ...), custom_call_target="tpu_custom_call" | custom-call | flops 3221225472 | bytes 8388608 | tf_op jit(solution)/shard_map/memory_read/pallas_call | solution.py:494
  158.2 7.2 %collective-permute-done.17 = bf16[4,4,24,768]{3,1,2,0:T(4,128)(2,1)} collective-permute-done((bf16[4,4,24,768]{3,1,2,0:T(4,128)(2,1)}, bf16[4,4,24,768]{3,1,2,0:T(4,128)(2,1)}, u32[]{:S(2)}, u32[]{:S(2)}) %collective-permute-start.17) | collective-permute-done | bytes 589856 | tf_op jit(solution)/shard_map/ppermute | solution.py:740
  168.4 10.3 %collective-permute-done.28 = bf16[2,3,96,768]{3,2,0,1:T(8,128)(2,1)S(1)} collective-permute-done((bf16[2,3,96,768]{3,2,0,1:T(8,128)(2,1)S(1)}, bf16[2,3,96,768]{3,2,0,1:T(8,128)(2,1)S(1)}, u32[]{:S(2)}, u32[]{:S(2)}) %collective-permute-start.28) | collective-permute-done | bytes 884768 | tf_op jit(solution)/shard_map/ppermute | solution.py:740
  186.7 34.2 %middle.1 = (bf16[512,768]{1,0:T(8,128)(2,1)}, f32[512,768]{1,0:T(8,128)}, bf16[512,192]{1,0:T(8,128)(2,1)}, bf16[512,192]{1,0:T(8,128)(2,1)}, bf16[512,192]{1,0...) custom-call(s32[1]{0:T(128)} %bitcast.place, ...), custom_call_target="tpu_custom_call" | custom-call | flops 16307453952 | bytes 31457280 | tf_op jit(solution)/shard_map/middle/pallas_call | solution.py:657
  242.8 13.9 %memory_read_back.2 = (f32[4,192,256]{2,1,0:T(8,128)}, bf16[512,192]{1,0:T(8,128)(2,1)}, f32[32,256]{1,0:T(8,128)}, f32[4,512,256]{2,1,0:T(8,128)}, f32[8,512]{1,0:T(8,128)}) custom-call(s32[4,4]{1,0:T(4,128)} %pad_add_fusion.info, bf16[4,256,768]{2,1,0:T(8,128)(2,1)} %bitcast.304, bf16[4,256,192]{2,1,0:T(8,128)(2,1)} %bitcast.267, ...), custom_call_target="tpu_custom_call" | custom-call | flops 6442450944 | bytes 8388608 | tf_op jit(solution)/shard_map/memory_read_back/pallas_call | solution.py:510
  260.3 13.8 %memory_read_back.3 = (f32[4,192,256]{2,1,0:T(8,128)}, bf16[512,192]{1,0:T(8,128)(2,1)}, f32[32,256]{1,0:T(8,128)}, f32[4,512,256]{2,1,0:T(8,128)}, f32[8,512]{1,0:T(8,128)}) custom-call(s32[4,4]{1,0:T(4,128)} %pad_add_fusion.info, bf16[4,256,768]{2,1,0:T(8,128)(2,1)} %bitcast.309, bf16[4,256,192]{2,1,0:T(8,128)(2,1)} %bitcast.269, ...), custom_call_target="tpu_custom_call" | custom-call | flops 6442450944 | bytes 8388608 | tf_op jit(solution)/shard_map/memory_read_back/pallas_call | solution.py:510
  276.7 23.5 %attention_back.3 = (bf16[4,256,768]{2,1,0:T(8,128)(2,1)}, f32[8,512]{1,0:T(8,128)}) custom-call(s32[4,4]{1,0:T(4,128)} %pad_add_fusion.info, bf16[4,256,768]{2,1,0:T(8,128)(2,1)} %bitcast.310, bf16[4,256,192]{2,1,0:T(8,128)(2,1)} %bitcast.270, f32[4,8,256]{2,1,0:T(8,128)} %get-tuple-element.112.logsum, f32[4,192,256]{2,1,0:T(8,128)} %get-tuple-element.113.read_query, ...), custom_call_target="tpu_custom_call" | custom-call | flops 21474836480 | bytes 8388608 | tf_op jit(solution)/shard_map/attention_back/pallas_call | solution.py:539
  303.0 23.9 %attention_back.2 = (bf16[4,256,768]{2,1,0:T(8,128)(2,1)}, f32[8,512]{1,0:T(8,128)}) custom-call(s32[4,4]{1,0:T(4,128)} %pad_add_fusion.info, bf16[4,256,768]{2,1,0:T(8,128)(2,1)} %bitcast.305, bf16[4,256,192]{2,1,0:T(8,128)(2,1)} %bitcast.268, f32[4,8,256]{2,1,0:T(8,128)} %get-tuple-element.96.logsum, f32[4,192,256]{2,1,0:T(8,128)} %get-tuple-element.99.read_query, ...), custom_call_target="tpu_custom_call" | custom-call | flops 21474836480 | bytes 8388608 | tf_op jit(solution)/shard_map/attention_back/pallas_call | solution.py:539
  334.5 7.4 %rev.69 = bf16[4,2,1,96,576]{3,1,0,4,2:T(2,128)(2,1)S(1)} reverse(bf16[4,2,1,96,576]{3,1,0,4,2:T(2,128)(2,1)S(1)} %reshape_reshape.58), dimensions={1} | reverse | bytes 1769472 | tf_op jit(solution)/shard_map/rev | solution.py:776
  359.7 9.7 %rev.72 = bf16[4,2,1,96,576]{3,1,0,4,2:T(2,128)(2,1)} reverse(bf16[4,2,1,96,576]{3,1,0,4,2:T(2,128)(2,1)S(1)} %reshape_reshape.61), dimensions={1} | reverse | bytes 1769472 | tf_op jit(solution)/shard_map/rev | solution.py:776
  384.0 22.3 %psum.7 = f32[4416]{0:T(1024)S(1)} all-reduce(f32[4416]{0:T(1024)S(1)} %fusion.40), channel_id=1, replica_groups=mesh['dp'=8,'head'=4] {'dp'}, use_global_device_ids=true, to_apply=%region_12.13 | all-reduce | flops 4416 | bytes 35328 | tf_op jit(solution)/shard_map/psum | solution.py:926
  432.1 6.8 %collective-permute-done.46 = bf16[2,96,576]{2,1,0:T(8,128)(2,1)S(1)} collective-permute-done((bf16[2,96,576]{2,1,0:T(8,128)(2,1)S(1)}, bf16[2,96,576]{2,1,0:T(8,128)(2,1)S(1)}, u32[]{:S(2)}, u32[]{:S(2)}) %collective-permute-start.46) | collective-permute-done | bytes 221216 | tf_op jit(solution)/shard_map/ppermute | solution.py:740
  475.7 6.9 %collective-permute-done.50 = bf16[2,96,576]{2,1,0:T(8,128)(2,1)S(1)} collective-permute-done((bf16[2,96,576]{2,1,0:T(8,128)(2,1)S(1)}, bf16[2,96,576]{2,1,0:T(8,128)(2,1)S(1)}, u32[]{:S(2)}, u32[]{:S(2)}) %collective-permute-start.50) | collective-permute-done | bytes 221216 | tf_op jit(solution)/shard_map/ppermute | solution.py:740
  499.1 9.8 %rev.75 = bf16[4,2,1,96,576]{3,1,0,4,2:T(2,128)(2,1)} reverse(bf16[4,2,1,96,576]{3,1,0,4,2:T(2,128)(2,1)S(1)} %bitcast.211), dimensions={1} | reverse | bytes 1769472 | tf_op jit(solution)/shard_map/rev | solution.py:776
  509.0 9.1 %collective-permute-done.65 = bf16[2,4,96,768]{3,2,1,0:T(8,128)(2,1)} collective-permute-done((bf16[2,4,96,768]{3,2,1,0:T(8,128)(2,1)}, bf16[2,4,96,768]{3,2,1,0:T(8,128)(2,1)}, u32[]{:S(2)}, u32[]{:S(2)}) %collective-permute-start.65) | collective-permute-done | bytes 1179680 | tf_op jit(solution)/shard_map/ppermute | solution.py:740
  525.2 9.3 %collective-permute-done.66 = bf16[1,4,96,768]{3,2,1,0:T(8,128)(2,1)S(1)} collective-permute-done((bf16[1,4,96,768]{3,2,1,0:T(8,128)(2,1)S(1)}, bf16[1,4,96,768]{3,2,1,0:T(8,128)(2,1)S(1)}, u32[]{:S(2)}, u32[]{:S(2)}) %collective-permute-start.66) | collective-permute-done | bytes 589856 | tf_op jit(solution)/shard_map/ppermute | solution.py:740
  544.3 13.3 %collective-permute-done.68 = bf16[96,768]{1,0:T(8,128)(2,1)S(1)} collective-permute-done((bf16[96,768]{1,0:T(8,128)(2,1)S(1)}, bf16[96,768]{1,0:T(8,128)(2,1)S(1)}, u32[]{:S(2)}, u32[]{:S(2)}) %collective-permute-start.68) | collective-permute-done | bytes 147488 | tf_op jit(solution)/shard_map/ppermute | solution.py:740
  (561 shorter events, 290.3 us)
Async XLA Ops:
  27.8 43.3 %collective-permute-start.4 = (bf16[4,96,576]{2,1,0:T(8,128)(2,1)S(1)}, bf16[4,96,576]{2,1,0:T(8,128)(2,1)S(1)}, u32[]{:S(2)}, u32[]{:S(2)}) collective-permute-start(bf16[4,96,576]{2,1,0:T(8,128)(2,1)S(1)} %pad_maximum_fusion.16), channel_id=1, source_target_pairs={{0,16},{4,20},{8,24},{12,28},{16,0},{20,4},{24,8},{28,12},{1,17},{... | collective-permute-start | bytes 1327112 | tf_op jit(solution)/shard_map/ppermute | solution.py:740
  34.2 30.9 %collective-permute-start.14 = (bf16[32,768]{1,0:T(8,128)(2,1)S(1)}, bf16[32,768]{1,0:T(8,128)(2,1)S(1)}, u32[]{:S(2)}, u32[]{:S(2)}) collective-permute-start(bf16[32,768]{1,0:T(8,128)(2,1)S(1)} %pad_maximum_fusion.31), channel_id=1, source_target_pairs={{0,3},{1,2},{2,1},{3,0},{4,7},{5,6},{6,5},{7,4},{8,11},{9,10},{10,... | collective-permute-start | bytes 147464 | tf_op jit(solution)/shard_map/ppermute | solution.py:740
  39.2 66.9 %collective-permute-start.20 = (bf16[96,768]{1,0:T(8,128)(2,1)}, bf16[96,768]{1,0:T(8,128)(2,1)S(1)}, u32[]{:S(2)}, u32[]{:S(2)}) collective-permute-start(bf16[96,768]{1,0:T(8,128)(2,1)} %get-tuple-element.90), channel_id=1, source_target_pairs={{0,3},{1,2},{2,1},{3,0},{4,7},{5,6},{6,5},{7,4},{8,11},{9,10},{10,... | collective-permute-start | bytes 442376 | tf_op jit(solution)/shard_map/ppermute | solution.py:740
  65.1 41.7 %collective-permute-start.19 = (bf16[96,768]{1,0:T(8,128)(2,1)}, bf16[96,768]{1,0:T(8,128)(2,1)}, u32[]{:S(2)}, u32[]{:S(2)}) collective-permute-start(bf16[96,768]{1,0:T(8,128)(2,1)} %get-tuple-element.90), channel_id=1, source_target_pairs={{0,2},{1,3},{2,0},{3,1},{4,6},{5,7},{6,4},{7,5},{8,10},{9,11},{10,... | collective-permute-start | bytes 442376 | tf_op jit(solution)/shard_map/ppermute | solution.py:740
  65.2 44.7 %collective-permute-start.18 = (bf16[96,768]{1,0:T(8,128)(2,1)}, bf16[96,768]{1,0:T(8,128)(2,1)}, u32[]{:S(2)}, u32[]{:S(2)}) collective-permute-start(bf16[96,768]{1,0:T(8,128)(2,1)} %get-tuple-element.90), channel_id=1, source_target_pairs={{0,1},{1,0},{2,3},{3,2},{4,5},{5,4},{6,7},{7,6},{8,9},{9,8},{10,11... | collective-permute-start | bytes 442376 | tf_op jit(solution)/shard_map/ppermute | solution.py:740
  65.4 47.9 %collective-permute-start.26 = (bf16[96,768]{1,0:T(8,128)(2,1)}, bf16[96,768]{1,0:T(8,128)(2,1)}, u32[]{:S(2)}, u32[]{:S(2)}) collective-permute-start(bf16[96,768]{1,0:T(8,128)(2,1)} %get-tuple-element.91), channel_id=1, source_target_pairs={{0,3},{1,2},{2,1},{3,0},{4,7},{5,6},{6,5},{7,4},{8,11},{9,10},{10,... | collective-permute-start | bytes 442376 | tf_op jit(solution)/shard_map/ppermute | solution.py:740
  71.1 43.6 %collective-permute-start.25 = (bf16[96,768]{1,0:T(8,128)(2,1)}, bf16[96,768]{1,0:T(8,128)(2,1)}, u32[]{:S(2)}, u32[]{:S(2)}) collective-permute-start(bf16[96,768]{1,0:T(8,128)(2,1)} %get-tuple-element.91), channel_id=1, source_target_pairs={{0,2},{1,3},{2,0},{3,1},{4,6},{5,7},{6,4},{7,5},{8,10},{9,11},{10,... | collective-permute-start | bytes 442376 | tf_op jit(solution)/shard_map/ppermute | solution.py:740
  114.8 31.6 %collective-permute-start.7 = (f32[32,256]{1,0:T(8,128)S(1)}, f32[32,256]{1,0:T(8,128)S(1)}, u32[]{:S(2)}, u32[]{:S(2)}) collective-permute-start(f32[32,256]{1,0:T(8,128)S(1)} %copy-done.68), channel_id=1, source_target_pairs={{0,2},{1,3},{4,6},{5,7},{8,10},{9,11},{12,14},{13,15},{16,18},{17,... | collective-permute-start | bytes 98312 | tf_op jit(solution)/shard_map/ppermute | solution.py:795
  120.5 36.0 %collective-permute-start.27 = (bf16[1,3,96,768]{3,2,0,1:T(8,128)(2,1)S(1)}, bf16[1,3,96,768]{3,2,0,1:T(8,128)(2,1)S(1)}, u32[]{:S(2)}, u32[]{:S(2)}) collective-permute-start(bf16[1,3,96,768]{3,2,0,1:T(8,128)(2,1)S(1)} %maximum_bitcast_fusion.1), channel_id=1, source_target_pairs={{0,16},{4,20},{8,24},{12,28},{16,0},{20,4},{24,8},{28,12},{1,17},{... | collective-permute-start | bytes 1327112 | tf_op jit(solution)/shard_map/ppermute | solution.py:740
  123.0 33.2 %collective-permute-start.22 = (bf16[2,3,96,768]{3,2,0,1:T(8,128)(2,1)S(1)}, bf16[2,3,96,768]{3,2,0,1:T(8,128)(2,1)S(1)}, u32[]{:S(2)}, u32[]{:S(2)}) collective-permute-start(bf16[2,3,96,768]{3,2,0,1:T(8,128)(2,1)S(1)} %pad_maximum_fusion.8), channel_id=1, source_target_pairs={{0,16},{4,20},{8,24},{12,28},{16,0},{20,4},{24,8},{28,12},{1,17},{... | collective-permute-start | bytes 2654216 | tf_op jit(solution)/shard_map/ppermute | solution.py:740
  135.0 49.8 %collective-permute-start.11 = (bf16[512,192]{1,0:T(8,128)(2,1)S(1)}, bf16[512,192]{1,0:T(8,128)(2,1)}, u32[]{:S(2)}, u32[]{:S(2)}) collective-permute-start(bf16[512,192]{1,0:T(8,128)(2,1)S(1)} %bitcast.274), channel_id=1, source_target_pairs={{0,1},{1,0},{2,3},{3,2},{4,5},{5,4},{6,7},{7,6},{8,9},{9,8},{10,11... | collective-permute-start | bytes 589832 | tf_op jit(solution)/shard_map/ppermute | solution.py:740
  225.4 32.7 %collective-permute-start.31 = (bf16[512,192]{1,0:T(8,128)(2,1)}, bf16[512,192]{1,0:T(8,128)(2,1)S(1)}, u32[]{:S(2)}, u32[]{:S(2)}) collective-permute-start(bf16[512,192]{1,0:T(8,128)(2,1)} %get-tuple-element.104), channel_id=1, source_target_pairs={{0,1},{1,0},{2,3},{3,2},{4,5},{5,4},{6,7},{7,6},{8,9},{9,8},{10,11... | collective-permute-start | bytes 589832 | tf_op jit(solution)/shard_map/ppermute | solution.py:740
  232.7 176.2 %collective-permute-start.55 = (bf16[4,4,24,768]{3,2,0,1:T(8,128)(2,1)}, bf16[4,4,24,768]{3,2,0,1:T(8,128)(2,1)}, u32[]{:S(2)}, u32[]{:S(2)}) collective-permute-start(bf16[4,4,24,768]{3,2,0,1:T(8,128)(2,1)} %pad_maximum_fusion.11), channel_id=1, source_target_pairs={{0,4},{4,0},{8,12},{12,8},{16,20},{20,16},{24,28},{28,24},{1,5},{5... | collective-permute-start | bytes 1769480 | tf_op jit(solution)/shard_map/ppermute | solution.py:740
  241.3 245.2 %collective-permute-start.64 = (bf16[4,4,96,768]{3,2,1,0:T(8,128)(2,1)}, bf16[4,4,96,768]{3,2,1,0:T(8,128)(2,1)}, u32[]{:S(2)}, u32[]{:S(2)}) collective-permute-start(bf16[4,4,96,768]{3,2,1,0:T(8,128)(2,1)} %pad_maximum_fusion), channel_id=1, source_target_pairs={{0,4},{4,0},{8,12},{12,8},{16,20},{20,16},{24,28},{28,24},{1,5},{5... | collective-permute-start | bytes 7077896 | tf_op jit(solution)/shard_map/ppermute | solution.py:740
  241.9 140.1 %collective-permute-start.54 = (f32[768]{0:T(1024)S(1)}, f32[768]{0:T(1024)S(1)}, u32[]{:S(2)}, u32[]{:S(2)}) collective-permute-start(f32[768]{0:T(1024)S(1)} %add.211), channel_id=1, source_target_pairs={{0,1},{1,0},{2,3},{3,2},{4,5},{5,4},{6,7},{7,6},{8,9},{9,8},{10,11... | collective-permute-start | bytes 9224 | tf_op jit(solution)/shard_map/ppermute | solution.py:740
  274.1 28.1 %collective-permute-start.32 = (f32[32,256]{1,0:T(8,128)}, f32[32,256]{1,0:T(8,128)S(1)}, u32[]{:S(2)}, u32[]{:S(2)}) collective-permute-start(f32[32,256]{1,0:T(8,128)} %get-tuple-element.107.row_grads), channel_id=1, source_target_pairs={{2,0},{3,1},{6,4},{7,5},{10,8},{11,9},{14,12},{15,13},{18,16},{19,... | collective-permute-start | bytes 98312 | tf_op jit(solution)/shard_map/ppermute | solution.py:796
  302.2 78.0 %collective-permute-start.52 = (f32[4416]{0:T(1024)S(1)}, f32[4416]{0:T(1024)S(1)}, u32[]{:S(2)}, u32[]{:S(2)}) collective-permute-start(f32[4416]{0:T(1024)S(1)} %concatenate.105), channel_id=1, source_target_pairs={{0,2},{1,3},{2,0},{3,1},{4,6},{5,7},{6,4},{7,5},{8,10},{9,11},{10,... | collective-permute-start | bytes 53000 | tf_op jit(solution)/shard_map/ppermute | solution.py:740
  349.5 60.9 %collective-permute-start.42 = (bf16[4,96,576]{2,1,0:T(8,128)(2,1)}, bf16[4,96,576]{2,1,0:T(8,128)(2,1)}, u32[]{:S(2)}, u32[]{:S(2)}) collective-permute-start(bf16[4,96,576]{2,1,0:T(8,128)(2,1)} %pad_maximum_fusion.17), channel_id=1, source_target_pairs={{0,4},{4,0},{8,12},{12,8},{16,20},{20,16},{24,28},{28,24},{1,5},{5... | collective-permute-start | bytes 1327112 | tf_op jit(solution)/shard_map/ppermute | solution.py:740
  380.1 33.7 %collective-permute-start.45 = (bf16[4,96,576]{2,1,0:T(8,128)(2,1)}, bf16[4,96,576]{2,1,0:T(8,128)(2,1)}, u32[]{:S(2)}, u32[]{:S(2)}) collective-permute-start(bf16[4,96,576]{2,1,0:T(8,128)(2,1)} %pad_maximum_fusion.18), channel_id=1, source_target_pairs={{0,4},{4,0},{8,12},{12,8},{16,20},{20,16},{24,28},{28,24},{1,5},{5... | collective-permute-start | bytes 1327112 | tf_op jit(solution)/shard_map/ppermute | solution.py:740
  381.9 61.5 %collective-permute-start.36 = (bf16[512,768]{1,0:T(8,128)(2,1)S(1)}, bf16[512,768]{1,0:T(8,128)(2,1)S(1)}, u32[]{:S(2)}, u32[]{:S(2)}) collective-permute-start(bf16[512,768]{1,0:T(8,128)(2,1)S(1)} %slice.680), channel_id=1, source_target_pairs={{0,1},{1,0},{2,3},{3,2},{4,5},{5,4},{6,7},{7,6},{8,9},{9,8},{10,11... | collective-permute-start | bytes 2359304 | tf_op jit(solution)/shard_map/ppermute | solution.py:740
  430.5 59.8 %collective-permute-start.73 = (bf16[4,4,96,768]{3,2,1,0:T(8,128)(2,1)S(1)}, bf16[4,4,96,768]{3,2,1,0:T(8,128)(2,1)S(1)}, u32[]{:S(2)}, u32[]{:S(2)}) collective-permute-start(bf16[4,4,96,768]{3,2,1,0:T(8,128)(2,1)S(1)} %copy-done.19), channel_id=1, source_target_pairs={{0,4},{4,0},{8,12},{12,8},{16,20},{20,16},{24,28},{28,24},{1,5},{5... | collective-permute-start | bytes 7077896 | tf_op jit(solution)/shard_map/ppermute | solution.py:740
  431.5 37.0 %collective-permute-start.44 = (bf16[1,96,576]{2,1,0:T(8,128)(2,1)S(1)}, bf16[1,96,576]{2,1,0:T(8,128)(2,1)S(1)}, u32[]{:S(2)}, u32[]{:S(2)}) collective-permute-start(bf16[1,96,576]{2,1,0:T(8,128)(2,1)S(1)} %slice.697), channel_id=1, source_target_pairs={{0,16},{4,20},{8,24},{12,28},{16,0},{20,4},{24,8},{28,12},{1,17},{... | collective-permute-start | bytes 331784 | tf_op jit(solution)/shard_map/ppermute | solution.py:740
  489.7 28.3 %collective-permute-start.65 = (bf16[2,4,96,768]{3,2,1,0:T(8,128)(2,1)}, bf16[2,4,96,768]{3,2,1,0:T(8,128)(2,1)}, u32[]{:S(2)}, u32[]{:S(2)}) collective-permute-start(bf16[2,4,96,768]{3,2,1,0:T(8,128)(2,1)} %concatenate.119), channel_id=1, source_target_pairs={{0,16},{4,20},{8,24},{12,28},{16,0},{20,4},{24,8},{28,12},{1,17},{... | collective-permute-start | bytes 3538952 | tf_op jit(solution)/shard_map/ppermute | solution.py:740
  493.6 28.5 %collective-permute-start.74 = (bf16[2,4,96,768]{3,2,1,0:T(8,128)(2,1)}, bf16[2,4,96,768]{3,2,1,0:T(8,128)(2,1)}, u32[]{:S(2)}, u32[]{:S(2)}) collective-permute-start(bf16[2,4,96,768]{3,2,1,0:T(8,128)(2,1)} %pad_maximum_fusion.6), channel_id=1, source_target_pairs={{0,8},{4,12},{8,0},{12,4},{16,24},{20,28},{24,16},{28,20},{1,9},{5... | collective-permute-start | bytes 3538952 | tf_op jit(solution)/shard_map/ppermute | solution.py:740
  (135 other events, 1149.1 us)

commit v4 on v3

--- a/solution.py
+++ b/solution.py
@@ -17,6 +17,7 @@
 TAU = 0.75
 RIDGE = 0.5
 EPSILON = 1e-05
+MESH = pl.DeviceIdType.MESH
 SPREAD = 1.0 / 64.0
 WIDTH = 1.0 / BASIS
 LIVE = BASIS // 2
@@ -556,6 +557,131 @@
         info, qkv, grad_mixed, logsum, read_query, row_grads, value_grads, musig, rows, row_back, value_back, key_end,
         probe_part, table,
     )
+
+
+def other_of(index, bit):
+    return index + bit - 2 * bit * ((index // bit) % 2)
+
+
+class Hops:
+    def __init__(self, send, recv):
+        self.send, self.recv, self.used = send, recv, 0
+
+    def start(self, source, target, axis, bit):
+        copy = pltpu.make_async_remote_copy(
+            src_ref=source,
+            dst_ref=target,
+            send_sem=self.send.at[self.used],
+            recv_sem=self.recv.at[self.used],
+            device_id={axis: other_of(lax.axis_index(axis), bit)},
+            device_id_type=MESH,
+        )
+        self.used += 1
+        copy.start()
+        return copy
+
+
+def greet(neighbours):
+    barrier = pltpu.get_barrier_semaphore()
+    for axis, bit in neighbours:
+        pl.semaphore_signal(
+            barrier, inc=1, device_id={axis: other_of(lax.axis_index(axis), bit)}, device_id_type=MESH
+        )
+    pl.semaphore_wait(barrier, len(neighbours))
+
+
+def front_kernel(
+    source, scales, weight, small, qkv_a, qkv_b, first_rows, first_cols, flat_a, flat_b, far_small,
+    near, far, far_row, send, recv,
+):
+    own_rows, model = source.shape
+    wide = weight.shape[1]
+    width = wide // 3
+    place = lax.axis_index("dp") % 8
+    y, x, c = place // 4, (place // 2) % 2, place % 2
+    rows = model // 8
+    greet((("head", 1), ("head", 2), ("dp", 1), ("dp", 2), ("dp", 4)))
+    hops = Hops(send, recv)
+    mine = weight.at[pl.ds(pl.multiple_of(place * rows, 16), rows)]
+    slice_copy = hops.start(mine, far.at[y, x, c], "head", 2)
+    small_copy = hops.start(small, far_row, "head", 2)
+
+    def norm(part):
+        value = source[part].astype(F32)
+        centred = value - jnp.mean(value, axis=-1, keepdims=True)
+        factor = lax.rsqrt(jnp.mean(centred * centred, axis=-1, keepdims=True) + EPSILON)
+        return (centred * factor * scales[0:1] + scales[1:2]).astype(BF16)
+
+    row_copies = []
+    for k in range(own_rows // UNIT):
+        part = slice(k * UNIT, (k + 1) * UNIT)
+        first_rows[part] = norm(part)
+        row_copies.append(hops.start(first_rows.at[part], near.at[part], "head", 1))
+
+    slice_copy.wait_recv()
+    x_copy = hops.start(far.at[y, x, c], far.at[y, x, c], "dp", 2)
+
+    def widen(flat, read):
+        flat[...] = jnp.zeros_like(flat)
+        for k in range(3):
+            flat[:, k * LANES : k * LANES + width] = read(slice(k * width, (k + 1) * width))
+
+    widen(flat_a, lambda span: weight[:, span])
+
+    def project(unit, rows_in, flat, shift, out):
+        out[unit] = (dot(rows_in, flat[...]) + shift).astype(BF16)
+
+    for k in range(own_rows // UNIT):
+        project(k, first_rows[k * UNIT : (k + 1) * UNIT], flat_a, small[0:1], qkv_a)
+    x_copy.wait_recv()
+    y_copy = hops.start(far.at[y, :, c], far.at[y, :, c], "dp", 4)
+    first_cols[:, :own_rows] = first_rows[:own_rows].astype(F32).T.astype(BF16)
+    y_copy.wait_recv()
+    core_copy = hops.start(far.at[:, :, c], far.at[:, :, c], "dp", 1)
+    small_copy.wait_recv()
+    far_small[...] = far_row[...]
+    for k, copy in enumerate(row_copies):
+        copy.wait_recv()
+        part = slice(k * UNIT, (k + 1) * UNIT)
+        first_rows[own_rows + k * UNIT : own_rows + (k + 1) * UNIT] = near[part]
+        project(own_rows // UNIT + k, near[part], flat_a, small[0:1], qkv_a)
+    first_cols[:, own_rows:] = near[...].astype(F32).T.astype(BF16)
+    core_copy.wait_recv()
+    widen(flat_b, lambda span: far[:, :, :, :, span].reshape(model, width))
+    for k in range(2 * own_rows // UNIT):
+        project(k, first_rows[k * UNIT : (k + 1) * UNIT], flat_b, far_row[0:1], qkv_b)
+    for copy in [slice_copy, small_copy, x_copy, y_copy, core_copy] + row_copies:
+        copy.wait_send()
+
+
+def front(source, scales, weight, small):
+    own_rows, model = source.shape
+    wide = weight.shape[1]
+    units = 2 * own_rows // UNIT
+    hops = 5 + own_rows // UNIT
+    vmem = pl.BlockSpec(memory_space=pltpu.VMEM)
+    qkv = jax.ShapeDtypeStruct((units, UNIT, 3 * LANES), BF16)
+    flat = jax.ShapeDtypeStruct((model, 3 * LANES), BF16)
+    return pl.pallas_call(
+        front_kernel,
+        in_specs=[vmem] * 4,
+        out_specs=[vmem] * 7,
+        out_shape=[
+            qkv, qkv, jax.ShapeDtypeStruct((2 * own_rows, model), BF16),
+            jax.ShapeDtypeStruct((model, 2 * own_rows), BF16), flat, flat, jax.ShapeDtypeStruct(small.shape, F32),
+        ],
+        scratch_shapes=[
+            pltpu.VMEM((own_rows, model), BF16),
+            pltpu.VMEM((2, 2, 2, model // 8, wide), BF16),
+            pltpu.VMEM(small.shape, F32),
+            pltpu.SemaphoreType.DMA((hops,)),
+            pltpu.SemaphoreType.DMA((hops,)),
+        ],
+        compiler_params=pltpu.CompilerParams(
+            collective_id=1, has_side_effects=True, vmem_limit_bytes=56 << 20
+        ),
+        name="front",
+    )(source, scales, weight, small)
 
 
 def middle_kernel(
@@ -809,32 +935,16 @@
 
     source = inputs.astype(F32)
     gain_one = ln1_gain.astype(F32)
-    normed1, normal1, inverse1 = layer_norm(source, gain_one, ln1_bias.astype(F32))
-    first_own = normed1.astype(BF16)
-    first_rows = jnp.concatenate([first_own, exchange(first_own, "head", 1)], axis=0)
-
+    _, normal1, inverse1 = layer_norm(source, gain_one, ln1_bias.astype(F32))
     info = segment_info(lax.dynamic_slice_in_dim(seg_lengths[0], run * slots, slots, 0), units, z % 2, run)
-
-    far_slice = exchange(mine(qkv_weight.reshape(model, 3 * width), rows), "head", 2)
-    far_weight = to_order(plane_gather(far_slice, plain), own).reshape(model, 3, width)
-    far_small = exchange(
-        jnp.concatenate([qkv_bias.reshape(1, 3 * width), mem_mu.reshape(1, -1), mem_sig.reshape(1, -1)], axis=1),
-        "head", 2,
+    scales = jnp.concatenate([ln1_gain[None], ln1_bias[None], jnp.zeros((6, model), BF16)], axis=0).astype(F32)
+    bias_row = jnp.pad(qkv_bias, ((0, 0), (0, LANES - width))).reshape(1, 3 * LANES)
+    probe_rows = jnp.pad(jnp.concatenate([mem_mu, mem_sig], axis=0), ((0, 15 - 2 * heads), (0, 3 * LANES - BASIS)))
+    small = jnp.concatenate([bias_row, probe_rows], axis=0).astype(F32)
+    qkv_a, qkv_b, first_rows, first_cols, flat_a, flat_b, far_small = front(
+        inputs, scales, qkv_weight.reshape(model, 3 * width), small
     )
-    far_bias, far_probe = far_small[:, : 3 * width].reshape(3, width), far_small[0, 3 * width :].reshape(-1, BASIS)
-
-    def project(weight, bias, probe):
-        pad = ((0, 0), (0, 0), (0, LANES - width))
-        flat = jnp.pad(weight, pad).reshape(model, 3 * LANES)
-        shift = jnp.pad(bias, pad[1:]).reshape(3 * LANES).astype(F32)
-        value = (jnp.dot(first_rows, flat, preferred_element_type=F32) + shift).astype(BF16)
-        musig = jnp.concatenate([probe, jnp.zeros((8 - 2 * heads, BASIS), BF16)], axis=0).astype(F32)
-        return flat, value.reshape(units, UNIT, 3 * LANES), musig
-
-    sides = [
-        project(qkv_weight, qkv_bias, jnp.concatenate([mem_mu, mem_sig], axis=0)),
-        project(far_weight, far_bias, far_probe),
-    ]
+    sides = [(flat_a, qkv_a, small[1:9, :BASIS]), (flat_b, qkv_b, far_small[1:9, :BASIS])]
     states = [memory_state(info, qkv, musig, heads) for _, qkv, musig in sides]
     arrived = [(next_run(state[1]), next_run(state[4])) for state in states[::-1]]
     discrete = [attention(info, qkv, heads) for _, qkv, _ in sides]
@@ -907,7 +1017,7 @@
     out_weight_sum = to_order(plane_gather(out_slice, forth), own).reshape(width, model).astype(F32)
 
     def qkv_part(flat):
-        part = jnp.dot(first_rows.T, flat, preferred_element_type=F32).reshape(model, 3, LANES)[:, :, :width]
+        part = jnp.dot(first_cols, flat, preferred_element_type=F32).reshape(model, 3, LANES)[:, :, :width]
         part = to_order(part.astype(BF16).reshape(slices, rows, 3 * width), own)
         return plane_sum(part, plain, outer)
 

time: 590 us -> 601 us (1.019)
  Pallas kernels: 166 us -> 188 us
  local copies, waits for them, and re-layouts: 103 us -> 88.2 us
  other arithmetic: 60.2 us -> 45.8 us
  waiting for transfers between devices: 123 us -> 134 us
  starting transfers between devices: 90.7 us -> 101 us
  matrix products: 18.1 us -> 9.94 us
    pallas_call x0 -> x1, Pallas kernels: none -> 30.4 us  [front(): pl.pallas_call(front_kernel, in_specs=[vmem] * 4, out_specs=[vmem] * 7, o...]
    ppermute x4, starting transfers between devices: 7.11 us -> 20.7 us  [local(): next_run = lambda value: lax.ppermute(value, 'head', [(0, 2), (1, 3)])]
    dot_general x4 -> x2, matrix products: 13.9 us -> 5.66 us  [qkv_part(): jnp.dot(first_cols, flat, preferred_element_type=F32)]
    ppermute x74 -> x68, waiting for transfers between devices: 123 us -> 131 us  [exchange(): return lax.ppermute(value, axis, [(j, j ^ bit) for j in range(size)])]
    rev x4 -> x3, local copies, waits for them, and re-layouts: 34.3 us -> 26.9 us  [to_order(): shaped[:, ::-1]]
    ppermute x74 -> x68, starting transfers between devices: 78.5 us -> 74.6 us  [exchange(): return lax.ppermute(value, axis, [(j, j ^ bit) for j in range(size)])]
    unnamed x192 -> x170, local copies, waits for them, and re-layouts: 17.1 us -> 15.6 us
  transfers between devices with their start and end apart: 82 -> 76, of which waited for: 32 -> 32; matrix products, arithmetic and copies ran while one was open for 29% -> 22% of each run, Pallas kernels for 22% -> 26%
where the time goes in v4:
time: 601 us; the launch traced here: 592 us
  Pallas kernels  188 us (31%)
  waiting for transfers between devices  134 us (22%)
  starting transfers between devices  101 us (17%)
  local copies, waits for them, and re-layouts  88.2 us (15%)
  other arithmetic  45.8 us (8%)
  blocking collectives  22.4 us (4%)
  matrix products  9.94 us (2%)
    ppermute x68, waiting for transfers between devices, exchange(): return lax.ppermute(value, axis, [(j, j ^ bit) for j in range(size)])  131 us
    ppermute x68, starting transfers between devices, exchange(): return lax.ppermute(value, axis, [(j, j ^ bit) for j in range(size)])  74.6 us
    pallas_call x2, Pallas kernels, attention_back(): call(attend_back_kernel, heads, units, [whole(qkv.shape), unit_block(grad...  43.1 us
    pallas_call x1, Pallas kernels, middle(): pl.pallas_call(middle_kernel, grid_spec=pltpu.PrefetchScalarGridSpec(num_...  34 us
    pallas_call x1, Pallas kernels, front(): pl.pallas_call(front_kernel, in_specs=[vmem] * 4, out_specs=[vmem] * 7, o...  30.4 us
    rev x3, local copies, waits for them, and re-layouts, to_order(): shaped[:, ::-1]  26.9 us
    pallas_call x2, Pallas kernels, memory_read_back(): call(read_back_kernel, heads, units, [unit_block((units, UNIT, LANES), Tr...  25.1 us
    pallas_call x2, Pallas kernels, memory_state(): call(state_kernel, heads, units, [unit_block(qkv.shape, True), whole(musi...  23.9 us
  transfers between devices with their start and end apart: 76, of which 32 were waited for; matrix products, arithmetic and copies ran while one was open for 22% of the time, Pallas kernels for 26%

profile of v4, /device:TPU:0, one launch (start us, length us, event | category | flops | bytes accessed | tf_op | source)
XLA Modules:
  0.0 591.8 jit_solution(3911023731551590531)
XLA Ops:
  18.8 30.4 %front.1 = (bf16[4,256,768]{2,1,0:T(8,128)(2,1)}, bf16[4,256,768]{2,1,0:T(8,128)(2,1)}, bf16[1024,768]{1,0:T(8,128)(2,1)}, bf16[768,1024]{1,0:T(8,128)(2,1)}, bf...) custom-call(bf16[512,768]{1,0:T(8,128)(2,1)} %source.3, ...), custom_call_target="tpu_custom_call" | custom-call | tf_op jit(solution)/shard_map/front/pallas_call | solution.py:665
  51.4 6.0 %attention.3 = (f32[4,192,256]{2,1,0:T(8,128)}, f32[4,8,256]{2,1,0:T(8,128)}) custom-call(s32[4,4]{1,0:T(4,128)} %pad_add_fusion.info, bf16[4,256,768]{2,1,0:T(8,128)(2,1)} %get-tuple-element.87.qkv), custom_call_target="tpu_custom_call" | custom-call | flops 8589934592 | bytes 8388608 | tf_op jit(solution)/shard_map/attention/pallas_call | solution.py:482
  57.4 6.2 %attention.2 = (f32[4,192,256]{2,1,0:T(8,128)}, f32[4,8,256]{2,1,0:T(8,128)}) custom-call(s32[4,4]{1,0:T(4,128)} %pad_add_fusion.info, bf16[4,256,768]{2,1,0:T(8,128)(2,1)} %get-tuple-element.84.qkv), custom_call_target="tpu_custom_call" | custom-call | flops 8589934592 | bytes 8388608 | tf_op jit(solution)/shard_map/attention/pallas_call | solution.py:482
  63.6 11.9 %memory_state.3 = (f32[4,512,512]{2,1,0:T(8,128)}, bf16[512,192]{1,0:T(8,128)(2,1)}, f32[512,256]{1,0:T(8,128)}, f32[32,512]{1,0:T(8,128)}, f32[32,256]{1,0:T(8,128)}) custom-call(s32[4,4]{1,0:T(4,128)} %pad_add_fusion.info, bf16[4,256,768]{2,1,0:T(8,128)(2,1)} %get-tuple-element.87.qkv, f32[8,512]{1,0:T(8,128)} %slice.508.musig, ...), custom_call_target="tpu_custom_call" | custom-call | flops 5368709120 | bytes 8388608 | tf_op jit(solution)/shard_map/memory_state/pallas_call | solution.py:470
  75.6 12.0 %memory_state.2 = (f32[4,512,512]{2,1,0:T(8,128)}, bf16[512,192]{1,0:T(8,128)(2,1)}, f32[512,256]{1,0:T(8,128)}, f32[32,512]{1,0:T(8,128)}, f32[32,256]{1,0:T(8,128)}) custom-call(s32[4,4]{1,0:T(4,128)} %pad_add_fusion.info, bf16[4,256,768]{2,1,0:T(8,128)(2,1)} %get-tuple-element.84.qkv, f32[8,512]{1,0:T(8,128)} %slice.655.musig, ...), custom_call_target="tpu_custom_call" | custom-call | flops 5368709120 | bytes 8388608 | tf_op jit(solution)/shard_map/memory_state/pallas_call | solution.py:470
  111.8 13.6 %collective-permute-start.1 = (f32[32,256]{1,0:T(8,128)S(1)}, f32[32,256]{1,0:T(8,128)S(1)}, u32[]{:S(2)}, u32[]{:S(2)}) collective-permute-start(f32[32,256]{1,0:T(8,128)S(1)} %copy-done.58), channel_id=1, source_target_pairs={{0,2},{1,3},{4,6},{5,7},{8,10},{9,11},{12,14},{13,15},{16,18},{17,... | collective-permute-start | bytes 98312 | tf_op jit(solution)/shard_map/ppermute | solution.py:921
  128.2 8.7 %memory_read.3 = (bf16[4,256,192]{2,1,0:T(8,128)(2,1)}, f32[4,512,256]{2,1,0:T(8,128)}, f32[4,8,256]{2,1,0:T(8,128)}) custom-call(s32[4,4]{1,0:T(4,128)} %pad_add_fusion.info, bf16[4,256,768]{2,1,0:T(8,128)(2,1)} %get-tuple-element.87.qkv, f32[4,192,256]{2,1,0:T(8,128)} %get-tuple-element.92.discrete, f32[4,512,512]{2,1,0:T(8,128)} %get-tuple-element.93.states, ...), custom_call_target="tpu_custom_call" | custom-call | flops 3221225472 | bytes 8388608 | tf_op jit(solution)/shard_map/memory_read/pallas_call | solution.py:495
  138.7 7.7 %collective-permute-done.10 = bf16[2,4,24,768]{3,1,2,0:T(4,128)(2,1)S(1)} collective-permute-done((bf16[2,4,24,768]{3,1,2,0:T(4,128)(2,1)S(1)}, bf16[2,4,24,768]{3,1,2,0:T(4,128)(2,1)S(1)}, u32[]{:S(2)}, u32[]{:S(2)}) %collective-permute-start.10) | collective-permute-done | bytes 294944 | tf_op jit(solution)/shard_map/ppermute | solution.py:866
  146.4 14.8 %collective-permute-start.5 = (bf16[512,192]{1,0:T(8,128)(2,1)S(1)}, bf16[512,192]{1,0:T(8,128)(2,1)}, u32[]{:S(2)}, u32[]{:S(2)}) collective-permute-start(bf16[512,192]{1,0:T(8,128)(2,1)S(1)} %bitcast.250), channel_id=1, source_target_pairs={{0,1},{1,0},{2,3},{3,2},{4,5},{5,4},{6,7},{7,6},{8,9},{9,8},{10,11... | collective-permute-start | bytes 589832 | tf_op jit(solution)/shard_map/ppermute | solution.py:866
  162.6 8.3 %memory_read.2 = (bf16[4,256,192]{2,1,0:T(8,128)(2,1)}, f32[4,512,256]{2,1,0:T(8,128)}, f32[4,8,256]{2,1,0:T(8,128)}) custom-call(s32[4,4]{1,0:T(4,128)} %pad_add_fusion.info, bf16[4,256,768]{2,1,0:T(8,128)(2,1)} %get-tuple-element.84.qkv, f32[4,192,256]{2,1,0:T(8,128)} %get-tuple-element.85.discrete, f32[4,512,512]{2,1,0:T(8,128)} %get-tuple-element.86.states, ...), custom_call_target="tpu_custom_call" | custom-call | flops 3221225472 | bytes 8388608 | tf_op jit(solution)/shard_map/memory_read/pallas_call | solution.py:495
  180.0 15.3 %collective-permute-done.16 = bf16[2,3,96,768]{3,2,0,1:T(8,128)(2,1)S(1)} collective-permute-done((bf16[2,3,96,768]{3,2,0,1:T(8,128)(2,1)S(1)}, bf16[2,3,96,768]{3,2,0,1:T(8,128)(2,1)S(1)}, u32[]{:S(2)}, u32[]{:S(2)}) %collective-permute-start.16) | collective-permute-done | bytes 884768 | tf_op jit(solution)/shard_map/ppermute | solution.py:866
  203.2 34.0 %middle.1 = (bf16[512,768]{1,0:T(8,128)(2,1)}, f32[512,768]{1,0:T(8,128)}, bf16[512,192]{1,0:T(8,128)(2,1)}, bf16[512,192]{1,0:T(8,128)(2,1)}, bf16[512,192]{1,0...) custom-call(s32[1]{0:T(128)} %bitcast.place, ...), custom_call_target="tpu_custom_call" | custom-call | flops 16307453952 | bytes 31457280 | tf_op jit(solution)/shard_map/middle/pallas_call | solution.py:783
  260.6 12.7 %memory_read_back.2 = (f32[4,192,256]{2,1,0:T(8,128)}, bf16[512,192]{1,0:T(8,128)(2,1)}, f32[32,256]{1,0:T(8,128)}, f32[4,512,256]{2,1,0:T(8,128)}, f32[8,512]{1,0:T(8,128)}) custom-call(s32[4,4]{1,0:T(4,128)} %pad_add_fusion.info, bf16[4,256,768]{2,1,0:T(8,128)(2,1)} %get-tuple-element.84.qkv, bf16[4,256,192]{2,1,0:T(8,128)(2,1)} %bitcast.243, ...), custom_call_target="tpu_custom_call" | custom-call | flops 6442450944 | bytes 8388608 | tf_op jit(solution)/shard_map/memory_read_back/pallas_call | solution.py:511
  276.8 12.5 %memory_read_back.3 = (f32[4,192,256]{2,1,0:T(8,128)}, bf16[512,192]{1,0:T(8,128)(2,1)}, f32[32,256]{1,0:T(8,128)}, f32[4,512,256]{2,1,0:T(8,128)}, f32[8,512]{1,0:T(8,128)}) custom-call(s32[4,4]{1,0:T(4,128)} %pad_add_fusion.info, bf16[4,256,768]{2,1,0:T(8,128)(2,1)} %get-tuple-element.87.qkv, bf16[4,256,192]{2,1,0:T(8,128)(2,1)} %bitcast.245, ...), custom_call_target="tpu_custom_call" | custom-call | flops 6442450944 | bytes 8388608 | tf_op jit(solution)/shard_map/memory_read_back/pallas_call | solution.py:511
  294.6 21.5 %attention_back.3 = (bf16[4,256,768]{2,1,0:T(8,128)(2,1)}, f32[8,512]{1,0:T(8,128)}) custom-call(s32[4,4]{1,0:T(4,128)} %pad_add_fusion.info, bf16[4,256,768]{2,1,0:T(8,128)(2,1)} %get-tuple-element.87.qkv, bf16[4,256,192]{2,1,0:T(8,128)(2,1)} %bitcast.246, f32[4,8,256]{2,1,0:T(8,128)} %get-tuple-element.121.logsum, ...), custom_call_target="tpu_custom_call" | custom-call | flops 21474836480 | bytes 8388608 | tf_op jit(solution)/shard_map/attention_back/pallas_call | solution.py:540
  318.8 21.6 %attention_back.2 = (bf16[4,256,768]{2,1,0:T(8,128)(2,1)}, f32[8,512]{1,0:T(8,128)}) custom-call(s32[4,4]{1,0:T(4,128)} %pad_add_fusion.info, bf16[4,256,768]{2,1,0:T(8,128)(2,1)} %get-tuple-element.84.qkv, bf16[4,256,192]{2,1,0:T(8,128)(2,1)} %bitcast.244, f32[4,8,256]{2,1,0:T(8,128)} %get-tuple-element.104.logsum, ...), custom_call_target="tpu_custom_call" | custom-call | flops 21474836480 | bytes 8388608 | tf_op jit(solution)/shard_map/attention_back/pallas_call | solution.py:540
  347.8 7.4 %rev.57 = bf16[4,2,1,96,576]{3,1,0,4,2:T(2,128)(2,1)S(1)} reverse(bf16[4,2,1,96,576]{3,1,0,4,2:T(2,128)(2,1)S(1)} %reshape_reshape.46), dimensions={1} | reverse | bytes 1769472 | tf_op jit(solution)/shard_map/rev | solution.py:902
  369.5 9.8 %rev.60 = bf16[4,2,1,96,576]{3,1,0,4,2:T(2,128)(2,1)} reverse(bf16[4,2,1,96,576]{3,1,0,4,2:T(2,128)(2,1)S(1)} %reshape_reshape.49), dimensions={1} | reverse | bytes 1769472 | tf_op jit(solution)/shard_map/rev | solution.py:902
  392.1 22.4 %psum.7 = f32[4416]{0:T(1024)S(1)} all-reduce(f32[4416]{0:T(1024)S(1)} %fusion.43), channel_id=1, replica_groups=mesh['dp'=8,'head'=4] {'dp'}, use_global_device_ids=true, to_apply=%region_12.13 | all-reduce | flops 4416 | bytes 35328 | tf_op jit(solution)/shard_map/psum | solution.py:1036
  483.3 6.8 %collective-permute-done.44 = bf16[2,96,576]{2,1,0:T(8,128)(2,1)S(1)} collective-permute-done((bf16[2,96,576]{2,1,0:T(8,128)(2,1)S(1)}, bf16[2,96,576]{2,1,0:T(8,128)(2,1)S(1)}, u32[]{:S(2)}, u32[]{:S(2)}) %collective-permute-start.44) | collective-permute-done | bytes 221216 | tf_op jit(solution)/shard_map/ppermute | solution.py:866
  500.1 23.1 %collective-permute-done.68 = bf16[2,4,96,768]{3,2,1,0:T(8,128)(2,1)S(1)} collective-permute-done((bf16[2,4,96,768]{3,2,1,0:T(8,128)(2,1)S(1)}, bf16[2,4,96,768]{3,2,1,0:T(8,128)(2,1)S(1)}, u32[]{:S(2)}, u32[]{:S(2)}) %collective-permute-start.68) | collective-permute-done | bytes 1179680 | tf_op jit(solution)/shard_map/ppermute | solution.py:866
  530.6 9.7 %rev.63 = bf16[4,2,1,96,576]{3,1,0,4,2:T(2,128)(2,1)} reverse(bf16[4,2,1,96,576]{3,1,0,4,2:T(2,128)(2,1)S(1)} %bitcast.194), dimensions={1} | reverse | bytes 1769472 | tf_op jit(solution)/shard_map/rev | solution.py:902
  548.5 6.8 %collective-permute-done.71 = bf16[96,768]{1,0:T(8,128)(2,1)S(1)} collective-permute-done((bf16[96,768]{1,0:T(8,128)(2,1)S(1)}, bf16[96,768]{1,0:T(8,128)(2,1)S(1)}, u32[]{:S(2)}, u32[]{:S(2)}) %collective-permute-start.71) | collective-permute-done | bytes 147488 | tf_op jit(solution)/shard_map/ppermute | solution.py:866
  563.3 7.7 %collective-permute-done.62 = bf16[96,768]{1,0:T(8,128)(2,1)S(1)} collective-permute-done((bf16[96,768]{1,0:T(8,128)(2,1)S(1)}, bf16[96,768]{1,0:T(8,128)(2,1)S(1)}, u32[]{:S(2)}, u32[]{:S(2)}) %collective-permute-start.62) | collective-permute-done | bytes 147488 | tf_op jit(solution)/shard_map/ppermute | solution.py:866
  (505 shorter events, 257.9 us)
Async XLA Ops:
  3.3 91.3 %collective-permute-start.18 = (bf16[96,768]{1,0:T(8,128)(2,1)S(1)}, bf16[96,768]{1,0:T(8,128)(2,1)S(1)}, u32[]{:S(2)}, u32[]{:S(2)}) collective-permute-start(bf16[96,768]{1,0:T(8,128)(2,1)S(1)} %get-tuple-element.99), channel_id=1, source_target_pairs={{0,1},{1,0},{2,3},{3,2},{4,5},{5,4},{6,7},{7,6},{8,9},{9,8},{10,11... | collective-permute-start | bytes 442376 | tf_op jit(solution)/shard_map/ppermute | solution.py:866
  6.4 89.5 %collective-permute-start.19 = (bf16[96,768]{1,0:T(8,128)(2,1)S(1)}, bf16[96,768]{1,0:T(8,128)(2,1)S(1)}, u32[]{:S(2)}, u32[]{:S(2)}) collective-permute-start(bf16[96,768]{1,0:T(8,128)(2,1)S(1)} %get-tuple-element.99), channel_id=1, source_target_pairs={{0,2},{1,3},{2,0},{3,1},{4,6},{5,7},{6,4},{7,5},{8,10},{9,11},{10,... | collective-permute-start | bytes 442376 | tf_op jit(solution)/shard_map/ppermute | solution.py:866
  9.0 90.6 %collective-permute-start.20 = (bf16[96,768]{1,0:T(8,128)(2,1)S(1)}, bf16[96,768]{1,0:T(8,128)(2,1)S(1)}, u32[]{:S(2)}, u32[]{:S(2)}) collective-permute-start(bf16[96,768]{1,0:T(8,128)(2,1)S(1)} %get-tuple-element.99), channel_id=1, source_target_pairs={{0,3},{1,2},{2,1},{3,0},{4,7},{5,6},{6,5},{7,4},{8,11},{9,10},{10,... | collective-permute-start | bytes 442376 | tf_op jit(solution)/shard_map/ppermute | solution.py:866
  9.0 79.0 %collective-permute-start.6 = (bf16[32,768]{1,0:T(8,128)(2,1)S(1)}, bf16[32,768]{1,0:T(8,128)(2,1)S(1)}, u32[]{:S(2)}, u32[]{:S(2)}) collective-permute-start(bf16[32,768]{1,0:T(8,128)(2,1)S(1)} %pad_maximum_fusion.27), channel_id=1, source_target_pairs={{0,1},{1,0},{2,3},{3,2},{4,5},{5,4},{6,7},{7,6},{8,9},{9,8},{10,11... | collective-permute-start | bytes 147464 | tf_op jit(solution)/shard_map/ppermute | solution.py:866
  9.9 79.6 %collective-permute-start.7 = (bf16[32,768]{1,0:T(8,128)(2,1)S(1)}, bf16[32,768]{1,0:T(8,128)(2,1)S(1)}, u32[]{:S(2)}, u32[]{:S(2)}) collective-permute-start(bf16[32,768]{1,0:T(8,128)(2,1)S(1)} %pad_maximum_fusion.27), channel_id=1, source_target_pairs={{0,2},{1,3},{2,0},{3,1},{4,6},{5,7},{6,4},{7,5},{8,10},{9,11},{10,... | collective-permute-start | bytes 147464 | tf_op jit(solution)/shard_map/ppermute | solution.py:866
  95.9 31.5 %collective-permute-start.3 = (bf16[512,192]{1,0:T(8,128)(2,1)S(1)}, bf16[512,192]{1,0:T(8,128)(2,1)S(1)}, u32[]{:S(2)}, u32[]{:S(2)}) collective-permute-start(bf16[512,192]{1,0:T(8,128)(2,1)S(1)} %copy-done.51), channel_id=1, source_target_pairs={{0,2},{1,3},{4,6},{5,7},{8,10},{9,11},{12,14},{13,15},{16,18},{17,... | collective-permute-start | bytes 589832 | tf_op jit(solution)/shard_map/ppermute | solution.py:921
  105.7 56.4 %collective-permute-start = (bf16[512,192]{1,0:T(8,128)(2,1)S(1)}, bf16[512,192]{1,0:T(8,128)(2,1)}, u32[]{:S(2)}, u32[]{:S(2)}) collective-permute-start(bf16[512,192]{1,0:T(8,128)(2,1)S(1)} %copy-done.50), channel_id=1, source_target_pairs={{0,2},{1,3},{4,6},{5,7},{8,10},{9,11},{12,14},{13,15},{16,18},{17,... | collective-permute-start | bytes 589832 | tf_op jit(solution)/shard_map/ppermute | solution.py:921
  110.9 50.7 %collective-permute-start.22 = (bf16[2,3,96,768]{3,2,0,1:T(8,128)(2,1)S(1)}, bf16[2,3,96,768]{3,2,0,1:T(8,128)(2,1)S(1)}, u32[]{:S(2)}, u32[]{:S(2)}) collective-permute-start(bf16[2,3,96,768]{3,2,0,1:T(8,128)(2,1)S(1)} %pad_maximum_fusion.7), channel_id=1, source_target_pairs={{0,8},{4,12},{8,0},{12,4},{16,24},{20,28},{24,16},{28,20},{1,9},{5... | collective-permute-start | bytes 2654216 | tf_op jit(solution)/shard_map/ppermute | solution.py:866
  111.8 50.2 %collective-permute-start.1 = (f32[32,256]{1,0:T(8,128)S(1)}, f32[32,256]{1,0:T(8,128)S(1)}, u32[]{:S(2)}, u32[]{:S(2)}) collective-permute-start(f32[32,256]{1,0:T(8,128)S(1)} %copy-done.58), channel_id=1, source_target_pairs={{0,2},{1,3},{4,6},{5,7},{8,10},{9,11},{12,14},{13,15},{16,18},{17,... | collective-permute-start | bytes 98312 | tf_op jit(solution)/shard_map/ppermute | solution.py:921
  125.7 45.3 %collective-permute-start.15 = (bf16[1,3,96,768]{3,2,0,1:T(8,128)(2,1)S(1)}, bf16[1,3,96,768]{3,2,0,1:T(8,128)(2,1)S(1)}, u32[]{:S(2)}, u32[]{:S(2)}) collective-permute-start(bf16[1,3,96,768]{3,2,0,1:T(8,128)(2,1)S(1)} %maximum_bitcast_fusion), channel_id=1, source_target_pairs={{0,8},{4,12},{8,0},{12,4},{16,24},{20,28},{24,16},{28,20},{1,9},{5... | collective-permute-start | bytes 1327112 | tf_op jit(solution)/shard_map/ppermute | solution.py:866
  146.4 55.0 %collective-permute-start.5 = (bf16[512,192]{1,0:T(8,128)(2,1)S(1)}, bf16[512,192]{1,0:T(8,128)(2,1)}, u32[]{:S(2)}, u32[]{:S(2)}) collective-permute-start(bf16[512,192]{1,0:T(8,128)(2,1)S(1)} %bitcast.250), channel_id=1, source_target_pairs={{0,1},{1,0},{2,3},{3,2},{4,5},{5,4},{6,7},{7,6},{8,9},{9,8},{10,11... | collective-permute-start | bytes 589832 | tf_op jit(solution)/shard_map/ppermute | solution.py:866
  162.0 34.8 %collective-permute-start.23 = (bf16[4,3,96,768]{3,2,0,1:T(8,128)(2,1)S(1)}, bf16[4,3,96,768]{3,2,0,1:T(8,128)(2,1)S(1)}, u32[]{:S(2)}, u32[]{:S(2)}) collective-permute-start(bf16[4,3,96,768]{3,2,0,1:T(8,128)(2,1)S(1)} %pad_maximum_fusion.3), channel_id=1, source_target_pairs={{0,4},{4,0},{8,12},{12,8},{16,20},{20,16},{24,28},{28,24},{1,5},{5... | collective-permute-start | bytes 5308424 | tf_op jit(solution)/shard_map/ppermute | solution.py:866
  174.1 27.3 %collective-permute-start.2 = (bf16[512,192]{1,0:T(8,128)(2,1)S(1)}, bf16[512,192]{1,0:T(8,128)(2,1)S(1)}, u32[]{:S(2)}, u32[]{:S(2)}) collective-permute-start(bf16[512,192]{1,0:T(8,128)(2,1)S(1)} %bitcast.253), channel_id=1, source_target_pairs={{0,1},{1,0},{2,3},{3,2},{4,5},{5,4},{6,7},{7,6},{8,9},{9,8},{10,11... | collective-permute-start | bytes 589832 | tf_op jit(solution)/shard_map/ppermute | solution.py:866
  243.4 249.4 %collective-permute-start.67 = (bf16[4,4,96,768]{3,2,1,0:T(8,128)(2,1)}, bf16[4,4,96,768]{3,2,1,0:T(8,128)(2,1)}, u32[]{:S(2)}, u32[]{:S(2)}) collective-permute-start(bf16[4,4,96,768]{3,2,1,0:T(8,128)(2,1)} %pad_maximum_fusion.1), channel_id=1, source_target_pairs={{0,4},{4,0},{8,12},{12,8},{16,20},{20,16},{24,28},{28,24},{1,5},{5... | collective-permute-start | bytes 7077896 | tf_op jit(solution)/shard_map/ppermute | solution.py:866
  249.8 167.2 %collective-permute-start.49 = (bf16[4,4,24,768]{3,2,0,1:T(8,128)(2,1)}, bf16[4,4,24,768]{3,2,0,1:T(8,128)(2,1)}, u32[]{:S(2)}, u32[]{:S(2)}) collective-permute-start(bf16[4,4,24,768]{3,2,0,1:T(8,128)(2,1)} %pad_maximum_fusion.9), channel_id=1, source_target_pairs={{0,4},{4,0},{8,12},{12,8},{16,20},{20,16},{24,28},{28,24},{1,5},{5... | collective-permute-start | bytes 1769480 | tf_op jit(solution)/shard_map/ppermute | solution.py:866
  255.0 137.0 %collective-permute-start.48 = (f32[768]{0:T(1024)S(1)}, f32[768]{0:T(1024)S(1)}, u32[]{:S(2)}, u32[]{:S(2)}) collective-permute-start(f32[768]{0:T(1024)S(1)} %add.174), channel_id=1, source_target_pairs={{0,1},{1,0},{2,3},{3,2},{4,5},{5,4},{6,7},{7,6},{8,9},{9,8},{10,11... | collective-permute-start | bytes 9224 | tf_op jit(solution)/shard_map/ppermute | solution.py:866
  318.0 72.2 %collective-permute-start.46 = (f32[4416]{0:T(1024)S(1)}, f32[4416]{0:T(1024)S(1)}, u32[]{:S(2)}, u32[]{:S(2)}) collective-permute-start(f32[4416]{0:T(1024)S(1)} %concatenate.101), channel_id=1, source_target_pairs={{0,2},{1,3},{2,0},{3,1},{4,6},{5,7},{6,4},{7,5},{8,10},{9,11},{10,... | collective-permute-start | bytes 53000 | tf_op jit(solution)/shard_map/ppermute | solution.py:866
  360.5 58.0 %collective-permute-start.36 = (bf16[4,96,576]{2,1,0:T(8,128)(2,1)}, bf16[4,96,576]{2,1,0:T(8,128)(2,1)}, u32[]{:S(2)}, u32[]{:S(2)}) collective-permute-start(bf16[4,96,576]{2,1,0:T(8,128)(2,1)} %pad_maximum_fusion.14), channel_id=1, source_target_pairs={{0,4},{4,0},{8,12},{12,8},{16,20},{20,16},{24,28},{28,24},{1,5},{5... | collective-permute-start | bytes 1327112 | tf_op jit(solution)/shard_map/ppermute | solution.py:866
  390.2 31.8 %collective-permute-start.39 = (bf16[4,96,576]{2,1,0:T(8,128)(2,1)}, bf16[4,96,576]{2,1,0:T(8,128)(2,1)}, u32[]{:S(2)}, u32[]{:S(2)}) collective-permute-start(bf16[4,96,576]{2,1,0:T(8,128)(2,1)} %pad_maximum_fusion.15), channel_id=1, source_target_pairs={{0,4},{4,0},{8,12},{12,8},{16,20},{20,16},{24,28},{28,24},{1,5},{5... | collective-permute-start | bytes 1327112 | tf_op jit(solution)/shard_map/ppermute | solution.py:866
  392.0 58.8 %collective-permute-start.30 = (bf16[512,768]{1,0:T(8,128)(2,1)S(1)}, bf16[512,768]{1,0:T(8,128)(2,1)S(1)}, u32[]{:S(2)}, u32[]{:S(2)}) collective-permute-start(bf16[512,768]{1,0:T(8,128)(2,1)S(1)} %slice.670), channel_id=1, source_target_pairs={{0,1},{1,0},{2,3},{3,2},{4,5},{5,4},{6,7},{7,6},{8,9},{9,8},{10,11... | collective-permute-start | bytes 2359304 | tf_op jit(solution)/shard_map/ppermute | solution.py:866
  437.4 59.2 %collective-permute-start.58 = (bf16[4,4,96,768]{3,2,1,0:T(8,128)(2,1)S(1)}, bf16[4,4,96,768]{3,2,1,0:T(8,128)(2,1)S(1)}, u32[]{:S(2)}, u32[]{:S(2)}) collective-permute-start(bf16[4,4,96,768]{3,2,1,0:T(8,128)(2,1)S(1)} %copy-done.19), channel_id=1, source_target_pairs={{0,4},{4,0},{8,12},{12,8},{16,20},{20,16},{24,28},{28,24},{1,5},{5... | collective-permute-start | bytes 7077896 | tf_op jit(solution)/shard_map/ppermute | solution.py:866
  441.5 34.4 %collective-permute-start.38 = (bf16[1,96,576]{2,1,0:T(8,128)(2,1)S(1)}, bf16[1,96,576]{2,1,0:T(8,128)(2,1)S(1)}, u32[]{:S(2)}, u32[]{:S(2)}) collective-permute-start(bf16[1,96,576]{2,1,0:T(8,128)(2,1)S(1)} %slice.687), channel_id=1, source_target_pairs={{0,16},{4,20},{8,24},{12,28},{16,0},{20,4},{24,8},{28,12},{1,17},{... | collective-permute-start | bytes 331784 | tf_op jit(solution)/shard_map/ppermute | solution.py:866
  495.1 28.1 %collective-permute-start.68 = (bf16[2,4,96,768]{3,2,1,0:T(8,128)(2,1)S(1)}, bf16[2,4,96,768]{3,2,1,0:T(8,128)(2,1)S(1)}, u32[]{:S(2)}, u32[]{:S(2)}) collective-permute-start(bf16[2,4,96,768]{3,2,1,0:T(8,128)(2,1)S(1)} %pad_maximum_fusion.5), channel_id=1, source_target_pairs={{0,8},{4,12},{8,0},{12,4},{16,24},{20,28},{24,16},{28,20},{1,9},{5... | collective-permute-start | bytes 3538952 | tf_op jit(solution)/shard_map/ppermute | solution.py:866
  497.4 28.5 %collective-permute-start.59 = (bf16[2,4,96,768]{3,2,1,0:T(8,128)(2,1)S(1)}, bf16[2,4,96,768]{3,2,1,0:T(8,128)(2,1)S(1)}, u32[]{:S(2)}, u32[]{:S(2)}) collective-permute-start(bf16[2,4,96,768]{3,2,1,0:T(8,128)(2,1)S(1)} %concatenate.115), channel_id=1, source_target_pairs={{0,16},{4,20},{8,24},{12,28},{16,0},{20,4},{24,8},{28,12},{1,17},{... | collective-permute-start | bytes 3538952 | tf_op jit(solution)/shard_map/ppermute | solution.py:866
  (118 other events, 938.2 us)

commit v5 on v4

--- a/solution.py
+++ b/solution.py
@@ -102,133 +102,9 @@
     return dot(high, value_high) + dot(high, value_low) + dot(low, value_high)
 
 
-def state_kernel(heads, info, qkv, musig, table, states, value_end, key_end, rows, proj, memory, sums):
-    b = pl.program_id(0)
-    width = heads * HEAD_DIM
-    start, length = info[0, b], info[1, b]
-
-    @pl.when(b == 0)
-    def _():
-        memory[...] = jnp.zeros_like(memory)
-        row = musig[...]
-        rows[0:8] = row
-        wide = 2 * (BASIS + LIVE)
-        for k in range(1, 4):
-            row = three_pass(row, table[:, :BASIS], table[:, wide : wide + BASIS])
-            rows[8 * k : 8 * k + 8] = row
-
-    @pl.when(start == b)
-    def _():
-        states[0] = memory[...]
-        sums[...] = jnp.zeros_like(sums)
-
-    token = lax.broadcasted_iota(jnp.int32, (LIVE, UNIT), 1) + (b - start) * UNIT
-    centre = (lax.broadcasted_iota(jnp.int32, (LIVE, UNIT), 0) + LIVE).astype(F32) / (BASIS - 1)
-    gap = place_of(token, length) - centre
-    psi = jnp.exp(gap * gap * (-0.5 / (WIDTH * WIDTH)))
-    psi_high = psi.astype(BF16)
-    psi_low = (psi - psi_high.astype(F32)).astype(BF16)
-    pairs = qkv[0, :, LANES : 3 * LANES]
-    sums[...] += dot(psi_high, pairs) + dot(psi_low, pairs)
-
-    @pl.when(b + 1 == start + length)
-    def _():
-        stacked = jnp.concatenate([memory[...], sums[...] * term_scale(length)], axis=0)
-        memory[...] = dot(table[...], split3(stacked))
-
-    @pl.when(b == pl.num_programs(0) - 1)
-    def _():
-        key = memory[:, :LANES]
-        key_end[...] = key
-        value_end[...] = memory[:, LANES : LANES + width].astype(BF16)
-        seen = dot(rows[...], key, precision=HIGHEST)
-        mask = head_rows(heads, LANES)
-        for k in range(4):
-            proj[8 * k : 8 * k + 8] = jnp.where(mask, seen[8 * k : 8 * k + 8], 0.0)
-
-
-def attend_kernel(heads, info, qkv, result, logsum, cols):
-    b = pl.program_id(0)
-    start = info[0, b]
-    flip = info[3, 0] * (pl.num_programs(0) // 2)
-    cols[b] = qkv[b ^ flip, :, 2 * LANES : 3 * LANES].astype(F32).T.astype(BF16)
-    query = qkv[b ^ flip, :, 0:LANES]
-    lane_head = lax.broadcasted_iota(jnp.int32, (UNIT, LANES), 1) // HEAD_DIM
-
-    def attend(blocks):
-        causal = lax.broadcasted_iota(jnp.int32, (UNIT, UNIT), 0) <= lax.broadcasted_iota(
-            jnp.int32, (UNIT, UNIT), 1
-        )
-        for h in range(heads):
-            own = jnp.where(lane_head == h, query.astype(F32) * (1.0 / math.sqrt(HEAD_DIM)), 0.0).astype(BF16)
-            scores = [
-                dot(qkv[(start + j) ^ flip, :, LANES : 2 * LANES], own, ((1,), (1,))) for j in range(blocks)
-            ]
-            scores[-1] = jnp.where(causal, scores[-1], -1e30)
-            highest = functools.reduce(jnp.maximum, [jnp.max(s, axis=0, keepdims=True) for s in scores])
-            weights = [jnp.exp(s - highest) for s in scores]
-            total = sum(jnp.sum(w, axis=0, keepdims=True) for w in weights)
-            rows = slice(h * HEAD_DIM, (h + 1) * HEAD_DIM)
-            part = sum(dot(cols[start + j, rows], weights[j].astype(BF16)) for j in range(blocks))
-            result[0, rows] = part * (1.0 / total)
-            logsum[0, h : h + 1] = highest + jnp.log(total)
-
-    for blocks in range(1, 5):
-        pl.when(b - start + 1 == blocks)(functools.partial(attend, blocks))
-
-
-def read_kernel(
-    heads, info, qkv, discrete, states, musig, table, value_in, proj, mixed, values, probes, carried, value_cols,
-):
-    b = pl.program_id(0)
-    width = heads * HEAD_DIM
-    start, order, run = info[0, b], info[2, b], info[3, 1]
-
-    @pl.when(b == 0)
-    def _():
-        carried[...] = jnp.zeros_like(carried)
-        carried[:, :width] = value_in[...].astype(F32)
-
-    @pl.when((start == b) & (b > 0) & (run > 0))
-    def _():
-        carried[...] = advance_values(table, carried[...])
-
-    seen = (start > 0) | (run > 0)
-
-    @pl.when(start == b)
-    def _():
-        rows = dot(musig[...], states[0, :, :LANES], precision=HIGHEST)
-        rows = jnp.where(head_rows(heads, LANES), rows, 0.0)
-        incoming = proj[pl.ds(pl.multiple_of(order * 8, 8), 8)]
-        probes[0] = (rows + incoming) * (1.0 / math.sqrt(HEAD_DIM))
-        value = states[0, :, LANES:] + carried[...]
-        values[0] = value
-        value_cols[...] = value.T.astype(BF16)
-
-    @pl.when(jnp.logical_not(seen))
-    def _():
-        mixed[0] = discrete[0].T.astype(BF16)
-
-    @pl.when(seen)
-    def _():
-        query = qkv[0]
-        logits = sum(dot(part, query, ((1,), (1,))) for part in split_rows(probes[0]))
-        location, variance = read_parts(logits, heads)
-        fall = -0.5 / variance
-        peak = WIDTH * lax.rsqrt(variance)
-        centres = lax.broadcasted_iota(jnp.int32, (BASIS, UNIT), 0).astype(F32) / (BASIS - 1)
-        parts = []
-        for h in range(heads):
-            gap = centres - location[h : h + 1]
-            density = jnp.exp(gap * gap * fall[h : h + 1]).astype(BF16)
-            rows = slice(h * HEAD_DIM, (h + 1) * HEAD_DIM)
-            parts.append(discrete[0, rows] + dot(value_cols[rows], density) * peak[h : h + 1])
-        mixed[0] = jnp.concatenate(parts, axis=0).T.astype(BF16)
-
-
 def read_back_kernel(
     heads, info, qkv, grad_mixed, values, probes, states, table, query_grad, value_back, row_grads, value_grads,
-    probe_grad, carried, value_high, value_low, grad_values, probe_cols, row_grad,
+    probe_grad, carried, grad_values, probe_cols, row_grad,
 ):
     step = pl.program_id(0)
     b = pl.num_programs(0) - 1 - step
@@ -247,10 +123,6 @@
         grad_values[...] = jnp.zeros_like(grad_values)
         row_grad[...] = jnp.zeros_like(row_grad)
         probe_cols[...] = jnp.concatenate([probes[0], jnp.zeros((120, LANES), F32)], axis=0).T
-        value = values[0]
-        high = value.astype(BF16)
-        value_high[...] = high
-        value_low[...] = (value - high.astype(F32)).astype(BF16)
 
     @pl.when(jnp.logical_not(seen))
     def _():
@@ -273,9 +145,7 @@
             gap = centres - location[h : h + 1]
             square = gap * gap
             density = jnp.exp(square * fall[h : h + 1]) * peak[h : h + 1]
-            grad_density = dot(value_high[...], own_given, ((1,), (1,))) + dot(
-                value_low[...], own_given, ((1,), (1,))
-            )
+            grad_density = dot(values[0], own_given, ((1,), (1,)))
             grad_values[...] += dot(density.astype(BF16), own_given)
             weighed = density * grad_density
             zeroth = jnp.sum(weighed, axis=0, keepdims=True)
@@ -297,7 +167,7 @@
     def _():
         rows = jnp.where(head_rows(heads, LANES), row_grad[...], 0.0) * (1.0 / math.sqrt(HEAD_DIM))
         row_grads[pl.ds(pl.multiple_of(order * 8, 8), 8)] = rows
-        probe_grad[...] += dot(rows, states[0], ((1,), (1,)), HIGHEST)
+        probe_grad[...] += dot(rows, states[0].astype(F32), ((1,), (1,)), HIGHEST)
 
     @pl.when(b == start)
     def _():
@@ -463,48 +333,6 @@
     )
 
 
-def memory_state(info, qkv, musig, heads):
-    units, width = qkv.shape[0], heads * HEAD_DIM
-    table = jnp.asarray(basis_tables()[0])
-    states = (units, BASIS, 2 * LANES)
-    return call(
-        state_kernel, heads, units,
-        [unit_block(qkv.shape, True), whole(musig.shape), whole(table.shape)],
-        [place_block(states), whole((BASIS, width)), whole((BASIS, LANES)), whole((32, BASIS)), whole((32, LANES))],
-        [(states, F32), ((BASIS, width), BF16), ((BASIS, LANES), F32), ((32, BASIS), F32), ((32, LANES), F32)],
-        [pltpu.VMEM((BASIS, 2 * LANES), F32), pltpu.VMEM((LIVE, 2 * LANES), F32)],
-        5 << 30, units * UNIT * LIVE, "memory_state",
-    )(info, qkv, musig, table)
-
-
-def attention(info, qkv, heads):
-    units, width = qkv.shape[0], heads * HEAD_DIM
-    return call(
-        attend_kernel, heads, units,
-        [whole(qkv.shape)],
-        [unit_block((units, width, UNIT), False), unit_block((units, 8, UNIT), False)],
-        [((units, width, UNIT), F32), ((units, 8, UNIT), F32)],
-        [pltpu.VMEM((units, LANES, UNIT), BF16)],
-        8 << 30, 2 << 20, "attention",
-    )(info, qkv)
-
-
-def memory_read(info, qkv, discrete, states, musig, value_in, proj, heads):
-    units, width = qkv.shape[0], heads * HEAD_DIM
-    table = jnp.asarray(basis_tables()[0])
-    return call(
-        read_kernel, heads, units,
-        [
-            unit_block((units, UNIT, LANES), True), unit_block(discrete.shape, False), place_block(states.shape),
-            whole(musig.shape), whole(table.shape), whole(value_in.shape), whole(proj.shape),
-        ],
-        [unit_block((units, UNIT, width), True), place_block((units, BASIS, LANES)), place_block((units, 8, LANES))],
-        [((units, UNIT, width), BF16), ((units, BASIS, LANES), F32), ((units, 8, LANES), F32)],
-        [pltpu.VMEM((BASIS, LANES), F32), pltpu.VMEM((LANES, BASIS), BF16)],
-        3 << 30, 2 << 20, "memory_read",
-    )(info, qkv, discrete, states, musig, table, value_in, proj)
-
-
 def memory_read_back(info, qkv, grad_mixed, values, probes, states, heads):
     units, width = qkv.shape[0], heads * HEAD_DIM
     table = jnp.asarray(basis_tables()[1])
@@ -512,8 +340,8 @@
         read_back_kernel, heads, units,
         [
             unit_block((units, UNIT, LANES), True, True), unit_block(grad_mixed.shape, True, True),
-            place_block(values.shape, True), place_block(probes.shape, True),
-            place_block((units, BASIS, LANES), True), whole(table.shape),
+            unit_block(values.shape, False, True), unit_block(probes.shape, False, True),
+            unit_block((units, BASIS, LANES), False, True), whole(table.shape),
         ],
         [
             unit_block((units, width, UNIT), False, True), whole((BASIS, width)), whole((32, LANES)),
@@ -524,8 +352,8 @@
             ((8, BASIS), F32),
         ],
         [
-            pltpu.VMEM((BASIS, LANES), F32), pltpu.VMEM((BASIS, LANES), BF16), pltpu.VMEM((BASIS, LANES), BF16),
-            pltpu.VMEM((BASIS, LANES), F32), pltpu.VMEM((LANES, 128), F32), pltpu.VMEM((8, LANES), F32),
+            pltpu.VMEM((BASIS, LANES), F32), pltpu.VMEM((BASIS, LANES), F32), pltpu.VMEM((LANES, 128), F32),
+            pltpu.VMEM((8, LANES), F32),
         ],
         6 << 30, 2 << 20, "memory_read_back",
     )(info, qkv, grad_mixed, values, probes, states, table)
@@ -559,8 +387,13 @@
     )
 
 
-def other_of(index, bit):
-    return index + bit - 2 * bit * ((index // bit) % 2)
+def other_of(index, distance):
+    bit = 1
+    while bit <= distance:
+        if distance & bit:
+            index = index + bit - 2 * bit * ((index // bit) % 2)
+        bit *= 2
+    return index
 
 
 class Hops:
@@ -590,105 +423,331 @@
     pl.semaphore_wait(barrier, len(neighbours))
 
 
-def front_kernel(
-    source, scales, weight, small, qkv_a, qkv_b, first_rows, first_cols, flat_a, flat_b, far_small,
-    near, far, far_row, send, recv,
+def set_out(pairs, sems, first):
+    copies = [pltpu.make_async_copy(a, b, sems.at[first + k]) for k, (a, b) in enumerate(pairs)]
+    for copy in copies:
+        copy.start()
+    return copies
+
+
+def forward_kernel(
+    heads, info, source, scales, weight, small, bias_row, table, ff_in, ff_out, out_weight,
+    qkv_out, first_cols_out, flat_a_out, flat_b_out, logsum, values, probes, key_states, key_end, rows,
+    mixed_0, mixed_1, mixed_2, mixed_3, in_bias, far_in, far_out, far_weight,
+    qkv, first_rows, first_cols, flats, near, far, far_row, memory, sums, value_states, carried, value_ends, value_ins,
+    projs, proj_ins, cols, discrete, mixed, mixed_in, send, recv, local_sems,
 ):
     own_rows, model = source.shape
-    wide = weight.shape[1]
-    width = wide // 3
+    width = heads * HEAD_DIM
+    units = qkv.shape[1]
+    half = units // 2
+    root = 1.0 / math.sqrt(HEAD_DIM)
+    z = lax.axis_index("head")
+    flip, run = (z % 2) * half, z // 2
     place = lax.axis_index("dp") % 8
     y, x, c = place // 4, (place // 2) % 2, place % 2
-    rows = model // 8
-    greet((("head", 1), ("head", 2), ("dp", 1), ("dp", 2), ("dp", 4)))
+    slice_rows = model // 8
+    at = lambda b: (b + flip) % units
+    starts = [info[0, b] for b in range(units)]
+    lengths = [info[1, b] for b in range(units)]
+    orders = [info[2, b] for b in range(units)]
+    greet((("head", 1), ("head", 2), ("head", 3), ("dp", 1), ("dp", 2), ("dp", 4)))
     hops = Hops(send, recv)
-    mine = weight.at[pl.ds(pl.multiple_of(place * rows, 16), rows)]
-    slice_copy = hops.start(mine, far.at[y, x, c], "head", 2)
-    small_copy = hops.start(small, far_row, "head", 2)
-
-    def norm(part):
+    started = []
+
+    def go(*args):
+        started.append(hops.start(*args))
+        return started[-1]
+
+    mine = weight.at[pl.ds(pl.multiple_of(place * slice_rows, 16), slice_rows)]
+    slice_copy = go(mine, far.at[y, x, c], "head", 2)
+    small_copy = go(small, far_row, "head", 2)
+    row_copies = []
+    for k in range(half):
+        part = slice(k * UNIT, (k + 1) * UNIT)
         value = source[part].astype(F32)
         centred = value - jnp.mean(value, axis=-1, keepdims=True)
         factor = lax.rsqrt(jnp.mean(centred * centred, axis=-1, keepdims=True) + EPSILON)
-        return (centred * factor * scales[0:1] + scales[1:2]).astype(BF16)
-
-    row_copies = []
-    for k in range(own_rows // UNIT):
-        part = slice(k * UNIT, (k + 1) * UNIT)
-        first_rows[part] = norm(part)
-        row_copies.append(hops.start(first_rows.at[part], near.at[part], "head", 1))
-
+        first_rows[part] = (centred * factor * scales[0:1] + scales[1:2]).astype(BF16)
+        row_copies.append(go(first_rows.at[part], near.at[part], "head", 1))
     slice_copy.wait_recv()
-    x_copy = hops.start(far.at[y, x, c], far.at[y, x, c], "dp", 2)
-
-    def widen(flat, read):
-        flat[...] = jnp.zeros_like(flat)
-        for k in range(3):
-            flat[:, k * LANES : k * LANES + width] = read(slice(k * width, (k + 1) * width))
-
-    widen(flat_a, lambda span: weight[:, span])
-
-    def project(unit, rows_in, flat, shift, out):
-        out[unit] = (dot(rows_in, flat[...]) + shift).astype(BF16)
-
-    for k in range(own_rows // UNIT):
-        project(k, first_rows[k * UNIT : (k + 1) * UNIT], flat_a, small[0:1], qkv_a)
+    x_copy = go(far.at[y, x, c], far.at[y, x, c], "dp", 2)
+
+    def widen(k, read):
+        flats[k] = jnp.zeros((model, 3 * LANES), BF16)
+        for i in range(3):
+            flats[k, :, i * LANES : i * LANES + width] = read(slice(i * width, (i + 1) * width))
+
+    def project(k, unit, shift):
+        span = slice(unit * UNIT, (unit + 1) * UNIT)
+        qkv[k, unit] = (dot(first_rows[span], flats[k]) + shift).astype(BF16)
+
+    widen(0, lambda span: weight[:, span])
+    for unit in range(half):
+        project(0, unit, small[0:1])
     x_copy.wait_recv()
-    y_copy = hops.start(far.at[y, :, c], far.at[y, :, c], "dp", 4)
+    y_copy = go(far.at[y, :, c], far.at[y, :, c], "dp", 4)
     first_cols[:, :own_rows] = first_rows[:own_rows].astype(F32).T.astype(BF16)
     y_copy.wait_recv()
-    core_copy = hops.start(far.at[:, :, c], far.at[:, :, c], "dp", 1)
+    core_copy = go(far.at[:, :, c], far.at[:, :, c], "dp", 1)
     small_copy.wait_recv()
-    far_small[...] = far_row[...]
     for k, copy in enumerate(row_copies):
         copy.wait_recv()
         part = slice(k * UNIT, (k + 1) * UNIT)
         first_rows[own_rows + k * UNIT : own_rows + (k + 1) * UNIT] = near[part]
-        project(own_rows // UNIT + k, near[part], flat_a, small[0:1], qkv_a)
+        project(0, half + k, small[0:1])
+
+    in_mine = ff_in.at[pl.ds(pl.multiple_of(place * slice_rows, 16), slice_rows)]
+    out_mine = ff_out.at[pl.ds(pl.multiple_of(place * slice_rows, 16), slice_rows)]
+    gathers = ((far_in, 2, 4), (far_weight, 2, 4), (far_out, 4, 2))
+    stage = {}
+    for r in (1, 2, 3):
+        stage[r] = [
+            go(in_mine, far_in.at[r - 1, y, x, c], "head", r),
+            go(out_weight.at[place], far_weight.at[r - 1, y, x, c], "head", r),
+            go(out_mine, far_out.at[r - 1, y, x, c], "head", r),
+        ]
+    in_bias[0] = bias_row[...]
+    bias_copies = [go(bias_row, in_bias.at[r], "head", r) for r in (1, 2, 3)]
+
+    def advance(r, step):
+        for copy in stage[r]:
+            copy.wait_recv()
+        stage[r] = []
+        for array, first, second in gathers:
+            block = array.at[r - 1]
+            if step == 1:
+                part, bit = block.at[y, x, c], first
+            elif step == 2:
+                part, bit = (block.at[y, :, c] if first == 2 else block.at[:, x, c]), second
+            else:
+                part, bit = block.at[:, :, c], 1
+            stage[r].append(go(part, part, "dp", bit))
+
     first_cols[:, own_rows:] = near[...].astype(F32).T.astype(BF16)
     core_copy.wait_recv()
-    widen(flat_b, lambda span: far[:, :, :, :, span].reshape(model, width))
-    for k in range(2 * own_rows // UNIT):
-        project(k, first_rows[k * UNIT : (k + 1) * UNIT], flat_b, far_row[0:1], qkv_b)
-    for copy in [slice_copy, small_copy, x_copy, y_copy, core_copy] + row_copies:
+    widen(1, lambda span: far[:, :, :, :, span].reshape(model, width))
+    for unit in range(units):
+        project(1, unit, far_row[0:1])
+    saved = set_out(
+        [(qkv, qkv_out), (first_cols, first_cols_out), (flats.at[0], flat_a_out), (flats.at[1], flat_b_out)],
+        local_sems, 0,
+    )
+
+    def probe_of(k):
+        return jnp.where(k == 0, small[1:9, :BASIS], far_row[1:9, :BASIS])
+
+    mask = head_rows(heads, LANES)
+
+    def first_state(k, carry):
+        memory[k] = jnp.zeros(memory.shape[1:], F32)
+        row = probe_of(k)
+        rows[k, 0:8] = row
+        wide = 2 * (BASIS + LIVE)
+        for i in range(1, 4):
+            row = three_pass(row, table[:, :BASIS], table[:, wide : wide + BASIS])
+            rows[k, 8 * i : 8 * i + 8] = row
+        return carry
+
+    lax.fori_loop(0, 2, first_state, 0)
+
+    def state(b, k, carry):
+        start, length = starts[b], lengths[b]
+        now = memory[k]
+        value_states[k, b] = now[:, LANES:]
+        key_states[k, b] = now[:, :LANES].astype(BF16)
+        if b > 0:
+            probes[k, b] = jnp.where(mask, dot(rows[k, 0:8], now[:, :LANES], precision=HIGHEST), 0.0)
+        else:
+            probes[k, b] = jnp.zeros((8, LANES), F32)
+        token = lax.broadcasted_iota(jnp.int32, (LIVE, UNIT), 1) + (b - start) * UNIT
+        centre = (lax.broadcasted_iota(jnp.int32, (LIVE, UNIT), 0) + LIVE).astype(F32) / (BASIS - 1)
+        gap = place_of(token, length) - centre
+        psi = jnp.exp(gap * gap * (-0.5 / (WIDTH * WIDTH)))
+        psi_high = psi.astype(BF16)
+        psi_low = (psi - psi_high.astype(F32)).astype(BF16)
+        pairs = qkv[k, at(b), :, LANES : 3 * LANES]
+        fresh = dot(psi_high, pairs) + dot(psi_low, pairs)
+        gathered = fresh if b == 0 else jnp.where(start == b, 0.0, sums[k]) + fresh
+        sums[k] = gathered
+        stacked = jnp.concatenate([now, gathered * term_scale(length)], axis=0)
+        later = dot(table[...], split3(stacked))
+        memory[k] = jnp.where(start + length == b + 1, later, now)
+        return carry
+
+    def end_state(k, carry):
+        key = memory[k, :, :LANES]
+        key_end[k] = key
+        value_ends[k] = memory[k, :, LANES : LANES + width].astype(BF16)
+        seen = dot(rows[k], key, precision=HIGHEST)
+        for i in range(4):
+            projs[k, 8 * i : 8 * i + 8] = jnp.where(mask, seen[8 * i : 8 * i + 8], 0.0)
+        return carry
+
+    def attend(b, k, carry):
+        cols[k, b] = qkv[k, at(b), :, 2 * LANES : 3 * LANES].astype(F32).T.astype(BF16)
+        query = qkv[k, at(b), :, 0:LANES].astype(F32) * root
+        lane_head = lax.broadcasted_iota(jnp.int32, (UNIT, LANES), 1) // HEAD_DIM
+        causal = lax.broadcasted_iota(jnp.int32, (UNIT, UNIT), 0) <= lax.broadcasted_iota(
+            jnp.int32, (UNIT, UNIT), 1
+        )
+        away = [jnp.where(starts[b] <= j, 0.0, 1e30) for j in range(b)] + [0.0]
+        for h in range(heads):
+            own = jnp.where(lane_head == h, query, 0.0).astype(BF16)
+            scores = [dot(qkv[k, at(j), :, LANES : 2 * LANES], own, ((1,), (1,))) for j in range(b + 1)]
+            scores[b] = jnp.where(causal, scores[b], -1e30)
+            highest = functools.reduce(
+                jnp.maximum, [jnp.max(s, axis=0, keepdims=True) - away[j] for j, s in enumerate(scores)]
+            )
+            weights = [jnp.exp(s - (highest + away[j])) for j, s in enumerate(scores)]
+            total = sum(jnp.sum(w, axis=0, keepdims=True) for w in weights)
+            span = slice(h * HEAD_DIM, (h + 1) * HEAD_DIM)
+            part = sum(dot(cols[k, j, span], weights[j].astype(BF16)) for j in range(b + 1))
+            discrete[k, b, span] = part * (1.0 / total)
+            logsum[k, b, h : h + 1] = highest + jnp.log(total)
+        return carry
+
+    def seen_value(k, carry):
+        incoming = jnp.where(run > 0, value_ins[k].astype(F32), 0.0)
+        carried[:, :width] = incoming
+        carried[:, width:] = jnp.zeros((BASIS, LANES - width), F32)
+        for b in range(units):
+            if b > 0:
+                carried[...] = jnp.where(starts[b] == b, advance_values(table, carried[...]), carried[...])
+            values[k, b] = (value_states[k, b] + carried[...]).astype(BF16)
+            gained = jnp.zeros((8, LANES), F32)
+            for i in range(4):
+                gained += jnp.where((orders[b] == i) & (run > 0), proj_ins[k, 8 * i : 8 * i + 8], 0.0)
+            probes[k, b] = (probes[k, b] + gained) * root
+        return carry
+
+    def read(rel, k, carry):
+        b = at(rel)
+        query = qkv[k, rel, :, 0:LANES]
+        logits = sum(dot(part, query, ((1,), (1,))) for part in split_rows(probes[k, b]))
+        location, variance = read_parts(logits, heads)
+        fall = -0.5 / variance
+        peak = WIDTH * lax.rsqrt(variance)
+        centres = lax.broadcasted_iota(jnp.int32, (BASIS, UNIT), 0).astype(F32) / (BASIS - 1)
+        value_cols = values[k, b].astype(F32).T.astype(BF16)
+        parts = []
+        for h in range(heads):
+            gap = centres - location[h : h + 1]
+            density = jnp.exp(gap * gap * fall[h : h + 1]).astype(BF16)
+            span = slice(h * HEAD_DIM, (h + 1) * HEAD_DIM)
+            parts.append(discrete[k, b, span] + dot(value_cols[span], density) * peak[h : h + 1])
+        mixed[k, rel] = jnp.concatenate(parts, axis=0).T.astype(BF16)
+        return carry
+
+    for b in range(units):
+        lax.fori_loop(0, 2, functools.partial(state, b), 0)
+        if b == 1:
+            advance(1, 1)
+    lax.fori_loop(0, 2, end_state, 0)
+    state_copies = [go(value_ends.at[k], value_ins.at[1 - k], "head", 2) for k in range(2)]
+    state_copies += [go(projs.at[k], proj_ins.at[1 - k], "head", 2) for k in range(2)]
+    advance(1, 2)
+    for b in range(units):
+        lax.fori_loop(0, 2, functools.partial(attend, b), 0)
+        if b == 2:
+            advance(2, 1)
+            advance(3, 1)
+    advance(1, 3)
+    for copy in state_copies:
+        copy.wait_recv()
+    lax.fori_loop(0, 2, seen_value, 0)
+    advance(2, 2)
+    mixed_copies = []
+    for rel in (2, 3, 0, 1):
+        lax.fori_loop(0, 2, functools.partial(read, rel), 0)
+        if rel == 3:
+            advance(3, 2)
+            mixed_copies = [
+                go(mixed.at[k, half:], mixed_in.at[k], "head", 1) for k in range(2)
+            ]
+    mixed_0[...] = mixed[0, :half].reshape(own_rows, width)
+    mixed_2[...] = mixed[1, :half].reshape(own_rows, width)
+    advance(2, 3)
+    for copy in mixed_copies:
+        copy.wait_recv()
+    mixed_1[...] = mixed_in[0].reshape(own_rows, width)
+    mixed_3[...] = mixed_in[1].reshape(own_rows, width)
+    advance(3, 3)
+    for copy in bias_copies + stage[1] + stage[2] + stage[3]:
+        copy.wait_recv()
+    for copy in started:
         copy.wait_send()
-
-
-def front(source, scales, weight, small):
+    for copy in saved:
+        copy.wait()
+
+
+def forward(info, source, scales, weight, small, bias_row, ff_in, ff_out, out_slices, heads):
     own_rows, model = source.shape
-    wide = weight.shape[1]
     units = 2 * own_rows // UNIT
-    hops = 5 + own_rows // UNIT
-    vmem = pl.BlockSpec(memory_space=pltpu.VMEM)
-    qkv = jax.ShapeDtypeStruct((units, UNIT, 3 * LANES), BF16)
-    flat = jax.ShapeDtypeStruct((model, 3 * LANES), BF16)
+    width = heads * HEAD_DIM
+    hidden_part = ff_in.shape[1]
+    rows = model // 8
+    table = jnp.asarray(basis_tables()[0])
+    vmem, anywhere = pl.BlockSpec(memory_space=pltpu.VMEM), pl.BlockSpec(memory_space=pl.ANY)
+    shape = jax.ShapeDtypeStruct
+    hops = 2 + units // 2 + 3 + 3 * 3 * 4 + 3 + 4 + 2
     return pl.pallas_call(
-        front_kernel,
-        in_specs=[vmem] * 4,
-        out_specs=[vmem] * 7,
+        functools.partial(forward_kernel, heads),
+        in_specs=[pl.BlockSpec(memory_space=pltpu.SMEM)] + [vmem] * 6 + [anywhere] * 3,
+        out_specs=[anywhere] * 4 + [vmem] * 11 + [anywhere] * 3,
         out_shape=[
-            qkv, qkv, jax.ShapeDtypeStruct((2 * own_rows, model), BF16),
-            jax.ShapeDtypeStruct((model, 2 * own_rows), BF16), flat, flat, jax.ShapeDtypeStruct(small.shape, F32),
+            shape((2, units, UNIT, 3 * LANES), BF16),
+            shape((model, 2 * own_rows), BF16),
+            shape((model, 3 * LANES), BF16),
+            shape((model, 3 * LANES), BF16),
+            shape((2, units, 8, UNIT), F32),
+            shape((2, units, BASIS, LANES), BF16),
+            shape((2, units, 8, LANES), F32),
+            shape((2, units, BASIS, LANES), BF16),
+            shape((2, BASIS, LANES), F32),
+            shape((2, 32, BASIS), F32),
+        ] + [shape((own_rows, width), BF16)] * 4 + [
+            shape((4,) + bias_row.shape, F32),
+            shape((3, 2, 2, 2, rows, hidden_part), BF16),
+            shape((3, 2, 2, 2, rows, model), BF16),
+            shape((3, 2, 2, 2) + out_slices.shape[1:], BF16),
         ],
         scratch_shapes=[
+            pltpu.VMEM((2, units, UNIT, 3 * LANES), BF16),
+            pltpu.VMEM((2 * own_rows, model), BF16),
+            pltpu.VMEM((model, 2 * own_rows), BF16),
+            pltpu.VMEM((2, model, 3 * LANES), BF16),
             pltpu.VMEM((own_rows, model), BF16),
-            pltpu.VMEM((2, 2, 2, model // 8, wide), BF16),
+            pltpu.VMEM((2, 2, 2, rows, weight.shape[1]), BF16),
             pltpu.VMEM(small.shape, F32),
+            pltpu.VMEM((2, BASIS, 2 * LANES), F32),
+            pltpu.VMEM((2, LIVE, 2 * LANES), F32),
+            pltpu.VMEM((2, units, BASIS, LANES), F32),
+            pltpu.VMEM((BASIS, LANES), F32),
+            pltpu.VMEM((2, BASIS, width), BF16),
+            pltpu.VMEM((2, BASIS, width), BF16),
+            pltpu.VMEM((2, 32, LANES), F32),
+            pltpu.VMEM((2, 32, LANES), F32),
+            pltpu.VMEM((2, units, LANES, UNIT), BF16),
+            pltpu.VMEM((2, units, width, UNIT), F32),
+            pltpu.VMEM((2, units, UNIT, width), BF16),
+            pltpu.VMEM((2, units // 2, UNIT, width), BF16),
             pltpu.SemaphoreType.DMA((hops,)),
             pltpu.SemaphoreType.DMA((hops,)),
+            pltpu.SemaphoreType.DMA((4,)),
         ],
         compiler_params=pltpu.CompilerParams(
-            collective_id=1, has_side_effects=True, vmem_limit_bytes=56 << 20
+            collective_id=1, has_side_effects=True, vmem_limit_bytes=60 << 20
         ),
-        name="front",
-    )(source, scales, weight, small)
+        name="forward",
+    )(info, source, scales, weight, small, bias_row, table, ff_in, ff_out, out_slices)
 
 
 def middle_kernel(
-    place, source, cotangent, mixed_0, mixed_1, mixed_2, mixed_3, out_weight, vectors, in_bias, own_in, own_out, far_in,
-    far_out, outputs, grad_residual, grad_mixed_0, grad_mixed_1, grad_mixed_2, grad_mixed_3, grad_in, grad_out,
+    place, source, cotangent, mixed_0, mixed_1, mixed_2, mixed_3, own_weight, far_weight, vectors, in_bias, own_in, own_out,
+    far_in, far_out, outputs, grad_residual, grad_mixed_0, grad_mixed_1, grad_mixed_2, grad_mixed_3, grad_in, grad_out,
     grad_out_weight, sums, grad_in_bias,
-    residual, inverse, second, second_cols, total, grad_second, in_now, out_now,
+    residual, inverse, second, second_cols, total, grad_second, in_now, out_now, out_weight,
 ):
     r = pl.program_id(0)
     own = place[0]
@@ -700,6 +759,11 @@
     @pl.when(r == 0)
     def _():
         value = source[...].astype(F32) + out_bias
+        out_weight[0] = own_weight[...]
+        narrow = own_weight.shape[0] // slices
+        for k in range(far_weight.shape[0]):
+            parts = [far_weight[k, j].astype(F32)[:narrow] for j in range(slices)]
+            out_weight[k + 1] = jnp.concatenate(parts, axis=0).astype(BF16)
         for k, mixed in enumerate((mixed_0, mixed_1, mixed_2, mixed_3)):
             value += dot(mixed[...], out_weight[k])
         residual[...] = value
@@ -721,13 +785,13 @@
     @pl.when(r > 0)
     def _():
         for j in range(slices):
-            in_now[j * rows : (j + 1) * rows] = far_in[0, j ^ own]
-            out_now[j * rows : (j + 1) * rows] = far_out[0, j ^ own]
+            in_now[j * rows : (j + 1) * rows] = far_in[0, j]
+            out_now[j * rows : (j + 1) * rows] = far_out[0, j]
 
     half = hidden_part // 2
     for t in range(2):
         span = slice(t * half, (t + 1) * half)
-        hidden = dot(second[...], in_now[:, span]) + in_bias[pl.ds(r, 1), span]
+        hidden = dot(second[...], in_now[:, span]) + in_bias[r, 0:1, span]
         cube = hidden * hidden
         root = math.sqrt(2.0 / math.pi)
         bent = jnp.tanh(hidden * (root + (root * 0.044715) * cube))
@@ -772,7 +836,7 @@
             grad_out_weight[k] = dot(mixed[...], rounded, ((0,), (0,))).astype(BF16)
 
 
-def middle(place, source, cotangent, mixed, out_weight, vectors, in_bias, own_in, own_out, far_in, far_out):
+def middle(place, source, cotangent, mixed, out_weight, far_weight, vectors, in_bias, own_in, own_out, far_in, far_out):
     own_rows, model = source.shape
     shards = far_in.shape[0] + 1
     slices, rows, hidden_part = own_in.shape
@@ -786,11 +850,11 @@
             num_scalar_prefetch=1,
             grid=(shards,),
             in_specs=[whole(source.shape)] * 2 + [whole(narrow)] * 4 + [
-                whole(out_weight.shape), whole(vectors.shape), whole(in_bias.shape), whole(own_in.shape),
+                whole(out_weight.shape), whole(far_weight.shape), whole(vectors.shape), whole(in_bias.shape), whole(own_in.shape),
                 whole(own_out.shape), far, far,
             ],
             out_specs=[whole(source.shape)] * 2 + [whole(narrow)] * 4 + [
-                part, part, whole(out_weight.shape), whole((8, model)), whole(in_bias.shape)
+                part, part, whole((shards,) + narrow[1:] + (model,)), whole((8, model)), whole((shards, hidden_part))
             ],
             scratch_shapes=[
                 pltpu.VMEM((own_rows, model), F32),
@@ -801,6 +865,7 @@
                 pltpu.VMEM((own_rows, model), F32),
                 pltpu.VMEM((model, hidden_part), BF16),
                 pltpu.VMEM((hidden_part, model), BF16),
+                pltpu.VMEM((shards,) + narrow[1:] + (model,), BF16),
             ],
         ),
         out_shape=[
@@ -809,16 +874,16 @@
         ] + [jax.ShapeDtypeStruct(narrow, BF16)] * 4 + [
             jax.ShapeDtypeStruct((shards, slices, rows, hidden_part), BF16),
             jax.ShapeDtypeStruct((shards, slices, rows, hidden_part), BF16),
-            jax.ShapeDtypeStruct(out_weight.shape, BF16),
+            jax.ShapeDtypeStruct((shards,) + narrow[1:] + (model,), BF16),
             jax.ShapeDtypeStruct((8, model), F32),
-            jax.ShapeDtypeStruct(in_bias.shape, F32),
+            jax.ShapeDtypeStruct((shards, hidden_part), F32),
         ],
         compiler_params=pltpu.CompilerParams(vmem_limit_bytes=60 << 20),
         cost_estimate=pl.CostEstimate(
             flops=2 * macs, bytes_accessed=30 << 20, transcendentals=own_rows * shards * hidden_part
         ),
         name="middle",
-    )(place, source, cotangent, *mixed, out_weight, vectors, in_bias, own_in, own_out, far_in, far_out)
+    )(place, source, cotangent, *mixed, out_weight, far_weight, vectors, in_bias, own_in, own_out, far_in, far_out)
 
 
 def finish_kernel(place, given_in, given_out, grad_in, grad_out):
@@ -941,43 +1006,19 @@
     bias_row = jnp.pad(qkv_bias, ((0, 0), (0, LANES - width))).reshape(1, 3 * LANES)
     probe_rows = jnp.pad(jnp.concatenate([mem_mu, mem_sig], axis=0), ((0, 15 - 2 * heads), (0, 3 * LANES - BASIS)))
     small = jnp.concatenate([bias_row, probe_rows], axis=0).astype(F32)
-    qkv_a, qkv_b, first_rows, first_cols, flat_a, flat_b, far_small = front(
-        inputs, scales, qkv_weight.reshape(model, 3 * width), small
-    )
-    sides = [(flat_a, qkv_a, small[1:9, :BASIS]), (flat_b, qkv_b, far_small[1:9, :BASIS])]
-    states = [memory_state(info, qkv, musig, heads) for _, qkv, musig in sides]
-    arrived = [(next_run(state[1]), next_run(state[4])) for state in states[::-1]]
-    discrete = [attention(info, qkv, heads) for _, qkv, _ in sides]
-    reads = [
-        memory_read(info, qkv, discrete[k][0], states[k][0], musig, *arrived[k], heads)
-        for k, (_, qkv, musig) in enumerate(sides)
-    ]
-    mixed = [None] * 4
-    for k in range(2):
-        shared_rows = reads[k][0].reshape(2, own_rows, width)
-        mixed[2 * k] = shared_rows[0]
-        mixed[2 * k + 1] = exchange(shared_rows[1], "head", 1)
-
-    small = jnp.concatenate(
-        [mine(out_weight, narrow), jnp.broadcast_to(ff_in_bias[None], (8, hidden_part))[:, :model]], axis=0
-    )
-    ff_mine = (mine(ff_in, rows), mine(ff_out, rows))
-    small, ff_mine, first_rows = lax.optimization_barrier((small, ff_mine, first_rows))
-    small = jnp.stack([small] + [exchange(small, "head", r) for r in range(1, shards)])
-    in_bias = small[:, narrow].astype(F32)
-    out_full = to_order(plane_gather(small[:, :narrow], plain), own)
-    out_full = jnp.swapaxes(out_full, 0, 1).reshape(shards, width, model)
-    far_in = jnp.stack([exchange(ff_mine[0], "head", r) for r in range(1, shards)])
-    far_out = jnp.stack([exchange(ff_mine[1], "head", r) for r in range(1, shards)])
-    far_in = jnp.swapaxes(plane_gather(far_in, forth), 0, 1)
-    far_out = jnp.swapaxes(plane_gather(far_out, turned), 0, 1)
-
+    bias_in = jnp.broadcast_to(ff_in_bias[None].astype(F32), (8, hidden_part))
+    out_slices = jnp.pad(out_weight.reshape(slices, narrow, model), ((0, 0), (0, -narrow % 16), (0, 0)))
+    (
+        qkv, first_cols, flat_a, flat_b, logsum, values, probes, key_states, key_end, state_rows,
+        *mixed, in_bias, far_in, far_out, far_weight,
+    ) = forward(info, inputs, scales, qkv_weight.reshape(model, 3 * width), small, bias_in, ff_in, ff_out, out_slices, heads)
+    flat = lambda array: array.reshape((shards - 1, slices) + array.shape[4:])
     vectors = jnp.concatenate(
         [out_bias[None], ln2_gain[None], ln2_bias[None], ff_out_bias[None], jnp.zeros((4, model), BF16)], axis=0
     ).astype(F32)
     outputs, grad_residual, *rest = middle(
-        place, inputs, cotangent, mixed, out_full, vectors, in_bias,
-        ff_in.reshape(slices, rows, hidden_part), ff_out.reshape(slices, rows, model), far_in, far_out,
+        place, inputs, cotangent, mixed, out_weight, flat(far_weight), vectors, in_bias,
+        ff_in.reshape(slices, rows, hidden_part), ff_out.reshape(slices, rows, model), flat(far_in), flat(far_out),
     )
     grad_mixed, (ff_in_part, ff_out_part, out_weight_part, sums, in_bias_part) = rest[:4], rest[4:]
     given = [
@@ -985,21 +1026,21 @@
         for k in range(2)
     ]
 
+    musigs = [small[1:9, :BASIS], lax.optimization_barrier(state_rows[1, :8])]
     read_backs = [
-        memory_read_back(info, qkv, given[k], reads[k][1], reads[k][2], states[k][0], heads)
-        for k, (_, qkv, _) in enumerate(sides)
+        memory_read_back(info, qkv[k], given[k], values[k], probes[k], key_states[k], heads) for k in range(2)
     ]
     returned = [(last_run(back[1]), last_run(back[2])) for back in read_backs[::-1]]
     grads = []
-    for k, (_, qkv, musig) in enumerate(sides):
+    for k in range(2):
         query_part, _, row_grads, value_grads, probe_part = read_backs[k]
         grads.append(attention_back(
-            info, qkv, given[k], discrete[k][1], query_part, row_grads, value_grads, musig, states[k][3],
-            returned[k][1], returned[k][0], states[k][2], probe_part, heads,
+            info, qkv[k], given[k], logsum[k], query_part, row_grads, value_grads, musigs[k], state_rows[k],
+            returned[k][1], returned[k][0], key_end[k], probe_part, heads,
         ))
     flats = [grad[0].reshape(2 * own_rows, 3 * LANES) for grad in grads]
     grad_rows = sum(
-        jnp.dot(flat, sides[k][0].T, preferred_element_type=F32) for k, flat in enumerate(flats)
+        jnp.dot(grad, weight.T, preferred_element_type=F32) for grad, weight in zip(flats, (flat_a, flat_b))
     ).astype(BF16)
     grad_first = grad_rows[:own_rows].astype(F32) + exchange(grad_rows[own_rows:], "head", 1).astype(F32)
     grad_source = grad_residual + norm_back(grad_first, normal1, inverse1, gain_one)

time: 601 us -> 550 us (0.915)
  starting transfers between devices: 101 us -> 47.3 us
  waiting for transfers between devices: 134 us -> 90.8 us
  Pallas kernels: 188 us -> 222 us
  local copies, waits for them, and re-layouts: 88.2 us -> 96.3 us
    ppermute x68 -> x48, waiting for transfers between devices: 131 us -> 89.7 us  [exchange(): return lax.ppermute(value, axis, [(j, j ^ bit) for j in range(size)])]
    pallas_call x7 -> x1, Pallas kernels: 83.7 us -> 118 us  [forward(): pl.pallas_call(functools.partial(forward_kernel, heads), in_specs=[pl.Blo...]
    ppermute x68 -> x48, starting transfers between devices: 74.6 us -> 42.1 us  [exchange(): return lax.ppermute(value, axis, [(j, j ^ bit) for j in range(size)])]
    ppermute x4 -> x0, starting transfers between devices: 20.7 us -> none  [local(): next_run = lambda value: lax.ppermute(value, 'head', [(0, 2), (1, 3)])]
    squeeze x0 -> x7, local copies, waits for them, and re-layouts: none -> 7.59 us  [the longest x1 2.12 us: local(): key_states[k]]
    unnamed x170 -> x129, local copies, waits for them, and re-layouts: 15.6 us -> 10.8 us
  transfers between devices with their start and end apart: 76 -> 52, of which waited for: 32 -> 25; matrix products, arithmetic and copies ran while one was open for 22% -> 25% of each run, Pallas kernels for 26% -> 13%
where the time goes in v5:
time: 550 us; the launch traced here: 539 us
  Pallas kernels  222 us (40%)
  local copies, waits for them, and re-layouts  96.3 us (18%)
  waiting for transfers between devices  90.8 us (17%)
  starting transfers between devices  47.3 us (9%)
  other arithmetic  45.4 us (8%)
  blocking collectives  22.3 us (4%)
  matrix products  12.5 us (2%)
    pallas_call x1, Pallas kernels, forward(): pl.pallas_call(functools.partial(forward_kernel, heads), in_specs=[pl.Blo...  118 us
    ppermute x48, waiting for transfers between devices, exchange(): return lax.ppermute(value, axis, [(j, j ^ bit) for j in range(size)])  89.7 us
    pallas_call x2, Pallas kernels, attention_back(): call(attend_back_kernel, heads, units, [whole(qkv.shape), unit_block(grad...  42.9 us
    ppermute x48, starting transfers between devices, exchange(): return lax.ppermute(value, axis, [(j, j ^ bit) for j in range(size)])  42.1 us
    pallas_call x1, Pallas kernels, middle(): pl.pallas_call(middle_kernel, grid_spec=pltpu.PrefetchScalarGridSpec(num_...  34.3 us
    rev x3, local copies, waits for them, and re-layouts, to_order(): shaped[:, ::-1]  27 us
    pallas_call x2, Pallas kernels, memory_read_back(): call(read_back_kernel, heads, units, [unit_block((units, UNIT, LANES), Tr...  24.6 us
    psum x1, blocking collectives, local(): kept = lax.psum(kept, 'dp')  22.3 us
  transfers between devices with their start and end apart: 52, of which 25 were waited for; matrix products, arithmetic and copies ran while one was open for 25% of the time, Pallas kernels for 13%

profile of v5, /device:TPU:0, one launch (start us, length us, event | category | flops | bytes accessed | tf_op | source)
XLA Modules:
  0.0 539.0 jit_solution(4343049814846216923)
XLA Ops:
  13.8 117.8 %forward.1 = (bf16[2,4,256,768]{3,2,1,0:T(8,128)(2,1)}, bf16[768,1024]{1,0:T(8,128)(2,1)}, bf16[768,768]{1,0:T(8,128)(2,1)}, bf16[768,768]{1,0:T(8,128)(2,1)}, f...) custom-call(s32[4,4]{1,0:T(4,128)} %pad_add_fusion.info, ...), custom_call_target="tpu_custom_call" | custom-call | tf_op jit(solution)/shard_map/forward/pallas_call | solution.py:694
  131.6 34.3 %middle.1 = (bf16[512,768]{1,0:T(8,128)(2,1)}, f32[512,768]{1,0:T(8,128)}, bf16[512,192]{1,0:T(8,128)(2,1)}, bf16[512,192]{1,0:T(8,128)(2,1)}, bf16[512,192]{1,0...) custom-call(s32[1]{0:T(128)} %bitcast.place, ...), custom_call_target="tpu_custom_call" | custom-call | flops 16307453952 | bytes 31457280 | tf_op jit(solution)/shard_map/middle/pallas_call | solution.py:847
  174.4 4.6 copy_bitcast_fusion
  202.3 12.3 %memory_read_back.3 = (f32[4,192,256]{2,1,0:T(8,128)}, bf16[512,192]{1,0:T(8,128)(2,1)}, f32[32,256]{1,0:T(8,128)}, f32[4,512,256]{2,1,0:T(8,128)}, f32[8,512]{1,0:T(8,128)}) custom-call(s32[4,4]{1,0:T(4,128)} %pad_add_fusion.info, bf16[4,256,768]{2,1,0:T(8,128)(2,1)} %get-tuple-element.162.qkv, bf16[4,256,192]{2,1,0:T(8,128)(2,1)} %bitcast.229, ...), custom_call_target="tpu_custom_call" | custom-call | flops 6442450944 | bytes 8388608 | tf_op jit(solution)/shard_map/memory_read_back/pallas_call | solution.py:339
  218.1 12.3 %memory_read_back.2 = (f32[4,192,256]{2,1,0:T(8,128)}, bf16[512,192]{1,0:T(8,128)(2,1)}, f32[32,256]{1,0:T(8,128)}, f32[4,512,256]{2,1,0:T(8,128)}, f32[8,512]{1,0:T(8,128)}) custom-call(s32[4,4]{1,0:T(4,128)} %pad_add_fusion.info, bf16[4,256,768]{2,1,0:T(8,128)(2,1)} %get-tuple-element.161.qkv, bf16[4,256,192]{2,1,0:T(8,128)(2,1)} %bitcast.231, ...), custom_call_target="tpu_custom_call" | custom-call | flops 6442450944 | bytes 8388608 | tf_op jit(solution)/shard_map/memory_read_back/pallas_call | solution.py:339
  234.0 21.3 %attention_back.2 = (bf16[4,256,768]{2,1,0:T(8,128)(2,1)}, f32[8,512]{1,0:T(8,128)}) custom-call(s32[4,4]{1,0:T(4,128)} %pad_add_fusion.info, bf16[4,256,768]{2,1,0:T(8,128)(2,1)} %get-tuple-element.161.qkv, bf16[4,256,192]{2,1,0:T(8,128)(2,1)} %bitcast.232, f32[4,8,256]{2,1,0:T(8,128)} %get-tuple-element.222.logsum, ...), custom_call_target="tpu_custom_call" | custom-call | flops 21474836480 | bytes 8388608 | tf_op jit(solution)/shard_map/attention_back/pallas_call | solution.py:368
  258.3 21.6 %attention_back.3 = (bf16[4,256,768]{2,1,0:T(8,128)(2,1)}, f32[8,512]{1,0:T(8,128)}) custom-call(s32[4,4]{1,0:T(4,128)} %pad_add_fusion.info, bf16[4,256,768]{2,1,0:T(8,128)(2,1)} %get-tuple-element.162.qkv, bf16[4,256,192]{2,1,0:T(8,128)(2,1)} %bitcast.230, f32[4,8,256]{2,1,0:T(8,128)} %get-tuple-element.223.logsum, ...), custom_call_target="tpu_custom_call" | custom-call | flops 21474836480 | bytes 8388608 | tf_op jit(solution)/shard_map/attention_back/pallas_call | solution.py:368
  284.9 3.3 fusion.12
  289.5 7.4 %rev.48 = bf16[4,2,1,96,576]{3,1,0,4,2:T(2,128)(2,1)S(1)} reverse(bf16[4,2,1,96,576]{3,1,0,4,2:T(2,128)(2,1)S(1)} %reshape_reshape.41), dimensions={1} | reverse | bytes 1769472 | tf_op jit(solution)/shard_map/rev | solution.py:967
  303.9 3.3 fusion.14
  308.2 4.3 reshape_reshape.38
  312.6 9.8 %rev.45 = bf16[4,2,1,96,576]{3,1,0,4,2:T(2,128)(2,1)} reverse(bf16[4,2,1,96,576]{3,1,0,4,2:T(2,128)(2,1)S(1)} %reshape_reshape.38), dimensions={1} | reverse | bytes 1769472 | tf_op jit(solution)/shard_map/rev | solution.py:967
  327.0 3.3 fusion.61
  339.0 22.3 %psum.7 = f32[4416]{0:T(1024)S(1)} all-reduce(f32[4416]{0:T(1024)S(1)} %fusion.42), channel_id=1, replica_groups=mesh['dp'=8,'head'=4] {'dp'}, use_global_device_ids=true, to_apply=%region_12.13 | all-reduce | flops 4416 | bytes 35328 | tf_op jit(solution)/shard_map/psum | solution.py:1077
  370.1 4.3 collective-permute-done.26
  375.5 4.2 collective-permute-done.27
  389.9 4.2 collective-permute-done.13
  422.6 4.8 collective-permute-done.19
  428.4 6.7 %collective-permute-done.20 = bf16[2,96,576]{2,1,0:T(8,128)(2,1)S(1)} collective-permute-done((bf16[2,96,576]{2,1,0:T(8,128)(2,1)S(1)}, bf16[2,96,576]{2,1,0:T(8,128)(2,1)S(1)}, u32[]{:S(2)}, u32[]{:S(2)}) %collective-permute-start.20) | collective-permute-done | bytes 221216 | tf_op jit(solution)/shard_map/ppermute | solution.py:931
  445.2 23.0 %collective-permute-done.44 = bf16[2,4,96,768]{3,2,1,0:T(8,128)(2,1)S(1)} collective-permute-done((bf16[2,4,96,768]{3,2,1,0:T(8,128)(2,1)S(1)}, bf16[2,4,96,768]{3,2,1,0:T(8,128)(2,1)S(1)}, u32[]{:S(2)}, u32[]{:S(2)}) %collective-permute-start.44) | collective-permute-done | bytes 1179680 | tf_op jit(solution)/shard_map/ppermute | solution.py:931
  475.5 9.8 %rev.51 = bf16[4,2,1,96,576]{3,1,0,4,2:T(2,128)(2,1)} reverse(bf16[4,2,1,96,576]{3,1,0,4,2:T(2,128)(2,1)S(1)} %bitcast.199), dimensions={1} | reverse | bytes 1769472 | tf_op jit(solution)/shard_map/rev | solution.py:967
  497.4 4.7 collective-permute-done.47
  513.0 5.0 collective-permute-done.38
  526.8 3.8 reshape.254
  (381 shorter events, 188.3 us)
Async XLA Ops:
  167.3 30.4 %collective-permute-start.23 = (f32[768]{0:T(1024)S(1)}, f32[768]{0:T(1024)S(1)}, u32[]{:S(2)}, u32[]{:S(2)}) collective-permute-start(f32[768]{0:T(1024)S(1)} %get-tuple-element.128), channel_id=1, source_target_pairs={{0,2},{1,3},{2,0},{3,1},{4,6},{5,7},{6,4},{7,5},{8,10},{9,11},{10,... | collective-permute-start | bytes 9224 | tf_op jit(solution)/shard_map/ppermute | solution.py:931
  167.4 48.5 %collective-permute-start = (bf16[512,192]{1,0:T(8,128)(2,1)}, bf16[512,192]{1,0:T(8,128)(2,1)S(1)}, u32[]{:S(2)}, u32[]{:S(2)}) collective-permute-start(bf16[512,192]{1,0:T(8,128)(2,1)} %get-tuple-element.85), channel_id=1, source_target_pairs={{0,1},{1,0},{2,3},{3,2},{4,5},{5,4},{6,7},{7,6},{8,9},{9,8},{10,11... | collective-permute-start | bytes 589832 | tf_op jit(solution)/shard_map/ppermute | solution.py:931
  170.2 30.2 %collective-permute-start.1 = (bf16[512,192]{1,0:T(8,128)(2,1)}, bf16[512,192]{1,0:T(8,128)(2,1)}, u32[]{:S(2)}, u32[]{:S(2)}) collective-permute-start(bf16[512,192]{1,0:T(8,128)(2,1)} %get-tuple-element.95), channel_id=1, source_target_pairs={{0,1},{1,0},{2,3},{3,2},{4,5},{5,4},{6,7},{7,6},{8,9},{9,8},{10,11... | collective-permute-start | bytes 589832 | tf_op jit(solution)/shard_map/ppermute | solution.py:931
  174.4 189.5 %collective-permute-start.25 = (bf16[4,4,24,768]{3,2,1,0:T(8,128)(2,1)}, bf16[4,4,24,768]{3,2,1,0:T(8,128)(2,1)}, u32[]{:S(2)}, u32[]{:S(2)}) collective-permute-start(bf16[4,4,24,768]{3,2,1,0:T(8,128)(2,1)} %pad_maximum_fusion.3), channel_id=1, source_target_pairs={{0,4},{4,0},{8,12},{12,8},{16,20},{20,16},{24,28},{28,24},{1,5},{5... | collective-permute-start | bytes 1769480 | tf_op jit(solution)/shard_map/ppermute | solution.py:931
  182.4 255.4 %collective-permute-start.43 = (bf16[4,4,96,768]{3,2,1,0:T(8,128)(2,1)}, bf16[4,4,96,768]{3,2,1,0:T(8,128)(2,1)}, u32[]{:S(2)}, u32[]{:S(2)}) collective-permute-start(bf16[4,4,96,768]{3,2,1,0:T(8,128)(2,1)} %pad_maximum_fusion.1), channel_id=1, source_target_pairs={{0,4},{4,0},{8,12},{12,8},{16,20},{20,16},{24,28},{28,24},{1,5},{5... | collective-permute-start | bytes 7077896 | tf_op jit(solution)/shard_map/ppermute | solution.py:931
  198.4 139.9 %collective-permute-start.24 = (f32[768]{0:T(1024)}, f32[768]{0:T(1024)}, u32[]{:S(2)}, u32[]{:S(2)}) collective-permute-start(f32[768]{0:T(1024)} %add.167), channel_id=1, source_target_pairs={{0,1},{1,0},{2,3},{3,2},{4,5},{5,4},{6,7},{7,6},{8,9},{9,8},{10,11... | collective-permute-start | bytes 9224 | tf_op jit(solution)/shard_map/ppermute | solution.py:931
  214.6 15.8 %collective-permute-start.2 = (f32[32,256]{1,0:T(8,128)}, f32[32,256]{1,0:T(8,128)S(1)}, u32[]{:S(2)}, u32[]{:S(2)}) collective-permute-start(f32[32,256]{1,0:T(8,128)} %get-tuple-element.96.row_grads), channel_id=1, source_target_pairs={{2,0},{3,1},{6,4},{7,5},{10,8},{11,9},{14,12},{15,13},{18,16},{19,... | collective-permute-start | bytes 98312 | tf_op jit(solution)/shard_map/ppermute | solution.py:987
  215.9 16.8 %collective-permute-start.3 = (bf16[512,192]{1,0:T(8,128)(2,1)}, bf16[512,192]{1,0:T(8,128)(2,1)S(1)}, u32[]{:S(2)}, u32[]{:S(2)}) collective-permute-start(bf16[512,192]{1,0:T(8,128)(2,1)} %get-tuple-element.97), channel_id=1, source_target_pairs={{2,0},{3,1},{6,4},{7,5},{10,8},{11,9},{14,12},{15,13},{18,16},{19,... | collective-permute-start | bytes 589832 | tf_op jit(solution)/shard_map/ppermute | solution.py:987
  230.4 27.2 %collective-permute-start.4 = (f32[32,256]{1,0:T(8,128)}, f32[32,256]{1,0:T(8,128)S(1)}, u32[]{:S(2)}, u32[]{:S(2)}) collective-permute-start(f32[32,256]{1,0:T(8,128)} %get-tuple-element.91.row_grads), channel_id=1, source_target_pairs={{2,0},{3,1},{6,4},{7,5},{10,8},{11,9},{14,12},{15,13},{18,16},{19,... | collective-permute-start | bytes 98312 | tf_op jit(solution)/shard_map/ppermute | solution.py:987
  232.7 24.9 %collective-permute-start.5 = (bf16[512,192]{1,0:T(8,128)(2,1)}, bf16[512,192]{1,0:T(8,128)(2,1)S(1)}, u32[]{:S(2)}, u32[]{:S(2)}) collective-permute-start(bf16[512,192]{1,0:T(8,128)(2,1)} %get-tuple-element.104), channel_id=1, source_target_pairs={{2,0},{3,1},{6,4},{7,5},{10,8},{11,9},{14,12},{15,13},{18,16},{19,... | collective-permute-start | bytes 589832 | tf_op jit(solution)/shard_map/ppermute | solution.py:987
  283.3 52.5 %collective-permute-start.22 = (f32[4416]{0:T(1024)}, f32[4416]{0:T(1024)}, u32[]{:S(2)}, u32[]{:S(2)}) collective-permute-start(f32[4416]{0:T(1024)} %concatenate.97), channel_id=1, source_target_pairs={{0,2},{1,3},{2,0},{3,1},{4,6},{5,7},{6,4},{7,5},{8,10},{9,11},{10,... | collective-permute-start | bytes 53000 | tf_op jit(solution)/shard_map/ppermute | solution.py:931
  302.3 63.2 %collective-permute-start.15 = (bf16[4,96,576]{2,1,0:T(8,128)(2,1)}, bf16[4,96,576]{2,1,0:T(8,128)(2,1)}, u32[]{:S(2)}, u32[]{:S(2)}) collective-permute-start(bf16[4,96,576]{2,1,0:T(8,128)(2,1)} %pad_maximum_fusion.9), channel_id=1, source_target_pairs={{0,4},{4,0},{8,12},{12,8},{16,20},{20,16},{24,28},{28,24},{1,5},{5... | collective-permute-start | bytes 1327112 | tf_op jit(solution)/shard_map/ppermute | solution.py:931
  335.7 33.2 %collective-permute-start.12 = (bf16[4,96,576]{2,1,0:T(8,128)(2,1)}, bf16[4,96,576]{2,1,0:T(8,128)(2,1)}, u32[]{:S(2)}, u32[]{:S(2)}) collective-permute-start(bf16[4,96,576]{2,1,0:T(8,128)(2,1)} %pad_maximum_fusion.8), channel_id=1, source_target_pairs={{0,4},{4,0},{8,12},{12,8},{16,20},{20,16},{24,28},{28,24},{1,5},{5... | collective-permute-start | bytes 1327112 | tf_op jit(solution)/shard_map/ppermute | solution.py:931
  338.3 60.4 %collective-permute-start.6 = (bf16[512,768]{1,0:T(8,128)(2,1)}, bf16[512,768]{1,0:T(8,128)(2,1)S(1)}, u32[]{:S(2)}, u32[]{:S(2)}) collective-permute-start(bf16[512,768]{1,0:T(8,128)(2,1)} %slice.629), channel_id=1, source_target_pairs={{0,1},{1,0},{2,3},{3,2},{4,5},{5,4},{6,7},{7,6},{8,9},{9,8},{10,11... | collective-permute-start | bytes 2359304 | tf_op jit(solution)/shard_map/ppermute | solution.py:931
  366.9 17.4 %collective-permute-start.16 = (bf16[2,96,576]{2,1,0:T(8,128)(2,1)S(1)}, bf16[2,96,576]{2,1,0:T(8,128)(2,1)S(1)}, u32[]{:S(2)}, u32[]{:S(2)}) collective-permute-start(bf16[2,96,576]{2,1,0:T(8,128)(2,1)S(1)} %pad_maximum_fusion.15), channel_id=1, source_target_pairs={{0,8},{4,12},{8,0},{12,4},{16,24},{20,28},{24,16},{28,20},{1,9},{5... | collective-permute-start | bytes 663560 | tf_op jit(solution)/shard_map/ppermute | solution.py:931
  384.8 56.8 %collective-permute-start.34 = (bf16[4,4,96,768]{3,2,1,0:T(8,128)(2,1)S(1)}, bf16[4,4,96,768]{3,2,1,0:T(8,128)(2,1)S(1)}, u32[]{:S(2)}, u32[]{:S(2)}) collective-permute-start(bf16[4,4,96,768]{3,2,1,0:T(8,128)(2,1)S(1)} %copy-done.15), channel_id=1, source_target_pairs={{0,4},{4,0},{8,12},{12,8},{16,20},{20,16},{24,28},{28,24},{1,5},{5... | collective-permute-start | bytes 7077896 | tf_op jit(solution)/shard_map/ppermute | solution.py:931
  389.1 12.1 %collective-permute-start.17 = (bf16[1,96,576]{2,1,0:T(8,128)(2,1)S(1)}, bf16[1,96,576]{2,1,0:T(8,128)(2,1)S(1)}, u32[]{:S(2)}, u32[]{:S(2)}) collective-permute-start(bf16[1,96,576]{2,1,0:T(8,128)(2,1)S(1)} %slice.661), channel_id=1, source_target_pairs={{0,16},{4,20},{8,24},{12,28},{16,0},{20,4},{24,8},{28,12},{1,17},{... | collective-permute-start | bytes 331784 | tf_op jit(solution)/shard_map/ppermute | solution.py:931
  398.1 22.9 %collective-permute-start.14 = (bf16[1,96,576]{2,1,0:T(8,128)(2,1)S(1)}, bf16[1,96,576]{2,1,0:T(8,128)(2,1)S(1)}, u32[]{:S(2)}, u32[]{:S(2)}) collective-permute-start(bf16[1,96,576]{2,1,0:T(8,128)(2,1)S(1)} %slice.646), channel_id=1, source_target_pairs={{0,16},{4,20},{8,24},{12,28},{16,0},{20,4},{24,8},{28,12},{1,17},{... | collective-permute-start | bytes 331784 | tf_op jit(solution)/shard_map/ppermute | solution.py:931
  402.4 18.6 %collective-permute-start.18 = (bf16[96,576]{1,0:T(8,128)(2,1)S(1)}, bf16[96,576]{1,0:T(8,128)(2,1)S(1)}, u32[]{:S(2)}, u32[]{:S(2)}) collective-permute-start(bf16[96,576]{1,0:T(8,128)(2,1)S(1)} %fusion.30), channel_id=1, source_target_pairs={{0,2},{1,3},{2,0},{3,1},{4,6},{5,7},{6,4},{7,5},{8,10},{9,11},{10,... | collective-permute-start | bytes 331784 | tf_op jit(solution)/shard_map/ppermute | solution.py:931
  440.1 28.1 %collective-permute-start.44 = (bf16[2,4,96,768]{3,2,1,0:T(8,128)(2,1)S(1)}, bf16[2,4,96,768]{3,2,1,0:T(8,128)(2,1)S(1)}, u32[]{:S(2)}, u32[]{:S(2)}) collective-permute-start(bf16[2,4,96,768]{3,2,1,0:T(8,128)(2,1)S(1)} %pad_maximum_fusion.2), channel_id=1, source_target_pairs={{0,8},{4,12},{8,0},{12,4},{16,24},{20,28},{24,16},{28,20},{1,9},{5... | collective-permute-start | bytes 3538952 | tf_op jit(solution)/shard_map/ppermute | solution.py:931
  442.4 28.4 %collective-permute-start.35 = (bf16[2,4,96,768]{3,2,1,0:T(8,128)(2,1)S(1)}, bf16[2,4,96,768]{3,2,1,0:T(8,128)(2,1)S(1)}, u32[]{:S(2)}, u32[]{:S(2)}) collective-permute-start(bf16[2,4,96,768]{3,2,1,0:T(8,128)(2,1)S(1)} %concatenate.111), channel_id=1, source_target_pairs={{0,16},{4,20},{8,24},{12,28},{16,0},{20,4},{24,8},{28,12},{1,17},{... | collective-permute-start | bytes 3538952 | tf_op jit(solution)/shard_map/ppermute | solution.py:931
  469.4 15.9 %collective-permute-start.45 = (bf16[1,4,96,768]{3,2,1,0:T(8,128)(2,1)}, bf16[1,4,96,768]{3,2,1,0:T(8,128)(2,1)}, u32[]{:S(2)}, u32[]{:S(2)}) collective-permute-start(bf16[1,4,96,768]{3,2,1,0:T(8,128)(2,1)} %slice.734), channel_id=1, source_target_pairs={{0,16},{4,20},{8,24},{12,28},{16,0},{20,4},{24,8},{28,12},{1,17},{... | collective-permute-start | bytes 1769480 | tf_op jit(solution)/shard_map/ppermute | solution.py:931
  472.0 18.1 %collective-permute-start.36 = (bf16[1,4,96,768]{3,2,1,0:T(8,128)(2,1)}, bf16[1,4,96,768]{3,2,1,0:T(8,128)(2,1)}, u32[]{:S(2)}, u32[]{:S(2)}) collective-permute-start(bf16[1,4,96,768]{3,2,1,0:T(8,128)(2,1)} %slice.710), channel_id=1, source_target_pairs={{0,8},{4,12},{8,0},{12,4},{16,24},{20,28},{24,16},{28,20},{1,9},{5... | collective-permute-start | bytes 1769480 | tf_op jit(solution)/shard_map/ppermute | solution.py:931
  489.5 12.6 %collective-permute-start.47 = (bf16[96,768]{1,0:T(8,128)(2,1)S(1)}, bf16[96,768]{1,0:T(8,128)(2,1)S(1)}, u32[]{:S(2)}, u32[]{:S(2)}) collective-permute-start(bf16[96,768]{1,0:T(8,128)(2,1)S(1)} %get-tuple-element.199), channel_id=1, source_target_pairs={{0,2},{1,3},{2,0},{3,1},{4,6},{5,7},{6,4},{7,5},{8,10},{9,11},{10,... | collective-permute-start | bytes 442376 | tf_op jit(solution)/shard_map/ppermute | solution.py:931
  (79 other events, 507.6 us)
